TPU v7x, 32 devices: a whole 2x2x4 slice. The times are simulated.
32 devices in a mesh: seq: 8 (over z, x), mp: 4 (over y, core).
Axes of the slice: x: 2, y: 2, z: 4, core: 2. Of those that a mesh axis runs over, the one named last changes fastest.
Arguments:
- voxels: bfloat16 [6144, 1024], P('seq'), may hold values from -6 to 6
- destination: int32 [6144], P('seq'), may hold values from 0 to 12287, as said below
- cond: bfloat16 [4096, 1024], P('seq'), may hold values from -40 to 40
- norm_gain: float32 [1024], replicated, may hold values from 0.1 to 1.9
- qkv_weight: bfloat16 [3, 1024, 1024], P(None, None, 'mp'), may hold values from -0.1875 to 0.1875
- self_out_weight: bfloat16 [1024, 1024], P('mp'), may hold values from -0.1875 to 0.1875
- cross_norm_gain: float32 [1024], replicated, may hold values from 0.1 to 1.9
- cross_q_weight: bfloat16 [1024, 1024], P(None, 'mp'), may hold values from -0.5 to 0.5
- cond_kv_weight: bfloat16 [2, 1024, 1024], P(None, None, 'mp'), may hold values from -0.1875 to 0.1875
- cross_out_weight: bfloat16 [1024, 1024], P('mp'), may hold values from -0.1875 to 0.1875
Outputs:
- layer_out: bfloat16 [6144, 1024], P(('seq', 'mp'))
Inputs may be any that keep to these rules, and one draw needn't show every extreme that they name: Write owner = destination // 1536. No two voxels share a destination. Among the rows of one index of seq no owner occurs more than 192 times, on every index some owner occurs exactly 192 times, and some owner occurs 192 times on every index.
All inputs are finite; a program needn't handle non-finite values.
Results may differ from a plain program's by a relative error of at most 0.033.
The roundings to bfloat16 on the way count: a program that leaves them out, or rounds other values in their place, can miss the bound.
Values may be sent and summed in bfloat16 or wider, within the bound.
No kernel may reach another device: no remote copies, remote signals or barrier semaphores. Data moves between devices by JAX's collectives and lax.ppermute only.
A program may use at most 64 MiB of HBM per device.

v0:
```python
import math

import jax
import jax.numpy as jnp
from jax import lax
from jax.sharding import PartitionSpec as P

HD = 64
WBLK = 64


def rms_norm(matrix, gain):
    values = matrix.astype(jnp.float32)
    spread = jnp.mean(values * values, axis=-1, keepdims=True)
    return (values * lax.rsqrt(spread + 1e-06) * gain).astype(jnp.bfloat16)


def window_attention(queries, keyset, valset, occupied, head_count):
    slot_count = queries.shape[0]
    window_count = slot_count // WBLK
    query_heads = queries.reshape(window_count, WBLK, head_count, HD)
    key_heads = keyset.reshape(window_count, WBLK, head_count, HD)
    value_heads = valset.reshape(window_count, WBLK, head_count, HD)
    scores = jnp.einsum(
        "wqhd,wkhd->whqk", query_heads, key_heads, preferred_element_type=jnp.float32
    ) * HD ** (-0.5)
    diagonal = (
        jnp.arange(WBLK, dtype=jnp.int32)[:, None] == jnp.arange(WBLK, dtype=jnp.int32)[None, :]
    )
    allowed = occupied.reshape(window_count, 1, WBLK) | diagonal[None]
    weights = jnp.where(allowed[:, None], jnp.exp(scores), 0.0)
    totals = jnp.sum(weights, axis=-1)
    mixed = jnp.einsum(
        "whqk,wkhd->wqhd",
        weights.astype(jnp.bfloat16),
        value_heads,
        preferred_element_type=jnp.float32,
    )
    mixed = mixed / jnp.transpose(totals, (0, 2, 1))[:, :, :, None]
    return mixed.astype(jnp.bfloat16).reshape(slot_count, head_count * HD)


def shards(
    voxels,
    destination,
    cond,
    norm_gain,
    qkv_weight,
    self_out_weight,
    cross_norm_gain,
    cross_q_weight,
    cond_kv_weight,
    cross_out_weight,
):
    peer_count = lax.axis_size("seq")
    part_count = lax.axis_size("mp")
    model_index = lax.axis_index("mp")
    row_count = voxels.shape[0]
    local_width = qkv_weight.shape[2]
    head_count = local_width // HD
    capacity = 2 * row_count // peer_count
    slot_count = peer_count * capacity
    owner_ids = destination // slot_count
    slot_ids = destination % slot_count
    matches = (owner_ids[:, None] == jnp.arange(peer_count, dtype=jnp.int32)[None, :]).astype(
        jnp.int32
    )
    within = jnp.sum(matches * (jnp.cumsum(matches, axis=0) - 1), axis=1)
    send_index = owner_ids * capacity + within
    normed = rms_norm(voxels, norm_gain)
    place_buffer = (
        jnp.full((slot_count,), slot_count, jnp.int32)
        .at[send_index]
        .set(slot_ids)
        .reshape(peer_count, capacity)
    )
    projected = jnp.einsum(
        "rd,cdh->rch", normed, qkv_weight, preferred_element_type=jnp.float32
    ).astype(jnp.bfloat16)
    send_buffer = (
        jnp.zeros((slot_count, 3 * local_width), jnp.bfloat16)
        .at[send_index]
        .set(projected.reshape(row_count, 3 * local_width))
    )
    received, places = (
        lax.all_to_all(
            send_buffer.reshape(peer_count, capacity, 3 * local_width),
            "seq",
            split_axis=0,
            concat_axis=0,
            tiled=True,
        ),
        lax.all_to_all(place_buffer, "seq", split_axis=0, concat_axis=0, tiled=True),
    )
    received = received.reshape(slot_count, 3 * local_width)
    places = places.reshape(slot_count)
    layout = (
        jnp.zeros((slot_count, 3 * local_width), jnp.bfloat16).at[places].set(received, mode="drop")
    )
    occupied = jnp.zeros((slot_count,), jnp.bool_).at[places].set(True, mode="drop")
    mixed = window_attention(
        layout[:, :local_width],
        layout[:, local_width : 2 * local_width],
        layout[:, 2 * local_width :],
        occupied,
        head_count,
    )
    outgoing = mixed[jnp.minimum(places, slot_count - 1)]
    returned = lax.all_to_all(
        outgoing.reshape(peer_count, capacity, local_width),
        "seq",
        split_axis=0,
        concat_axis=0,
        tiled=True,
    )
    window_mix = returned.reshape(slot_count, local_width)[send_index]
    row_share = row_count // part_count
    summed_out = lax.psum(
        jnp.dot(window_mix, self_out_weight, preferred_element_type=jnp.float32), "mp"
    )
    hidden = voxels.astype(jnp.float32) + summed_out
    normed2 = rms_norm(hidden, cross_norm_gain)
    own_hidden = lax.dynamic_slice_in_dim(hidden, model_index * row_share, row_share, 0)
    cross_query = (
        jnp.dot(normed2, cross_q_weight, preferred_element_type=jnp.float32)
        .astype(jnp.bfloat16)
        .reshape(row_count, head_count, HD)
    )
    cond_pair = jnp.einsum(
        "td,cdh->cth", cond, cond_kv_weight, preferred_element_type=jnp.float32
    ).astype(jnp.bfloat16)

    def fold_block(running, key_block, value_block):
        row_max, totals, mixed_sum = running
        scores = jnp.einsum(
            "qhd,khd->qhk", cross_query, key_block, preferred_element_type=jnp.float32
        ) * HD ** (-0.5)
        new_max = jnp.maximum(row_max, jnp.max(scores, axis=-1))
        rescale = jnp.exp(row_max - new_max)
        weights = jnp.exp(scores - new_max[:, :, None])
        totals = totals * rescale + jnp.sum(weights, axis=-1)
        update = jnp.einsum(
            "qhk,khd->qhd",
            weights.astype(jnp.bfloat16),
            value_block,
            preferred_element_type=jnp.float32,
        )
        return (new_max, totals, mixed_sum * rescale[:, :, None] + update)

    start_state = (
        jnp.full((row_count, head_count), -1e30, jnp.float32),
        jnp.zeros((row_count, head_count), jnp.float32),
        jnp.zeros((row_count, head_count, HD), jnp.float32),
    )
    key_piece = lax.all_gather(cond_pair[0], "seq", axis=0, tiled=True)
    value_piece = lax.all_gather(cond_pair[1], "seq", axis=0, tiled=True)
    token_count = key_piece.shape[0]
    sub_block = math.gcd(token_count, 512)
    key_blocks = key_piece.reshape(token_count // sub_block, sub_block, head_count, HD)
    value_blocks = value_piece.reshape(token_count // sub_block, sub_block, head_count, HD)

    def advance(state, operands):
        return (fold_block(state, operands[0], operands[1]), None)

    folded, unused = lax.scan(advance, start_state, (key_blocks, value_blocks))
    row_max, totals, mixed_sum = folded
    cross_mix = (
        (mixed_sum / totals[:, :, None]).astype(jnp.bfloat16).reshape(row_count, local_width)
    )
    cross_sum = lax.psum_scatter(
        jnp.dot(cross_mix, cross_out_weight, preferred_element_type=jnp.float32),
        "mp",
        scatter_dimension=0,
        tiled=True,
    )
    return (own_hidden + cross_sum).astype(jnp.bfloat16)


def solution(mesh):
    return jax.shard_map(
        shards,
        mesh=mesh,
        in_specs=(
            P("seq", None),
            P("seq"),
            P("seq", None),
            P(),
            P(None, None, "mp"),
            P("mp", None),
            P(),
            P(None, "mp"),
            P(None, None, "mp"),
            P("mp", None),
        ),
        out_specs=P(("seq", "mp"), None),
        check_vma=False,
    )
```

profile of v0, /device:TPU:0, one launch (start us, length us, event | category | flops | bytes accessed | tf_op | source)
XLA Modules:
  0.0 404.7 jit_solution(4742281311101803393)
XLA Ops:
  15.2 7.3 %all-to-all-start = ((s32[8,1,192]{2,1,0:T(1,128)}), s32[8,1,192]{2,1,0:T(1,128)S(1)}, u32[]{:S(2)}, u32[]{:S(2)}) async-start(s32[8,1,192]{2,1,0:T(1,128)} %all_to_all.12), calls=%async_computation | async-start | bytes 16384 | tf_op jit(solution)/shard_map/all_to_all | solution.py:93
  30.5 7.3 %scatter_custom_fusion.1 = bf16[1536,768]{1,0:T(8,128)(2,1)} fusion(s32[768]{0:T(1024)S(1)} %get-tuple-element.111, bf16[768,768]{1,0:T(8,128)(2,1)S(1)} %copy.23, bf16[]{:T(256)} %constant.28.clone.1), kind=kCustom, calls=%fused_computation.62 | custom fusion | bytes 2359298 | tf_op jit(solution)/shard_map/scatter | solution.py:83
  37.8 6.0 %all-to-all-start.1 = ((bf16[8,192,768]{2,1,0:T(8,128)(2,1)}), bf16[8,192,768]{2,1,0:T(8,128)(2,1)}, u32[]{:S(2)}, u32[]{:S(2)}) async-start(bf16[8,192,768]{2,1,0:T(8,128)(2,1)} %bitcast.94), calls=%async_computation.1 | async-start | bytes 4718592 | tf_op jit(solution)/shard_map/all_to_all | solution.py:86
  44.7 11.2 %scatter_custom_fusion.3 = pred[1536]{0:T(1024)(128)(4,1)S(1)} fusion(s32[1536]{0:T(1024)S(1)} %get-tuple-element.84, pred[1536]{0:T(1024)(128)(4,1)S(1)} %broadcast.137, pred[]{:T(512)} %constant.45.clone.1), kind=kCustom, calls=%fused_computation.89 | custom fusion | bytes 1537 | tf_op jit(solution)/shard_map/scatter | solution.py:100
  56.3 61.5 %all-to-all-done.1 = bf16[8,192,768]{2,1,0:T(8,128)(2,1)} async-done(((bf16[8,192,768]{2,1,0:T(8,128)(2,1)}), bf16[8,192,768]{2,1,0:T(8,128)(2,1)}, u32[]{:S(2)}, u32[]{:S(2)}) %all-to-all-start.1) | async-done | bytes 2359328 | tf_op jit(solution)/shard_map/all_to_all | solution.py:86
  117.8 9.6 %scatter_custom_fusion.2 = bf16[1536,768]{1,0:T(8,128)(2,1)} fusion(s32[1536]{0:T(1024)S(1)} %get-tuple-element.84, bf16[1536,768]{1,0:T(8,128)(2,1)} %bitcast.7, bf16[]{:T(256)} %constant.28.clone.1), kind=kCustom, calls=%fused_computation.60 | custom fusion | bytes 2359808 | tf_op jit(solution)/shard_map/scatter | solution.py:98
  148.7 5.3 %gather_fusion = bf16[1536,256]{1,0:T(8,128)(2,1)} fusion(bf16[1536,256]{1,0:T(8,128)(2,1)S(1)} %reshape.225, s32[2048]{0:T(1024)S(1)} %pad_clamp_fusion), kind=kCustom, calls=%fused_computation | custom fusion | bytes 1579008 | tf_op jit(solution)/shard_map/gather | solution.py:108
  157.6 26.4 %all-to-all-done.2 = bf16[8,192,256]{2,1,0:T(8,128)(2,1)S(1)} async-done(((bf16[8,192,256]{2,1,0:T(8,128)(2,1)}), bf16[8,192,256]{2,1,0:T(8,128)(2,1)S(1)}, u32[]{:S(2)}, u32[]{:S(2)}) %all-to-all-start.2) | async-done | bytes 786464 | tf_op jit(solution)/shard_map/all_to_all | solution.py:109
  199.4 57.5 %all-reduce.2.cloned.1.call-done = f32[768,1024]{1,0:T(8,128)} async-done(((f32[768,1024]{1,0:T(8,128)}), f32[768,1024]{1,0:T(8,128)}) %all-reduce.2.cloned.1.call-update) | async-done | bytes 3145744 | tf_op jit(solution)/shard_map/psum | solution.py:118
  261.8 92.8 %while.15 = (s32[]{:T(128)}, f32[768,4]{0,1:T(4,128)S(1)}, f32[768,4]{0,1:T(4,128)S(1)}, f32[768,4,64]{0,2,1:T(8,128)S(1)}, bf16[8,512,4,64]{1,3,2,0:T(8,128)(2,...) while((s32[]{:T(128)}, f32[768,4]{0,1:T(4,128)S(1)}, ...), condition=%wide.region_14.15_spmd.clone, body=%wide.region_11.14_spmd.clone.sunk | while | flops 415841280 | bytes 46728324 | solution.py:165
  261.9 4.7 %bitcast_reduce_fusion.2 = (f32[768,4]{0,1:T(4,128)S(1)}, f32[4,512,768]{2,1,0:T(8,128)}) fusion(bf16[768,4,64]{0,2,1:T(8,128)(2,1)S(1)} %get-tuple-element.190, bf16[8,512,4,64]{1,3,2,0:T(8,128)(2,1)} %get-tuple-element.189, s32[]{:T(128)} %get-tuple-element.176), kind=kOutput, calls=%fused_computation.7.clone.1 | convolution fusion | flops 204469248 | bytes 6959616 | tf_op jit(solution)/shard_map/while/body/eval_jaxpr/qhd,khd->qhk/dot_general | solution.py:135
  273.5 4.6 %bitcast_reduce_fusion.2 = (f32[768,4]{0,1:T(4,128)S(1)}, f32[4,512,768]{2,1,0:T(8,128)}) fusion(bf16[768,4,64]{0,2,1:T(8,128)(2,1)S(1)} %get-tuple-element.190, bf16[8,512,4,64]{1,3,2,0:T(8,128)(2,1)} %get-tuple-element.189, s32[]{:T(128)} %get-tuple-element.176), kind=kOutput, calls=%fused_computation.7.clone.1 | convolution fusion | flops 204469248 | bytes 6959616 | tf_op jit(solution)/shard_map/while/body/eval_jaxpr/qhd,khd->qhk/dot_general | solution.py:135
  278.2 4.0 fusion.87
  285.1 4.6 %bitcast_reduce_fusion.2 = (f32[768,4]{0,1:T(4,128)S(1)}, f32[4,512,768]{2,1,0:T(8,128)}) fusion(bf16[768,4,64]{0,2,1:T(8,128)(2,1)S(1)} %get-tuple-element.190, bf16[8,512,4,64]{1,3,2,0:T(8,128)(2,1)} %get-tuple-element.189, s32[]{:T(128)} %get-tuple-element.176), kind=kOutput, calls=%fused_computation.7.clone.1 | convolution fusion | flops 204469248 | bytes 6959616 | tf_op jit(solution)/shard_map/while/body/eval_jaxpr/qhd,khd->qhk/dot_general | solution.py:135
  296.7 4.6 %bitcast_reduce_fusion.2 = (f32[768,4]{0,1:T(4,128)S(1)}, f32[4,512,768]{2,1,0:T(8,128)}) fusion(bf16[768,4,64]{0,2,1:T(8,128)(2,1)S(1)} %get-tuple-element.190, bf16[8,512,4,64]{1,3,2,0:T(8,128)(2,1)} %get-tuple-element.189, s32[]{:T(128)} %get-tuple-element.176), kind=kOutput, calls=%fused_computation.7.clone.1 | convolution fusion | flops 204469248 | bytes 6959616 | tf_op jit(solution)/shard_map/while/body/eval_jaxpr/qhd,khd->qhk/dot_general | solution.py:135
  301.3 4.0 fusion.87
  308.3 4.6 %bitcast_reduce_fusion.2 = (f32[768,4]{0,1:T(4,128)S(1)}, f32[4,512,768]{2,1,0:T(8,128)}) fusion(bf16[768,4,64]{0,2,1:T(8,128)(2,1)S(1)} %get-tuple-element.190, bf16[8,512,4,64]{1,3,2,0:T(8,128)(2,1)} %get-tuple-element.189, s32[]{:T(128)} %get-tuple-element.176), kind=kOutput, calls=%fused_computation.7.clone.1 | convolution fusion | flops 204469248 | bytes 6959616 | tf_op jit(solution)/shard_map/while/body/eval_jaxpr/qhd,khd->qhk/dot_general | solution.py:135
  312.9 4.0 fusion.87
  319.8 4.6 %bitcast_reduce_fusion.2 = (f32[768,4]{0,1:T(4,128)S(1)}, f32[4,512,768]{2,1,0:T(8,128)}) fusion(bf16[768,4,64]{0,2,1:T(8,128)(2,1)S(1)} %get-tuple-element.190, bf16[8,512,4,64]{1,3,2,0:T(8,128)(2,1)} %get-tuple-element.189, s32[]{:T(128)} %get-tuple-element.176), kind=kOutput, calls=%fused_computation.7.clone.1 | convolution fusion | flops 204469248 | bytes 6959616 | tf_op jit(solution)/shard_map/while/body/eval_jaxpr/qhd,khd->qhk/dot_general | solution.py:135
  324.5 4.0 fusion.87
  331.4 4.6 %bitcast_reduce_fusion.2 = (f32[768,4]{0,1:T(4,128)S(1)}, f32[4,512,768]{2,1,0:T(8,128)}) fusion(bf16[768,4,64]{0,2,1:T(8,128)(2,1)S(1)} %get-tuple-element.190, bf16[8,512,4,64]{1,3,2,0:T(8,128)(2,1)} %get-tuple-element.189, s32[]{:T(128)} %get-tuple-element.176), kind=kOutput, calls=%fused_computation.7.clone.1 | convolution fusion | flops 204469248 | bytes 6959616 | tf_op jit(solution)/shard_map/while/body/eval_jaxpr/qhd,khd->qhk/dot_general | solution.py:135
  336.1 4.0 fusion.87
  343.0 4.6 %bitcast_reduce_fusion.2 = (f32[768,4]{0,1:T(4,128)S(1)}, f32[4,512,768]{2,1,0:T(8,128)}) fusion(bf16[768,4,64]{0,2,1:T(8,128)(2,1)S(1)} %get-tuple-element.190, bf16[8,512,4,64]{1,3,2,0:T(8,128)(2,1)} %get-tuple-element.189, s32[]{:T(128)} %get-tuple-element.176), kind=kOutput, calls=%fused_computation.7.clone.1 | convolution fusion | flops 204469248 | bytes 6959616 | tf_op jit(solution)/shard_map/while/body/eval_jaxpr/qhd,khd->qhk/dot_general | solution.py:135
  357.0 38.1 %reduce-scatter.2.cloned.1.call-done = f32[192,1024]{1,0:T(8,128)} async-done(((f32[768,1024]{1,0:T(8,128)}), f32[192,1024]{1,0:T(8,128)}) %reduce-scatter.2.cloned.1.call-update) | async-done | bytes 786448 | tf_op jit(solution)/shard_map/reduce_scatter | solution.py:170
  (130 shorter events, 101.9 us)
Async XLA Ops:
  7.4 18.9 %copy-start = (bf16[3,1024,256]{2,1,0:T(8,128)(2,1)S(1)}, bf16[3,1024,256]{2,1,0:T(8,128)(2,1)}, u32[]{:S(2)}) copy-start(bf16[3,1024,256]{2,1,0:T(8,128)(2,1)} %param.16) | copy-start | bytes 4718596
  15.2 22.6 %all-to-all-start = ((s32[8,1,192]{2,1,0:T(1,128)}), s32[8,1,192]{2,1,0:T(1,128)S(1)}, u32[]{:S(2)}, u32[]{:S(2)}) async-start(s32[8,1,192]{2,1,0:T(1,128)} %all_to_all.12), calls=%async_computation | async-start | bytes 16384 | tf_op jit(solution)/shard_map/all_to_all | solution.py:93
  22.5 3.3 copy-start.4
  22.5 3.7 copy-start.9
  22.5 167.9 %all-gather.5.cloned.1.call-start = ((), (), s32[]{:S(2)}) async-start(), calls=%async_computation.6 | async-start | bytes 2359296 | tf_op jit(solution)/shard_map/all_gather | solution.py:155
  37.8 80.0 %all-to-all-start.1 = ((bf16[8,192,768]{2,1,0:T(8,128)(2,1)}), bf16[8,192,768]{2,1,0:T(8,128)(2,1)}, u32[]{:S(2)}, u32[]{:S(2)}) async-start(bf16[8,192,768]{2,1,0:T(8,128)(2,1)} %bitcast.94), calls=%async_computation.1 | async-start | bytes 4718592 | tf_op jit(solution)/shard_map/all_to_all | solution.py:86
  43.8 151.1 %all-gather.7.cloned.1.call-start = ((), (), s32[]{:S(2)}) async-start(), calls=%async_computation.7 | async-start | bytes 2359296 | tf_op jit(solution)/shard_map/all_gather | solution.py:156
  136.7 3.2 copy-start.5
  154.0 30.0 %all-to-all-start.2 = ((bf16[8,192,256]{2,1,0:T(8,128)(2,1)}), bf16[8,192,256]{2,1,0:T(8,128)(2,1)S(1)}, u32[]{:S(2)}, u32[]{:S(2)}) async-start(bf16[8,192,256]{2,1,0:T(8,128)(2,1)} %bitcast.10), calls=%async_computation.2 | async-start | bytes 1572864 | tf_op jit(solution)/shard_map/all_to_all | solution.py:109
  157.6 99.3 %all-reduce.2.cloned.1.call-start = ((), (), s32[]{:S(2)}) async-start(), calls=%async_computation.4 | async-start | bytes 6291456 | tf_op jit(solution)/shard_map/psum | solution.py:118
  190.0 205.0 %reduce-scatter.2.cloned.1.call-start = ((), (), s32[]{:S(2)}) async-start(), calls=%async_computation.5 | async-start | bytes 3932160 | tf_op jit(solution)/shard_map/reduce_scatter | solution.py:170
  199.4 61.6 %copy-start.8 = (f32[1024]{0:T(1024)S(1)}, f32[1024]{0:T(1024)}, u32[]{:S(2)}) copy-start(f32[1024]{0:T(1024)} %param.18) | copy-start | bytes 12292
  256.9 4.1 %copy-start.6 = (bf16[1024,256]{1,0:T(8,128)(2,1)S(1)}, bf16[1024,256]{1,0:T(8,128)(2,1)}, u32[]{:S(2)}) copy-start(bf16[1024,256]{1,0:T(8,128)(2,1)} %param.19) | copy-start | bytes 1572868
  259.3 1.7 copy-start.3
  261.8 92.8 %copy-start.7 = (bf16[256,1024]{1,0:T(8,128)(2,1)S(1)}, bf16[256,1024]{1,0:T(8,128)(2,1)}, u32[]{:S(2)}) copy-start(bf16[256,1024]{1,0:T(8,128)(2,1)} %param.21) | copy-start | bytes 1572868
  266.6 4.6 %copy-start.2 = (f32[4,512,768]{2,1,0:T(8,128)S(1)}, f32[4,512,768]{2,1,0:T(8,128)}, u32[]{:S(2)}) copy-start(f32[4,512,768]{2,1,0:T(8,128)} %get-tuple-element.164) | copy-start | bytes 18874372 | tf_op jit(solution)/shard_map/while
  278.1 4.6 %copy-start.2 = (f32[4,512,768]{2,1,0:T(8,128)S(1)}, f32[4,512,768]{2,1,0:T(8,128)}, u32[]{:S(2)}) copy-start(f32[4,512,768]{2,1,0:T(8,128)} %get-tuple-element.164) | copy-start | bytes 18874372 | tf_op jit(solution)/shard_map/while
  289.7 4.6 %copy-start.2 = (f32[4,512,768]{2,1,0:T(8,128)S(1)}, f32[4,512,768]{2,1,0:T(8,128)}, u32[]{:S(2)}) copy-start(f32[4,512,768]{2,1,0:T(8,128)} %get-tuple-element.164) | copy-start | bytes 18874372 | tf_op jit(solution)/shard_map/while
  301.3 4.6 %copy-start.2 = (f32[4,512,768]{2,1,0:T(8,128)S(1)}, f32[4,512,768]{2,1,0:T(8,128)}, u32[]{:S(2)}) copy-start(f32[4,512,768]{2,1,0:T(8,128)} %get-tuple-element.164) | copy-start | bytes 18874372 | tf_op jit(solution)/shard_map/while
  312.9 4.6 %copy-start.2 = (f32[4,512,768]{2,1,0:T(8,128)S(1)}, f32[4,512,768]{2,1,0:T(8,128)}, u32[]{:S(2)}) copy-start(f32[4,512,768]{2,1,0:T(8,128)} %get-tuple-element.164) | copy-start | bytes 18874372 | tf_op jit(solution)/shard_map/while
  324.5 4.6 %copy-start.2 = (f32[4,512,768]{2,1,0:T(8,128)S(1)}, f32[4,512,768]{2,1,0:T(8,128)}, u32[]{:S(2)}) copy-start(f32[4,512,768]{2,1,0:T(8,128)} %get-tuple-element.164) | copy-start | bytes 18874372 | tf_op jit(solution)/shard_map/while
  336.1 4.6 %copy-start.2 = (f32[4,512,768]{2,1,0:T(8,128)S(1)}, f32[4,512,768]{2,1,0:T(8,128)}, u32[]{:S(2)}) copy-start(f32[4,512,768]{2,1,0:T(8,128)} %get-tuple-element.164) | copy-start | bytes 18874372 | tf_op jit(solution)/shard_map/while
  347.7 4.6 %copy-start.2 = (f32[4,512,768]{2,1,0:T(8,128)S(1)}, f32[4,512,768]{2,1,0:T(8,128)}, u32[]{:S(2)}) copy-start(f32[4,512,768]{2,1,0:T(8,128)} %get-tuple-element.164) | copy-start | bytes 18874372 | tf_op jit(solution)/shard_map/while
  356.9 40.3 %copy-start.1 = (bf16[3,1024,256]{2,1,0:T(8,128)(2,1)S(1)}, bf16[3,1024,256]{2,1,0:T(8,128)(2,1)}, u32[]{:S(2)}) copy-start(bf16[3,1024,256]{2,1,0:T(8,128)(2,1)} %param.16) | copy-start | bytes 4718596
Sparse Core Ops, SparseCore 0:
  25.9 88.9 all-gather.4
  116.9 58.1 all-gather.6
Sparse Core Ops, SparseCore 1:
  190.1 66.7 all-reduce.1
  357.1 37.9 reduce-scatter.1
where the time goes:
time: 406 us; the launch traced here: 405 us
  waiting for transfers between devices  184 us (45%)
  local copies, waits for them, and re-layouts  74.4 us (18%)
  matrix products  72.3 us (18%)
  other arithmetic  41 us (10%)
  starting transfers between devices  17.4 us (4%)
  between operations  15.1 us (4%)
    all_to_all x1, waiting for transfers between devices, shards(): lax.all_to_all(send_buffer.reshape(peer_count, capacity, 3 * local_width)...  61.5 us
    psum x1, waiting for transfers between devices, shards(): lax.psum(jnp.dot(window_mix, self_out_weight, preferred_element_type=jnp....  57.5 us
    reduce_scatter x1, waiting for transfers between devices, shards(): lax.psum_scatter(jnp.dot(cross_mix, cross_out_weight, preferred_element_t...  38.1 us
    dot_general x8, matrix products, fold_block(): jnp.einsum('qhd,khd->qhk', cross_query, key_block, preferred_element_type...  37.2 us
    reduce_sum x8, other arithmetic, fold_block(): totals = totals * rescale + jnp.sum(weights, axis=-1)  31.8 us
    all_to_all x1, waiting for transfers between devices, shards(): lax.all_to_all(outgoing.reshape(peer_count, capacity, local_width), 'seq'...  26.4 us
    dot_general x8, matrix products, fold_block(): jnp.einsum('qhk,khd->qhd', weights.astype(jnp.bfloat16), value_block, pre...  18.4 us
    scatter x1, local copies, waits for them, and re-layouts, shards(): jnp.zeros((slot_count,), jnp.bool_).at[places].set(True, mode='drop')  11.2 us
  transfers between devices with their start and end apart: 7, of which 4 were waited for; matrix products, arithmetic and copies ran while one was open for 19% of the time, Pallas kernels for 0%

commit v1 on v0

--- a/solution.py
+++ b/solution.py
@@ -1,12 +1,334 @@
+import functools
 import math
 
 import jax
 import jax.numpy as jnp
 from jax import lax
+from jax.experimental import pallas as pl
+from jax.experimental.pallas import tpu as pltpu
 from jax.sharding import PartitionSpec as P
 
 HD = 64
 WBLK = 64
+LANES = 128
+ID_ROWS = 16
+VMEM_LIMIT = 48 * 1024 * 1024
+CORE_SWAP = ((0, 1), (1, 0), (2, 3), (3, 2))
+CHIP_SWAP = ((0, 2), (2, 0), (1, 3), (3, 1))
+
+
+def low_lanes(shape):
+    return lax.broadcasted_iota(jnp.int32, shape, 1) < HD
+
+
+def swap_halves(values):
+    return pltpu.roll(values, HD, 1)
+
+
+def project_kernel(core_ref, vox_ref, gain_ref, ids_ref, own_ref, other_ref, out_ref, normed_ref):
+    step = pl.program_id(0)
+    rows = vox_ref.shape[0]
+    packed = rows // 2
+
+    @pl.when(step == 0)
+    def _():
+        values = vox_ref[...].astype(jnp.float32)
+        spread = jnp.mean(values * values, axis=-1, keepdims=True)
+        normed_ref[...] = (values * lax.rsqrt(spread + 1e-06) * gain_ref[...]).astype(jnp.bfloat16)
+
+    def emit(weight_ref):
+        normed = normed_ref[...]
+        low = low_lanes((rows, LANES))
+        low_packed = low_lanes((packed, LANES))
+        query, key, value = (
+            jnp.dot(normed, weight_ref[part], preferred_element_type=jnp.float32)
+            for part in range(3)
+        )
+        query = query * HD ** (-0.5)
+        first, second = query[:packed], query[packed:]
+        pairs = (
+            (
+                jnp.where(low, key, swap_halves(value)),
+                jnp.where(low_packed, first, swap_halves(second)),
+            ),
+            (
+                jnp.where(low, swap_halves(key), value),
+                jnp.where(low_packed, swap_halves(first), second),
+            ),
+        )
+        for head, (keyval, queries) in enumerate(pairs):
+            out_ref[head, :rows] = keyval.astype(jnp.bfloat16)
+            out_ref[head, rows : rows + ID_ROWS] = ids_ref[...]
+            out_ref[head, rows + ID_ROWS :] = queries.astype(jnp.bfloat16)
+
+    @pl.when(step < 2)
+    def _():
+        emit(own_ref)
+
+    @pl.when(step >= 2)
+    def _():
+        emit(other_ref)
+
+
+def project(core, vox, gain, ids, own_weight, other_weight):
+    rows, width = vox.shape
+    local_width = own_weight.shape[2]
+    heads = 2 * local_width // HD
+    pair_steps = heads // 2
+    half_steps = pair_steps // 2
+    blob = rows + ID_ROWS + rows // 2
+
+    def out_map(step, core_ref):
+        side = step // half_steps
+        absolute = jnp.where(side == 0, core_ref[0], 1 - core_ref[0])
+        return (absolute * half_steps + step % half_steps, 0, 0)
+
+    return pl.pallas_call(
+        project_kernel,
+        out_shape=jax.ShapeDtypeStruct((heads, blob, LANES), jnp.bfloat16),
+        grid_spec=pltpu.PrefetchScalarGridSpec(
+            num_scalar_prefetch=1,
+            grid=(pair_steps,),
+            in_specs=[
+                pl.BlockSpec((rows, width), lambda step, core_ref: (0, 0)),
+                pl.BlockSpec((1, width), lambda step, core_ref: (0, 0)),
+                pl.BlockSpec((ID_ROWS, LANES), lambda step, core_ref: (0, 0)),
+                pl.BlockSpec(
+                    (3, width, LANES),
+                    lambda step, core_ref: (0, 0, jnp.minimum(step, half_steps - 1)),
+                ),
+                pl.BlockSpec(
+                    (3, width, LANES),
+                    lambda step, core_ref: (0, 0, jnp.maximum(step - half_steps, 0)),
+                ),
+            ],
+            out_specs=pl.BlockSpec((2, blob, LANES), out_map),
+            scratch_shapes=[pltpu.VMEM((rows, width), jnp.bfloat16)],
+        ),
+        compiler_params=pltpu.CompilerParams(vmem_limit_bytes=VMEM_LIMIT),
+    )(core, vox, gain, ids, own_weight, other_weight)
+
+
+def read_ids(ref, index, rows):
+    tile = ref[index, rows : rows + ID_ROWS].astype(jnp.float32)
+    return tile[:8] * 256.0 + tile[8:]
+
+
+def window_kernel(mine_ref, theirs_ref, out_ref):
+    source = pl.program_id(0)
+    sources = mine_ref.shape[0]
+    packed = out_ref.shape[1]
+    rows = 2 * packed
+    groups = rows // LANES
+    low_packed = low_lanes((packed, LANES))
+    wire = mine_ref[source, rows + ID_ROWS :].astype(jnp.float32)
+    query = jnp.concatenate(
+        [jnp.where(low_packed, wire, 0.0), jnp.where(low_packed, swap_halves(wire), 0.0)], axis=0
+    ).astype(jnp.bfloat16)
+    columns = jnp.transpose(read_ids(mine_ref, source, rows))
+    query_ids = jnp.concatenate([columns[:, g : g + 1] for g in range(groups)], axis=0)
+    low = low_lanes((rows, LANES))
+    one = jnp.ones((), jnp.bfloat16)
+
+    def fold(ref, index, total):
+        keyval = ref[index, :rows]
+        key_ids = read_ids(ref, index, rows)
+        scores = lax.dot_general(
+            query, keyval, (((1,), (1,)), ((), ())), preferred_element_type=jnp.float32
+        )
+        weights = jnp.concatenate(
+            [
+                jnp.where(
+                    query_ids == key_ids[g : g + 1],
+                    jnp.exp(scores[:, g * LANES : (g + 1) * LANES]),
+                    0.0,
+                ).astype(jnp.bfloat16)
+                for g in range(groups)
+            ],
+            axis=1,
+        )
+        return total + jnp.dot(
+            weights, jnp.where(low, one, keyval), preferred_element_type=jnp.float32
+        )
+
+    def body(index, total):
+        return fold(theirs_ref, index, fold(mine_ref, index, total))
+
+    total = lax.fori_loop(0, sources, body, jnp.zeros((rows, LANES), jnp.float32))
+    mixed = total / swap_halves(total)
+    out_ref[0] = jnp.where(low_packed, swap_halves(mixed[:packed]), mixed[packed:]).astype(
+        jnp.bfloat16
+    )
+
+
+def window_mixing(mine, theirs, packed):
+    sources, blob, _ = mine.shape
+    return pl.pallas_call(
+        window_kernel,
+        out_shape=jax.ShapeDtypeStruct((sources, packed, LANES), jnp.bfloat16),
+        grid=(sources,),
+        in_specs=[
+            pl.BlockSpec(mine.shape, lambda source: (0, 0, 0)),
+            pl.BlockSpec(theirs.shape, lambda source: (0, 0, 0)),
+        ],
+        out_specs=pl.BlockSpec((1, packed, LANES), lambda source: (source, 0, 0)),
+        compiler_params=pltpu.CompilerParams(vmem_limit_bytes=VMEM_LIMIT),
+    )(mine, theirs)
+
+
+def cross_kernel(query_ref, key_ref, value_ref, out_ref, score_ref):
+    rows = query_ref.shape[0]
+    tokens = key_ref.shape[0]
+    chunk = math.gcd(tokens, 512)
+    low = low_lanes((rows, LANES))
+    wire = query_ref[...]
+    zero = jnp.zeros((), jnp.bfloat16)
+    ones = jnp.ones((chunk, LANES), jnp.bfloat16)
+    mixes = []
+    for head in range(2):
+        query = jnp.where(low == (head == 0), wire, zero)
+        peak = jnp.full((rows, LANES), -jnp.inf, jnp.float32)
+        for start in range(0, tokens, chunk):
+            scores = lax.dot_general(
+                query,
+                key_ref[start : start + chunk],
+                (((1,), (1,)), ((), ())),
+                preferred_element_type=jnp.float32,
+            )
+            score_ref[head, :, start : start + chunk] = scores
+            for g in range(chunk // LANES):
+                peak = jnp.maximum(peak, scores[:, g * LANES : (g + 1) * LANES])
+        row_max = jnp.max(peak, axis=-1, keepdims=True)
+        total = jnp.zeros((rows, 2 * LANES), jnp.float32)
+        for start in range(0, tokens, chunk):
+            weights = jnp.exp(score_ref[head, :, start : start + chunk] - row_max).astype(
+                jnp.bfloat16
+            )
+            values = jnp.concatenate([value_ref[start : start + chunk], ones], axis=1)
+            total = total + jnp.dot(weights, values, preferred_element_type=jnp.float32)
+        mixes.append(total[:, :LANES] / total[:, LANES:])
+    out_ref[...] = jnp.where(low, mixes[0], mixes[1]).astype(jnp.bfloat16)
+
+
+def cross_mixing(queries, keyval):
+    rows, local_width = queries.shape
+    tokens = keyval.shape[0]
+    pairs = local_width // LANES
+    block = rows // 2
+    return pl.pallas_call(
+        cross_kernel,
+        out_shape=jax.ShapeDtypeStruct((rows, local_width), jnp.bfloat16),
+        grid=(pairs, rows // block),
+        in_specs=[
+            pl.BlockSpec((block, LANES), lambda pair, part: (part, pair)),
+            pl.BlockSpec((tokens, LANES), lambda pair, part: (0, pair)),
+            pl.BlockSpec((tokens, LANES), lambda pair, part: (0, pairs + pair)),
+        ],
+        out_specs=pl.BlockSpec((block, LANES), lambda pair, part: (part, pair)),
+        scratch_shapes=[pltpu.VMEM((2, block, tokens), jnp.float32)],
+        compiler_params=pltpu.CompilerParams(vmem_limit_bytes=VMEM_LIMIT),
+    )(queries, keyval, keyval)
+
+
+def swap(array, pairs):
+    return lax.ppermute(array, "mp", pairs)
+
+
+def by_head(
+    voxels,
+    destination,
+    cond,
+    norm_gain,
+    qkv_weight,
+    self_out_weight,
+    cross_norm_gain,
+    cross_q_weight,
+    cond_kv_weight,
+    cross_out_weight,
+):
+    model_index = lax.axis_index("mp")
+    core = model_index % 2
+    chip = model_index // 2
+    row_count, width = voxels.shape
+    local_width = qkv_weight.shape[2]
+    share = row_count // 4
+    rows = 2 * share
+    head_count = 2 * local_width // HD
+
+    other_qkv = swap(qkv_weight, CORE_SWAP)
+    cond_pair = [
+        jnp.dot(cond, cond_kv_weight[part], preferred_element_type=jnp.float32).astype(jnp.bfloat16)
+        for part in range(2)
+    ]
+    own_keyval = lax.all_gather(jnp.concatenate(cond_pair, axis=1), "seq", axis=0, tiled=True)
+
+    vox = lax.dynamic_index_in_dim(
+        voxels.reshape(2, 2, share, width), core, axis=1, keepdims=False
+    ).reshape(rows, width)
+    window_ids = (
+        lax.dynamic_index_in_dim(
+            destination.reshape(2, 2, share), core, axis=1, keepdims=False
+        ).reshape(rows // LANES, LANES)
+        // WBLK
+    )
+    blank = jnp.zeros((8 - rows // LANES, LANES), jnp.int32)
+    ids = jnp.concatenate([window_ids // 256, blank, window_ids % 256, blank], axis=0).astype(
+        jnp.bfloat16
+    )
+    sent = project(
+        core.reshape(1).astype(jnp.int32), vox, norm_gain.reshape(1, width), ids, qkv_weight, other_qkv
+    )
+
+    chip_out = swap(jnp.concatenate([self_out_weight, cross_out_weight], axis=0), CHIP_SWAP)
+    other_q = swap(cross_q_weight, CORE_SWAP)
+
+    mine = lax.all_to_all(sent, "seq", split_axis=0, concat_axis=0, tiled=True)
+    theirs = swap(mine[:, : rows + ID_ROWS], CORE_SWAP)
+    mixed = window_mixing(mine, theirs, share)
+    returned = lax.all_to_all(mixed, "seq", split_axis=0, concat_axis=0, tiled=True)
+    near_mix = (
+        returned.reshape(head_count, share, 2, HD).transpose(2, 1, 0, 3).reshape(rows, head_count * HD)
+    )
+    far_mix = swap(near_mix, CHIP_SWAP)
+
+    own_out = jnp.concatenate([self_out_weight, cross_out_weight], axis=0)
+    own_other_out = swap(own_out, CORE_SWAP)
+    chip_other_out = swap(chip_out, CORE_SWAP)
+    split = self_out_weight.shape[0]
+
+    def in_order(first, second):
+        return jnp.where(
+            core == 0,
+            jnp.concatenate([first[:split], second[:split]], axis=0),
+            jnp.concatenate([second[:split], first[:split]], axis=0),
+        )
+
+    summed = jnp.dot(
+        near_mix, in_order(own_out, own_other_out), preferred_element_type=jnp.float32
+    ) + jnp.dot(far_mix, in_order(chip_out, chip_other_out), preferred_element_type=jnp.float32)
+    hidden = vox.astype(jnp.float32) + summed
+    spread = jnp.mean(hidden * hidden, axis=-1, keepdims=True)
+    normed = (hidden * lax.rsqrt(spread + 1e-06) * cross_norm_gain).astype(jnp.bfloat16)
+    own_hidden = lax.dynamic_slice_in_dim(hidden, chip * share, share, 0)
+
+    def queries_of(weight):
+        return (
+            jnp.dot(normed, weight, preferred_element_type=jnp.float32).astype(jnp.bfloat16)
+            * HD ** (-0.5)
+        ).astype(jnp.bfloat16)
+
+    other_keyval = swap(own_keyval, CORE_SWAP)
+    own_cross = cross_mixing(queries_of(cross_q_weight), own_keyval)
+    other_cross = cross_mixing(queries_of(other_q), other_keyval)
+    both = jnp.concatenate([own_cross, other_cross], axis=1).reshape(2, share, 2 * local_width)
+    kept = lax.dynamic_index_in_dim(both, chip, axis=0, keepdims=False)
+    arrived = swap(lax.dynamic_index_in_dim(both, 1 - chip, axis=0, keepdims=False), CHIP_SWAP)
+    near_out = jnp.concatenate([own_out[split:], own_other_out[split:]], axis=0)
+    far_out = jnp.concatenate([chip_out[split:], chip_other_out[split:]], axis=0)
+    crossed = jnp.dot(kept, near_out, preferred_element_type=jnp.float32) + jnp.dot(
+        arrived, far_out, preferred_element_type=jnp.float32
+    )
+    return (own_hidden + crossed).astype(jnp.bfloat16)
 
 
 def rms_norm(matrix, gain):
@@ -40,7 +362,7 @@
     return mixed.astype(jnp.bfloat16).reshape(slot_count, head_count * HD)
 
 
-def shards(
+def by_owner(
     voxels,
     destination,
     cond,
@@ -177,8 +499,9 @@
 
 
 def solution(mesh):
+    heads_match = mesh.shape["mp"] == 4 and mesh.shape["seq"] == 8
     return jax.shard_map(
-        shards,
+        by_head if heads_match else by_owner,
         mesh=mesh,
         in_specs=(
             P("seq", None),

time: 406 us -> 248 us (0.61)
  Pallas kernels: 0 us -> 72.6 us
  waiting for transfers between devices: 184 us -> 121 us
  matrix products: 72.3 us -> 9.66 us
  local copies, waits for them, and re-layouts: 74.4 us -> 14 us
  other arithmetic: 41 us -> 0.92 us
    all_to_all x3 -> x2, waiting for transfers between devices: 87.9 us -> 9.73 us  [the longest x1 9.73 us: by_head(): lax.all_to_all(mixed, 'seq', split_axis=0, concat_axis=0, tiled=True)]
    all_gather x2 -> x1, waiting for transfers between devices: 0.02 us -> 74 us  [by_head(): lax.all_gather(jnp.concatenate(cond_pair, axis=1), 'seq', axis=0, tiled=T...]
    pallas_call x0 -> x4, Pallas kernels: none -> 72.6 us  [the longest x1 41.9 us: window_mixing(): pl.pallas_call(window_kernel, out_shape=jax.ShapeDtypeStruct((sources, pa...]
    dot_general x23 -> x8, matrix products: 72.3 us -> 9.66 us  [the longest x2 3.09 us: queries_of(): jnp.dot(normed, weight, preferred_element_type=jnp.float32)]
    psum x1 -> x0, waiting for transfers between devices: 57.5 us -> none  [shards(): lax.psum(jnp.dot(window_mix, self_out_weight, preferred_element_type=jnp....]
    reduce_scatter x1 -> x0, waiting for transfers between devices: 38.1 us -> none  [shards(): lax.psum_scatter(jnp.dot(cross_mix, cross_out_weight, preferred_element_t...]
    ppermute x0 -> x9, waiting for transfers between devices: none -> 37.1 us  [swap(): return lax.ppermute(array, 'mp', pairs)]
    reduce_sum x11 -> x0, other arithmetic: 34.7 us -> none  [the longest x8 31.8 us: fold_block(): totals = totals * rescale + jnp.sum(weights, axis=-1)]
  transfers between devices with their start and end apart: 7 -> 12, of which waited for: 4 -> 6; matrix products, arithmetic and copies ran while one was open for 19% -> 6% of each run, Pallas kernels for 0% -> 24%
where the time goes in v1:
time: 248 us
  waiting for transfers between devices  121 us (49%)
  Pallas kernels  72.6 us (29%)
  starting transfers between devices  16.1 us (6%)
  local copies, waits for them, and re-layouts  14 us (6%)
  between operations  13.6 us (5%)
  matrix products  9.66 us (4%)
    all_gather x1, waiting for transfers between devices, by_head(): lax.all_gather(jnp.concatenate(cond_pair, axis=1), 'seq', axis=0, tiled=T...  74 us
    pallas_call x1, Pallas kernels, window_mixing(): pl.pallas_call(window_kernel, out_shape=jax.ShapeDtypeStruct((sources, pa...  41.9 us
    ppermute x9, waiting for transfers between devices, swap(): return lax.ppermute(array, 'mp', pairs)  37.1 us
    pallas_call x2, Pallas kernels, cross_mixing(): pl.pallas_call(cross_kernel, out_shape=jax.ShapeDtypeStruct((rows, local_...  25.4 us
    all_to_all x1, waiting for transfers between devices, by_head(): lax.all_to_all(mixed, 'seq', split_axis=0, concat_axis=0, tiled=True)  9.73 us
    all_to_all x1, starting transfers between devices, by_head(): mine = lax.all_to_all(sent, 'seq', split_axis=0, concat_axis=0, tiled=True)  7.31 us
    pallas_call x1, Pallas kernels, project(): pl.pallas_call(project_kernel, out_shape=jax.ShapeDtypeStruct((heads, blo...  5.34 us
    ppermute x9, starting transfers between devices, swap(): return lax.ppermute(array, 'mp', pairs)  5.16 us
  transfers between devices with their start and end apart: 12, of which 6 were waited for; matrix products, arithmetic and copies ran while one was open for 6% of the time, Pallas kernels for 24%

profile of v1, /device:TPU:0, one launch (start us, length us, event | category | flops | bytes accessed | tf_op | source)
XLA Modules:
  0.0 247.9 jit_solution(9036810664319282566)
XLA Ops:
  6.5 1.9 convolution_convert_fusion
  10.9 2.8 %collective-permute-done.other_ref = bf16[3,1024,256]{2,1,0:T(8,128)(2,1)} collective-permute-done((bf16[3,1024,256]{2,1,0:T(8,128)(2,1)S(1)}, bf16[3,1024,256]{2,1,0:T(8,128)(2,1)}, u32[]{:S(2)}, u32[]{:S(2)}) %collective-permute-start) | collective-permute-done | bytes 1572896 | tf_op jit(solution)/shard_map/ppermute | solution.py:234
  13.7 5.3 %shard_map.100 = bf16[8,592,128]{2,1,0:T(8,128)(2,1)S(1)} custom-call(s32[1]{0:T(128)} %bitcast.2.core_ref, bf16[384,1024]{1,0:T(8,128)(2,1)S(1)} %bitcast.31, f32[1,1024]{1,0:T(1,128)S(1)} %bitcast.33, bf16[16,128]{1,0:T(8,128)(2,1)S(1)} %pad_maximum_fusion.2.ids_ref, bf16[3,1024,256]{2,1,0:T(8,128)(2,1)S(1)} %copy-done.5, ...), custom_call_target="tpu_custom_call" | custom-call | tf_op jit(solution)/shard_map/pallas_call | solution.py:86
  19.1 1.1 copy-done.2
  21.0 7.3 %all-to-all-start = ((bf16[8,592,128]{2,1,0:T(8,128)(2,1)}), bf16[8,592,128]{2,1,0:T(8,128)(2,1)S(1)}, u32[]{:S(2)}, u32[]{:S(2)}) async-start(bf16[8,592,128]{2,1,0:T(8,128)(2,1)} %copy-done.2), calls=%async_computation | async-start | bytes 2424832 | tf_op jit(solution)/shard_map/all_to_all | solution.py:285
  28.3 74.0 %all-gather.2.cloned.1.call-done.key_ref.value_ref = bf16[4096,512]{1,0:T(8,128)(2,1)} async-done(((bf16[512,512]{1,0:T(8,128)(2,1)}), bf16[4096,512]{1,0:T(8,128)(2,1)}) %all-gather.2.cloned.1.call-update) | async-done | bytes 4194320 | tf_op jit(solution)/shard_map/all_gather | solution.py:263
  102.4 1.9 constant_dynamic-update-slice_fusion.1
  105.2 1.3 collective-permute-start.4
  107.1 23.9 %collective-permute-done.4 = bf16[512,1024]{1,0:T(8,128)(2,1)} collective-permute-done((bf16[512,1024]{1,0:T(8,128)(2,1)}, bf16[512,1024]{1,0:T(8,128)(2,1)}, u32[]{:S(2)}, u32[]{:S(2)}) %collective-permute-start.4) | collective-permute-done | bytes 1048608 | tf_op jit(solution)/shard_map/ppermute | solution.py:234
  131.0 41.9 %shard_map.101 = bf16[8,192,128]{2,1,0:T(8,128)(2,1)} custom-call(bf16[8,592,128]{2,1,0:T(8,128)(2,1)S(1)} %all-to-all-done.mine_ref, bf16[8,400,128]{2,1,0:T(8,128)(2,1)S(1)} %collective-permute-done.1.theirs_ref), custom_call_target="tpu_custom_call" | custom-call | tf_op jit(solution)/shard_map/pallas_call | solution.py:166
  172.9 3.6 %all-to-all-start.1 = ((bf16[8,192,128]{2,1,0:T(8,128)(2,1)}), bf16[8,192,128]{2,1,0:T(8,128)(2,1)S(1)}, u32[]{:S(2)}, u32[]{:S(2)}) async-start(bf16[8,192,128]{2,1,0:T(8,128)(2,1)} %shard_map.101), calls=%async_computation.1 | async-start | bytes 786432 | tf_op jit(solution)/shard_map/all_to_all | solution.py:288
  177.1 2.1 fusion.41
  179.1 9.7 %all-to-all-done.1 = bf16[8,192,128]{2,1,0:T(8,128)(2,1)S(1)} async-done(((bf16[8,192,128]{2,1,0:T(8,128)(2,1)}), bf16[8,192,128]{2,1,0:T(8,128)(2,1)S(1)}, u32[]{:S(2)}, u32[]{:S(2)}) %all-to-all-start.1) | async-done | bytes 393248 | tf_op jit(solution)/shard_map/all_to_all | solution.py:288
  189.9 1.4 collective-permute-start.3
  191.3 2.1 fusion.40
  193.4 2.1 fusion.42
  195.5 5.3 %collective-permute-done.3 = bf16[384,512]{0,1:T(8,128)(2,1)S(1)} collective-permute-done((bf16[384,512]{0,1:T(8,128)(2,1)S(1)}, bf16[384,512]{0,1:T(8,128)(2,1)S(1)}, u32[]{:S(2)}, u32[]{:S(2)}) %collective-permute-start.3) | collective-permute-done | bytes 393248 | tf_op jit(solution)/shard_map/ppermute | solution.py:234
  202.9 1.6 fusion.2.query_ref
  204.5 1.5 fusion.3.query_ref
  206.0 12.4 %shard_map.102 = bf16[384,256]{1,0:T(8,128)(2,1)S(1)} custom-call(bf16[384,256]{1,0:T(8,128)(2,1)S(1)} %fusion.2.query_ref, bf16[4096,512]{1,0:T(8,128)(2,1)S(1)} %copy-done.1, bf16[4096,512]{1,0:T(8,128)(2,1)S(1)} %copy-done.1), custom_call_target="tpu_custom_call" | custom-call | tf_op jit(solution)/shard_map/pallas_call | solution.py:218
  218.4 13.1 %shard_map.103 = bf16[384,256]{1,0:T(8,128)(2,1)S(1)} custom-call(bf16[384,256]{1,0:T(8,128)(2,1)S(1)} %fusion.3.query_ref, bf16[4096,512]{1,0:T(8,128)(2,1)} %collective-permute-done.7.key_ref.value_ref, bf16[4096,512]{1,0:T(8,128)(2,1)} %collective-permute-done.7.key_ref.value_ref), custom_call_target="tpu_custom_call" | custom-call | tf_op jit(solution)/shard_map/pallas_call | solution.py:218
  233.1 5.1 %collective-permute-done.8 = bf16[192,512]{1,0:T(8,128)(2,1)} collective-permute-done((bf16[192,512]{1,0:T(8,128)(2,1)}, bf16[192,512]{1,0:T(8,128)(2,1)}, u32[]{:S(2)}, u32[]{:S(2)}) %collective-permute-start.8) | collective-permute-done | bytes 196640 | tf_op jit(solution)/shard_map/ppermute | solution.py:234
  238.2 1.7 fusion.18
  239.9 1.1 fusion.1
  (68 shorter events, 10.1 us)
Async XLA Ops:
  6.5 4.3 %copy-start = (bf16[768,1024]{1,0:T(8,128)(2,1)S(1)}, bf16[768,1024]{1,0:T(8,128)(2,1)}, u32[]{:S(2)}) copy-start(bf16[768,1024]{1,0:T(8,128)(2,1)} %param.10) | copy-start | bytes 4718596
  6.5 95.8 %all-gather.2.cloned.1.call-start = ((), (), s32[]{:S(2)}) async-start(), calls=%async_computation.2 | async-start | bytes 4718592 | tf_op jit(solution)/shard_map/all_gather | solution.py:263
  6.5 2.0 copy-start.15
  6.5 2.1 copy-start.16
  8.7 1.4 copy-start.5
  8.7 1.9 copy-start.14
  9.1 4.6 %copy-start.6 = (f32[1024]{0:T(1024)S(1)}, f32[1024]{0:T(1024)}, u32[]{:S(2)}) copy-start(f32[1024]{0:T(1024)} %param.13) | copy-start | bytes 12292
  10.1 3.6 %collective-permute-start = (bf16[3,1024,256]{2,1,0:T(8,128)(2,1)S(1)}, bf16[3,1024,256]{2,1,0:T(8,128)(2,1)}, u32[]{:S(2)}, u32[]{:S(2)}) collective-permute-start(bf16[3,1024,256]{2,1,0:T(8,128)(2,1)S(1)} %copy-done.5), channel_id=1, source_target_pairs={{0,1},{1,0},{2,3},{3,2},{4,5},{5,4},{6,7},{7,6},{8,9},{9,8},{10,11... | collective-permute-start | bytes 4718600 | tf_op jit(solution)/shard_map/ppermute | solution.py:234
  21.0 83.3 %copy-start.7 = (bf16[256,1024]{1,0:T(8,128)(2,1)S(1)}, bf16[256,1024]{1,0:T(8,128)(2,1)}, u32[]{:S(2)}) copy-start(bf16[256,1024]{1,0:T(8,128)(2,1)} %param.19) | copy-start | bytes 1572868
  21.0 85.4 %all-to-all-start = ((bf16[8,592,128]{2,1,0:T(8,128)(2,1)}), bf16[8,592,128]{2,1,0:T(8,128)(2,1)S(1)}, u32[]{:S(2)}, u32[]{:S(2)}) async-start(bf16[8,592,128]{2,1,0:T(8,128)(2,1)} %copy-done.2), calls=%async_computation | async-start | bytes 2424832 | tf_op jit(solution)/shard_map/all_to_all | solution.py:285
  102.4 116.0 %collective-permute-start.7 = (bf16[4096,512]{1,0:T(8,128)(2,1)}, bf16[4096,512]{1,0:T(8,128)(2,1)}, u32[]{:S(2)}, u32[]{:S(2)}) collective-permute-start(bf16[4096,512]{1,0:T(8,128)(2,1)} %all-gather.2.cloned.1.call-done.key_ref.value_ref), channel_id=1, source_target_pairs={{0,1},{1,0},{2,3},{3,2},{4,5},{5,4},{6,7},{7,6},{8,9},{9,8},{10,11... | collective-permute-start | bytes 12582920 | tf_op jit(solution)/shard_map/ppermute | solution.py:234
  105.2 25.8 %collective-permute-start.4 = (bf16[512,1024]{1,0:T(8,128)(2,1)}, bf16[512,1024]{1,0:T(8,128)(2,1)}, u32[]{:S(2)}, u32[]{:S(2)}) collective-permute-start(bf16[512,1024]{1,0:T(8,128)(2,1)} %constant_dynamic-update-slice_fusion), channel_id=1, source_target_pairs={{0,2},{2,0},{1,3},{3,1},{4,6},{6,4},{5,7},{7,5},{8,10},{10,8},{9,1... | collective-permute-start | bytes 3145736 | tf_op jit(solution)/shard_map/ppermute | solution.py:234
  106.5 24.5 %collective-permute-start.1 = (bf16[8,400,128]{2,1,0:T(8,128)(2,1)S(1)}, bf16[8,400,128]{2,1,0:T(8,128)(2,1)S(1)}, u32[]{:S(2)}, u32[]{:S(2)}) collective-permute-start(bf16[8,400,128]{2,1,0:T(8,128)(2,1)S(1)} %slice.39), channel_id=1, source_target_pairs={{0,1},{1,0},{2,3},{3,2},{4,5},{5,4},{6,7},{7,6},{8,9},{9,8},{10,11... | collective-permute-start | bytes 2457608 | tf_op jit(solution)/shard_map/ppermute | solution.py:234
  106.8 84.5 %collective-permute-start.2 = (bf16[512,1024]{1,0:T(8,128)(2,1)}, bf16[512,1024]{1,0:T(8,128)(2,1)}, u32[]{:S(2)}, u32[]{:S(2)}) collective-permute-start(bf16[512,1024]{1,0:T(8,128)(2,1)} %constant_dynamic-update-slice_fusion), channel_id=1, source_target_pairs={{0,1},{1,0},{2,3},{3,2},{4,5},{5,4},{6,7},{7,6},{8,9},{9,8},{10,11... | collective-permute-start | bytes 3145736 | tf_op jit(solution)/shard_map/ppermute | solution.py:234
  131.0 62.4 %collective-permute-start.5 = (bf16[512,1024]{1,0:T(8,128)(2,1)}, bf16[512,1024]{1,0:T(8,128)(2,1)}, u32[]{:S(2)}, u32[]{:S(2)}) collective-permute-start(bf16[512,1024]{1,0:T(8,128)(2,1)} %collective-permute-done.4), channel_id=1, source_target_pairs={{0,1},{1,0},{2,3},{3,2},{4,5},{5,4},{6,7},{7,6},{8,9},{9,8},{10,11... | collective-permute-start | bytes 3145736 | tf_op jit(solution)/shard_map/ppermute | solution.py:234
  172.9 16.0 %all-to-all-start.1 = ((bf16[8,192,128]{2,1,0:T(8,128)(2,1)}), bf16[8,192,128]{2,1,0:T(8,128)(2,1)S(1)}, u32[]{:S(2)}, u32[]{:S(2)}) async-start(bf16[8,192,128]{2,1,0:T(8,128)(2,1)} %shard_map.101), calls=%async_computation.1 | async-start | bytes 786432 | tf_op jit(solution)/shard_map/all_to_all | solution.py:288
  176.5 28.0 %collective-permute-start.6 = (bf16[1024,256]{1,0:T(8,128)(2,1)}, bf16[1024,256]{1,0:T(8,128)(2,1)}, u32[]{:S(2)}, u32[]{:S(2)}) collective-permute-start(bf16[1024,256]{1,0:T(8,128)(2,1)} %param.17), channel_id=1, source_target_pairs={{0,1},{1,0},{2,3},{3,2},{4,5},{5,4},{6,7},{7,6},{8,9},{9,8},{10,11... | collective-permute-start | bytes 1572872 | tf_op jit(solution)/shard_map/ppermute | solution.py:234
  189.9 5.5 %copy-start.11 = (bf16[384,512]{0,1:T(8,128)(2,1)}, bf16[384,512]{0,1:T(8,128)(2,1)S(1)}, u32[]{:S(2)}) copy-start(bf16[384,512]{0,1:T(8,128)(2,1)S(1)} %reshape.45) | copy-start | bytes 1179652
  189.9 10.8 %collective-permute-start.3 = (bf16[384,512]{0,1:T(8,128)(2,1)S(1)}, bf16[384,512]{0,1:T(8,128)(2,1)S(1)}, u32[]{:S(2)}, u32[]{:S(2)}) collective-permute-start(bf16[384,512]{0,1:T(8,128)(2,1)S(1)} %reshape.45), channel_id=1, source_target_pairs={{0,2},{2,0},{1,3},{3,1},{4,6},{6,4},{5,7},{7,5},{8,10},{10,8},{9,1... | collective-permute-start | bytes 1179656 | tf_op jit(solution)/shard_map/ppermute | solution.py:234
  200.7 1.4 copy-start.12
  202.9 3.1 %copy-start.1 = (bf16[4096,512]{1,0:T(8,128)(2,1)S(1)}, bf16[4096,512]{1,0:T(8,128)(2,1)}, u32[]{:S(2)}) copy-start(bf16[4096,512]{1,0:T(8,128)(2,1)} %all-gather.2.cloned.1.call-done.key_ref.value_ref) | copy-start | bytes 12582916
  232.2 6.0 %collective-permute-start.8 = (bf16[192,512]{1,0:T(8,128)(2,1)}, bf16[192,512]{1,0:T(8,128)(2,1)}, u32[]{:S(2)}, u32[]{:S(2)}) collective-permute-start(bf16[192,512]{1,0:T(8,128)(2,1)} %dynamic-slice_bitcast_fusion), channel_id=1, source_target_pairs={{0,2},{2,0},{1,3},{3,1},{4,6},{6,4},{5,7},{7,5},{8,10},{10,8},{9,1... | collective-permute-start | bytes 589832 | tf_op jit(solution)/shard_map/ppermute | solution.py:234
  233.1 6.8 %copy-start.8 = (bf16[256,1024]{1,0:T(8,128)(2,1)S(1)}, bf16[256,1024]{1,0:T(8,128)(2,1)}, u32[]{:S(2)}) copy-start(bf16[256,1024]{1,0:T(8,128)(2,1)} %param.19) | copy-start | bytes 1572868
  233.1 6.8 %copy-start.9 = (bf16[256,1024]{1,0:T(8,128)(2,1)S(1)}, bf16[256,1024]{1,0:T(8,128)(2,1)}, u32[]{:S(2)}) copy-start(bf16[256,1024]{1,0:T(8,128)(2,1)} %get-tuple-element.7) | copy-start | bytes 1572868
  (5 other events, 5.2 us)
Sparse Core Ops, SparseCore 0:
  10.1 92.2 all-gather.1

commit v2 on v1

--- a/solution.py
+++ b/solution.py
@@ -127,35 +127,32 @@
     ).astype(jnp.bfloat16)
     columns = jnp.transpose(read_ids(mine_ref, source, rows))
     query_ids = jnp.concatenate([columns[:, g : g + 1] for g in range(groups)], axis=0)
-    low = low_lanes((rows, LANES))
-    one = jnp.ones((), jnp.bfloat16)
-
-    def fold(ref, index, total):
+
+    def fold(ref, index, state):
+        sums, total = state
         keyval = ref[index, :rows]
         key_ids = read_ids(ref, index, rows)
         scores = lax.dot_general(
             query, keyval, (((1,), (1,)), ((), ())), preferred_element_type=jnp.float32
         )
-        weights = jnp.concatenate(
-            [
-                jnp.where(
-                    query_ids == key_ids[g : g + 1],
-                    jnp.exp(scores[:, g * LANES : (g + 1) * LANES]),
-                    0.0,
-                ).astype(jnp.bfloat16)
-                for g in range(groups)
-            ],
-            axis=1,
-        )
-        return total + jnp.dot(
-            weights, jnp.where(low, one, keyval), preferred_element_type=jnp.float32
-        )
-
-    def body(index, total):
-        return fold(theirs_ref, index, fold(mine_ref, index, total))
-
-    total = lax.fori_loop(0, sources, body, jnp.zeros((rows, LANES), jnp.float32))
-    mixed = total / swap_halves(total)
+        weights = [
+            jnp.where(
+                query_ids == key_ids[g : g + 1],
+                jnp.exp(scores[:, g * LANES : (g + 1) * LANES]),
+                0.0,
+            )
+            for g in range(groups)
+        ]
+        sums = functools.reduce(jnp.add, weights, sums)
+        rounded = jnp.concatenate([part.astype(jnp.bfloat16) for part in weights], axis=1)
+        return sums, total + jnp.dot(rounded, keyval, preferred_element_type=jnp.float32)
+
+    def body(index, state):
+        return fold(theirs_ref, index, fold(mine_ref, index, state))
+
+    nothing = jnp.zeros((rows, LANES), jnp.float32)
+    sums, total = lax.fori_loop(0, sources, body, (nothing, nothing))
+    mixed = total / jnp.sum(sums, axis=-1, keepdims=True)
     out_ref[0] = jnp.where(low_packed, swap_halves(mixed[:packed]), mixed[packed:]).astype(
         jnp.bfloat16
     )
@@ -173,61 +170,72 @@
         ],
         out_specs=pl.BlockSpec((1, packed, LANES), lambda source: (source, 0, 0)),
         compiler_params=pltpu.CompilerParams(vmem_limit_bytes=VMEM_LIMIT),
+        cost_estimate=pl.CostEstimate(
+            flops=32 * LANES * (sources * packed) ** 2,
+            transcendentals=8 * (sources * packed) ** 2,
+            bytes_accessed=2 * (mine.size + theirs.size),
+        ),
     )(mine, theirs)
 
 
-def cross_kernel(query_ref, key_ref, value_ref, out_ref, score_ref):
-    rows = query_ref.shape[0]
-    tokens = key_ref.shape[0]
+def cross_kernel(query_ref, keyval_ref, out_ref, score_ref):
+    rows, local_width = query_ref.shape
+    tokens = keyval_ref.shape[0]
     chunk = math.gcd(tokens, 512)
     low = low_lanes((rows, LANES))
-    wire = query_ref[...]
     zero = jnp.zeros((), jnp.bfloat16)
-    ones = jnp.ones((chunk, LANES), jnp.bfloat16)
-    mixes = []
-    for head in range(2):
-        query = jnp.where(low == (head == 0), wire, zero)
-        peak = jnp.full((rows, LANES), -jnp.inf, jnp.float32)
-        for start in range(0, tokens, chunk):
-            scores = lax.dot_general(
-                query,
-                key_ref[start : start + chunk],
-                (((1,), (1,)), ((), ())),
-                preferred_element_type=jnp.float32,
-            )
-            score_ref[head, :, start : start + chunk] = scores
-            for g in range(chunk // LANES):
-                peak = jnp.maximum(peak, scores[:, g * LANES : (g + 1) * LANES])
-        row_max = jnp.max(peak, axis=-1, keepdims=True)
-        total = jnp.zeros((rows, 2 * LANES), jnp.float32)
-        for start in range(0, tokens, chunk):
-            weights = jnp.exp(score_ref[head, :, start : start + chunk] - row_max).astype(
-                jnp.bfloat16
-            )
-            values = jnp.concatenate([value_ref[start : start + chunk], ones], axis=1)
-            total = total + jnp.dot(weights, values, preferred_element_type=jnp.float32)
-        mixes.append(total[:, :LANES] / total[:, LANES:])
-    out_ref[...] = jnp.where(low, mixes[0], mixes[1]).astype(jnp.bfloat16)
+
+    def lane_groups(values):
+        return [values[:, g : g + LANES] for g in range(0, chunk, LANES)]
+
+    for pair in range(0, local_width, LANES):
+        mixes = []
+        for head in range(2):
+            query = jnp.where(low == (head == 0), query_ref[:, pair : pair + LANES], zero)
+            peak = jnp.full((rows, LANES), -jnp.inf, jnp.float32)
+            for start in range(0, tokens, chunk):
+                scores = lax.dot_general(
+                    query,
+                    keyval_ref[start : start + chunk, pair : pair + LANES],
+                    (((1,), (1,)), ((), ())),
+                    preferred_element_type=jnp.float32,
+                )
+                score_ref[head, :, start : start + chunk] = scores
+                peak = functools.reduce(jnp.maximum, lane_groups(scores), peak)
+            row_max = jnp.max(peak, axis=-1, keepdims=True)
+            sums = jnp.zeros((rows, LANES), jnp.float32)
+            total = jnp.zeros((rows, LANES), jnp.float32)
+            for start in range(0, tokens, chunk):
+                weights = jnp.exp(score_ref[head, :, start : start + chunk] - row_max)
+                sums = functools.reduce(jnp.add, lane_groups(weights), sums)
+                total = total + jnp.dot(
+                    weights.astype(jnp.bfloat16),
+                    keyval_ref[
+                        start : start + chunk, local_width + pair : local_width + pair + LANES
+                    ],
+                    preferred_element_type=jnp.float32,
+                )
+            mixes.append(total / jnp.sum(sums, axis=-1, keepdims=True))
+        out_ref[:, pair : pair + LANES] = jnp.where(low, mixes[0], mixes[1]).astype(jnp.bfloat16)
 
 
 def cross_mixing(queries, keyval):
     rows, local_width = queries.shape
     tokens = keyval.shape[0]
-    pairs = local_width // LANES
-    block = rows // 2
+    scored = rows * tokens * local_width // HD
     return pl.pallas_call(
         cross_kernel,
         out_shape=jax.ShapeDtypeStruct((rows, local_width), jnp.bfloat16),
-        grid=(pairs, rows // block),
-        in_specs=[
-            pl.BlockSpec((block, LANES), lambda pair, part: (part, pair)),
-            pl.BlockSpec((tokens, LANES), lambda pair, part: (0, pair)),
-            pl.BlockSpec((tokens, LANES), lambda pair, part: (0, pairs + pair)),
-        ],
-        out_specs=pl.BlockSpec((block, LANES), lambda pair, part: (part, pair)),
-        scratch_shapes=[pltpu.VMEM((2, block, tokens), jnp.float32)],
+        in_specs=[pl.BlockSpec(memory_space=pltpu.VMEM)] * 2,
+        out_specs=pl.BlockSpec(memory_space=pltpu.VMEM),
+        scratch_shapes=[pltpu.VMEM((2, rows, tokens), jnp.float32)],
         compiler_params=pltpu.CompilerParams(vmem_limit_bytes=VMEM_LIMIT),
-    )(queries, keyval, keyval)
+        cost_estimate=pl.CostEstimate(
+            flops=8 * LANES * scored,
+            transcendentals=scored,
+            bytes_accessed=2 * (keyval.size + 2 * queries.size),
+        ),
+    )(queries, keyval)
 
 
 def swap(array, pairs):
@@ -290,6 +298,7 @@
         returned.reshape(head_count, share, 2, HD).transpose(2, 1, 0, 3).reshape(rows, head_count * HD)
     )
     far_mix = swap(near_mix, CHIP_SWAP)
+    own_keyval, chip_out, _ = lax.optimization_barrier((own_keyval, chip_out, mixed))
 
     own_out = jnp.concatenate([self_out_weight, cross_out_weight], axis=0)
     own_other_out = swap(own_out, CORE_SWAP)

time: 248 us -> 188 us (0.76)
  waiting for transfers between devices: 121 us -> 23.5 us
  blocking collectives: 0 us -> 48.7 us
  starting transfers between devices: 16.1 us -> 8.02 us
  local copies, waits for them, and re-layouts: 14 us -> 11 us
    all_gather x1, waiting for transfers between devices: 74 us -> 0.01 us  [by_head(): lax.all_gather(jnp.concatenate(cond_pair, axis=1), 'seq', axis=0, tiled=T...]
    all_to_all x0 -> x1, blocking collectives: none -> 48.7 us  [by_head(): mine = lax.all_to_all(sent, 'seq', split_axis=0, concat_axis=0, tiled=True)]
    ppermute x9, waiting for transfers between devices: 37.1 us -> 18.2 us  [swap(): return lax.ppermute(array, 'mp', pairs)]
    all_to_all x1 -> x0, starting transfers between devices: 7.31 us -> none  [by_head(): mine = lax.all_to_all(sent, 'seq', split_axis=0, concat_axis=0, tiled=True)]
    all_to_all x1, waiting for transfers between devices: 9.73 us -> 5.28 us  [by_head(): lax.all_to_all(mixed, 'seq', split_axis=0, concat_axis=0, tiled=True)]
    pallas_call x2, Pallas kernels: 25.4 us -> 21.3 us  [cross_mixing(): pl.pallas_call(cross_kernel, out_shape=jax.ShapeDtypeStruct((rows, local_...]
    unnamed x35 -> x31, local copies, waits for them, and re-layouts: 4.92 us -> 1.68 us
    pallas_call x1, Pallas kernels: 41.9 us -> 44.4 us  [window_mixing(): pl.pallas_call(window_kernel, out_shape=jax.ShapeDtypeStruct((sources, pa...]
  transfers between devices with their start and end apart: 12 -> 11, of which waited for: 6 -> 5; matrix products, arithmetic and copies ran while one was open for 6% -> 8% of each run, Pallas kernels for 24% -> 32%
where the time goes in v2:
time: 188 us; the launch traced here: 187 us
  Pallas kernels  71.2 us (38%)
  blocking collectives  48.7 us (26%)
  waiting for transfers between devices  23.5 us (12%)
  between operations  13.7 us (7%)
  local copies, waits for them, and re-layouts  11 us (6%)
  matrix products  10 us (5%)
  starting transfers between devices  8.02 us (4%)
    all_to_all x1, blocking collectives, by_head(): mine = lax.all_to_all(sent, 'seq', split_axis=0, concat_axis=0, tiled=True)  48.7 us
    pallas_call x1, Pallas kernels, window_mixing(): pl.pallas_call(window_kernel, out_shape=jax.ShapeDtypeStruct((sources, pa...  44.4 us
    pallas_call x2, Pallas kernels, cross_mixing(): pl.pallas_call(cross_kernel, out_shape=jax.ShapeDtypeStruct((rows, local_...  21.3 us
    ppermute x9, waiting for transfers between devices, swap(): return lax.ppermute(array, 'mp', pairs)  18.2 us
    pallas_call x1, Pallas kernels, project(): pl.pallas_call(project_kernel, out_shape=jax.ShapeDtypeStruct((heads, blo...  5.45 us
    all_to_all x1, waiting for transfers between devices, by_head(): lax.all_to_all(mixed, 'seq', split_axis=0, concat_axis=0, tiled=True)  5.28 us
    ppermute x9, starting transfers between devices, swap(): return lax.ppermute(array, 'mp', pairs)  4.38 us
  transfers between devices with their start and end apart: 11, of which 5 were waited for; matrix products, arithmetic and copies ran while one was open for 8% of the time, Pallas kernels for 32%

profile of v2, /device:TPU:0, one launch (start us, length us, event | category | flops | bytes accessed | tf_op | source)
XLA Modules:
  0.0 187.0 jit_solution(16763107471700364251)
XLA Ops:
  6.5 1.9 %convolution_convert_fusion = bf16[512,256]{1,0:T(8,128)(2,1)S(1)} fusion(bf16[512,1024]{1,0:T(8,128)(2,1)} %param.12, bf16[2,1024,256]{2,1,0:T(8,128)(2,1)} %param.18), kind=kOutput, calls=%fused_computation.6 | convolution fusion | flops 268566528 | bytes 1835008 | tf_op jit(solution)/shard_map/dot_general | solution.py:268
  9.1 0.8 pad_maximum_fusion
  10.8 3.0 %collective-permute-done.other_ref = bf16[3,1024,256]{2,1,0:T(8,128)(2,1)} collective-permute-done((bf16[3,1024,256]{2,1,0:T(8,128)(2,1)}, bf16[3,1024,256]{2,1,0:T(8,128)(2,1)}, u32[]{:S(2)}, u32[]{:S(2)}) %collective-permute-start) | collective-permute-done | bytes 1572896 | tf_op jit(solution)/shard_map/ppermute | solution.py:242
  13.9 5.4 %shard_map.100 = bf16[8,592,128]{2,1,0:T(8,128)(2,1)S(1)} custom-call(s32[1]{0:T(128)} %bitcast.2.core_ref, bf16[384,1024]{1,0:T(8,128)(2,1)S(1)} %bitcast.31, f32[1,1024]{1,0:T(1,128)S(1)} %bitcast.33, bf16[16,128]{1,0:T(8,128)(2,1)S(1)} %pad_maximum_fusion.2.ids_ref, bf16[3,1024,256]{2,1,0:T(8,128)(2,1)} %own_ref.1, ...), custom_call_target="tpu_custom_call" | custom-call | tf_op jit(solution)/shard_map/pallas_call | solution.py:86
  19.3 48.7 %all_to_all.10.mine_ref = bf16[8,592,128]{2,1,0:T(8,128)(2,1)S(1)} all-to-all(bf16[8,592,128]{2,1,0:T(8,128)(2,1)S(1)} %shard_map.100), channel_id=1, replica_groups=mesh['seq'=8,'mp'=4] {'seq'}, dimensions={0} | all-to-all | bytes 2424832 | tf_op jit(solution)/shard_map/all_to_all | solution.py:293
  68.2 0.8 constant_dynamic-update-slice_fusion.1
  69.1 0.8 constant_dynamic-update-slice_fusion
  70.0 1.4 collective-permute-start.4
  71.4 44.4 %shard_map.101 = bf16[8,192,128]{2,1,0:T(8,128)(2,1)} custom-call(bf16[8,592,128]{2,1,0:T(8,128)(2,1)S(1)} %all_to_all.10.mine_ref, bf16[8,400,128]{2,1,0:T(8,128)(2,1)S(1)} %collective-permute-done.1.theirs_ref), custom_call_target="tpu_custom_call" | custom-call | flops 9663676416 | bytes 2031616 | tf_op jit(solution)/shard_map/pallas_call | solution.py:163
  116.5 3.6 %all-to-all-start.1 = ((bf16[8,192,128]{2,1,0:T(8,128)(2,1)}), bf16[8,192,128]{2,1,0:T(8,128)(2,1)S(1)}, u32[]{:S(2)}, u32[]{:S(2)}) async-start(bf16[8,192,128]{2,1,0:T(8,128)(2,1)} %shard_map.101), calls=%async_computation.1 | async-start | bytes 786432 | tf_op jit(solution)/shard_map/all_to_all | solution.py:296
  120.5 4.3 %collective-permute-done.2 = bf16[512,1024]{1,0:T(8,128)(2,1)} collective-permute-done((bf16[512,1024]{1,0:T(8,128)(2,1)}, bf16[512,1024]{1,0:T(8,128)(2,1)}, u32[]{:S(2)}, u32[]{:S(2)}) %collective-permute-start.2) | collective-permute-done | bytes 1048608 | tf_op jit(solution)/shard_map/ppermute | solution.py:242
  124.8 2.2 %fusion.40 = (bf16[256,1024]{1,0:T(8,128)(2,1)}, bf16[256,1024]{1,0:T(8,128)(2,1)}) fusion(bf16[512,1024]{1,0:T(8,128)(2,1)} %collective-permute-done.2), kind=kLoop, calls=%fused_computation.71 | loop fusion | bytes 2097152 | tf_op jit(solution)/shard_map/slice | solution.py:335
  127.0 5.3 %all-to-all-done.1 = bf16[8,192,128]{2,1,0:T(8,128)(2,1)S(1)} async-done(((bf16[8,192,128]{2,1,0:T(8,128)(2,1)}), bf16[8,192,128]{2,1,0:T(8,128)(2,1)S(1)}, u32[]{:S(2)}, u32[]{:S(2)}) %all-to-all-start.1) | async-done | bytes 393248 | tf_op jit(solution)/shard_map/all_to_all | solution.py:296
  134.0 2.1 %fusion.41 = (bf16[256,1024]{1,0:T(8,128)(2,1)}, bf16[256,1024]{1,0:T(8,128)(2,1)S(1)}) fusion(bf16[512,1024]{1,0:T(8,128)(2,1)} %collective-permute-done.4), kind=kLoop, calls=%fused_computation.72 | loop fusion | bytes 2097152 | tf_op jit(solution)/shard_map/slice | solution.py:336
  136.1 2.1 %fusion.42 = (bf16[256,1024]{1,0:T(8,128)(2,1)}, bf16[256,1024]{1,0:T(8,128)(2,1)S(1)}) fusion(bf16[512,1024]{1,0:T(8,128)(2,1)} %collective-permute-done.5), kind=kLoop, calls=%fused_computation.73 | loop fusion | bytes 2097152 | tf_op jit(solution)/shard_map/slice | solution.py:336
  138.2 5.5 %collective-permute-done.3 = bf16[384,512]{0,1:T(8,128)(2,1)S(1)} collective-permute-done((bf16[384,512]{0,1:T(8,128)(2,1)S(1)}, bf16[384,512]{0,1:T(8,128)(2,1)S(1)}, u32[]{:S(2)}, u32[]{:S(2)}) %collective-permute-start.3) | collective-permute-done | bytes 393248 | tf_op jit(solution)/shard_map/ppermute | solution.py:242
  145.0 0.8 multiply_reduce_fusion
  145.7 2.0 %fusion.2.query_ref = bf16[384,256]{1,0:T(8,128)(2,1)S(1)} fusion(bf16[1024,256]{1,0:T(8,128)(2,1)} %param.17, f32[384,1024]{1,0:T(8,128)S(1)} %get-tuple-element.18, f32[1024]{0:T(1024)S(1)} %copy-done.11, f32[384]{0:T(512)S(1)} %add_rsqrt_fusion), kind=kOutput, calls=%fused_computation.10 | convolution fusion | flops 202702848 | bytes 2299392 | tf_op jit(solution)/shard_map/dot_general | solution.py:325
  147.8 1.5 fusion.3.query_ref
  149.3 9.7 %shard_map.102 = bf16[384,256]{1,0:T(8,128)(2,1)S(1)} custom-call(bf16[384,256]{1,0:T(8,128)(2,1)S(1)} %fusion.2.query_ref, bf16[4096,512]{1,0:T(8,128)(2,1)S(1)} %copy-done.2), custom_call_target="tpu_custom_call" | custom-call | flops 6442450944 | bytes 4587520 | tf_op jit(solution)/shard_map/pallas_call | solution.py:226
  159.0 11.6 %shard_map.103 = bf16[384,256]{1,0:T(8,128)(2,1)S(1)} custom-call(bf16[384,256]{1,0:T(8,128)(2,1)S(1)} %fusion.3.query_ref, bf16[4096,512]{1,0:T(8,128)(2,1)} %collective-permute-done.7.keyval_ref), custom_call_target="tpu_custom_call" | custom-call | flops 6442450944 | bytes 4587520 | tf_op jit(solution)/shard_map/pallas_call | solution.py:226
  172.0 5.4 %collective-permute-done.8 = bf16[192,512]{1,0:T(8,128)(2,1)} collective-permute-done((bf16[192,512]{1,0:T(8,128)(2,1)}, bf16[192,512]{1,0:T(8,128)(2,1)}, u32[]{:S(2)}, u32[]{:S(2)}) %collective-permute-start.8) | collective-permute-done | bytes 196640 | tf_op jit(solution)/shard_map/ppermute | solution.py:242
  177.4 1.7 fusion.18
  179.1 1.1 fusion.1
  (63 shorter events, 7.0 us)
Async XLA Ops:
  6.5 4.2 %copy-start = (bf16[768,1024]{1,0:T(8,128)(2,1)S(1)}, bf16[768,1024]{1,0:T(8,128)(2,1)}, u32[]{:S(2)}) copy-start(bf16[768,1024]{1,0:T(8,128)(2,1)} %param.10) | copy-start | bytes 4718596
  6.5 2.0 %copy-start.13 = (bf16[512,1024]{1,0:T(8,128)(2,1)S(1)}, bf16[512,1024]{1,0:T(8,128)(2,1)}, u32[]{:S(2)}) copy-start(bf16[512,1024]{1,0:T(8,128)(2,1)} %param.12) | copy-start | bytes 3145732
  6.5 109.3 %all-gather.2.cloned.1.call-start = ((), (), s32[]{:S(2)}) async-start(), calls=%async_computation.2 | async-start | bytes 4718592 | tf_op jit(solution)/shard_map/all_gather | solution.py:271
  6.5 2.1 %copy-start.14 = (bf16[2,1024,256]{2,1,0:T(8,128)(2,1)S(1)}, bf16[2,1024,256]{2,1,0:T(8,128)(2,1)}, u32[]{:S(2)}) copy-start(bf16[2,1024,256]{2,1,0:T(8,128)(2,1)} %param.18) | copy-start | bytes 3145732
  8.7 1.8 copy-start.12
  9.1 4.8 %copy-start.1 = (f32[1024]{0:T(1024)S(1)}, f32[1024]{0:T(1024)}, u32[]{:S(2)}) copy-start(f32[1024]{0:T(1024)} %param.13) | copy-start | bytes 12292
  10.0 3.9 %collective-permute-start = (bf16[3,1024,256]{2,1,0:T(8,128)(2,1)}, bf16[3,1024,256]{2,1,0:T(8,128)(2,1)}, u32[]{:S(2)}, u32[]{:S(2)}) collective-permute-start(bf16[3,1024,256]{2,1,0:T(8,128)(2,1)} %own_ref.1), channel_id=1, source_target_pairs={{0,1},{1,0},{2,3},{3,2},{4,5},{5,4},{6,7},{7,6},{8,9},{9,8},{10,11... | collective-permute-start | bytes 4718600 | tf_op jit(solution)/shard_map/ppermute | solution.py:242
  19.3 48.9 %copy-start.8 = (bf16[256,1024]{1,0:T(8,128)(2,1)S(1)}, bf16[256,1024]{1,0:T(8,128)(2,1)}, u32[]{:S(2)}) copy-start(bf16[256,1024]{1,0:T(8,128)(2,1)} %param.15) | copy-start | bytes 1572868
  68.1 1.0 copy-start.5
  68.2 3.2 %collective-permute-start.1 = (bf16[8,400,128]{2,1,0:T(8,128)(2,1)S(1)}, bf16[8,400,128]{2,1,0:T(8,128)(2,1)S(1)}, u32[]{:S(2)}, u32[]{:S(2)}) collective-permute-start(bf16[8,400,128]{2,1,0:T(8,128)(2,1)S(1)} %slice.39), channel_id=1, source_target_pairs={{0,1},{1,0},{2,3},{3,2},{4,5},{5,4},{6,7},{7,6},{8,9},{9,8},{10,11... | collective-permute-start | bytes 2457608 | tf_op jit(solution)/shard_map/ppermute | solution.py:242
  70.0 45.8 %collective-permute-start.4 = (bf16[512,1024]{1,0:T(8,128)(2,1)}, bf16[512,1024]{1,0:T(8,128)(2,1)}, u32[]{:S(2)}, u32[]{:S(2)}) collective-permute-start(bf16[512,1024]{1,0:T(8,128)(2,1)} %constant_dynamic-update-slice_fusion), channel_id=1, source_target_pairs={{0,2},{2,0},{1,3},{3,1},{4,6},{6,4},{5,7},{7,5},{8,10},{10,8},{9,1... | collective-permute-start | bytes 3145736 | tf_op jit(solution)/shard_map/ppermute | solution.py:242
  115.8 43.2 %collective-permute-start.7 = (bf16[4096,512]{1,0:T(8,128)(2,1)}, bf16[4096,512]{1,0:T(8,128)(2,1)}, u32[]{:S(2)}, u32[]{:S(2)}) collective-permute-start(bf16[4096,512]{1,0:T(8,128)(2,1)} %all-gather.2.cloned.1.call-done.keyval_ref), channel_id=1, source_target_pairs={{0,1},{1,0},{2,3},{3,2},{4,5},{5,4},{6,7},{7,6},{8,9},{9,8},{10,11... | collective-permute-start | bytes 12582920 | tf_op jit(solution)/shard_map/ppermute | solution.py:242
  116.0 8.8 %collective-permute-start.2 = (bf16[512,1024]{1,0:T(8,128)(2,1)}, bf16[512,1024]{1,0:T(8,128)(2,1)}, u32[]{:S(2)}, u32[]{:S(2)}) collective-permute-start(bf16[512,1024]{1,0:T(8,128)(2,1)} %constant_dynamic-update-slice_fusion), channel_id=1, source_target_pairs={{0,1},{1,0},{2,3},{3,2},{4,5},{5,4},{6,7},{7,6},{8,9},{9,8},{10,11... | collective-permute-start | bytes 3145736 | tf_op jit(solution)/shard_map/ppermute | solution.py:242
  116.3 19.8 %collective-permute-start.5 = (bf16[512,1024]{1,0:T(8,128)(2,1)}, bf16[512,1024]{1,0:T(8,128)(2,1)}, u32[]{:S(2)}, u32[]{:S(2)}) collective-permute-start(bf16[512,1024]{1,0:T(8,128)(2,1)} %collective-permute-done.4), channel_id=1, source_target_pairs={{0,1},{1,0},{2,3},{3,2},{4,5},{5,4},{6,7},{7,6},{8,9},{9,8},{10,11... | collective-permute-start | bytes 3145736 | tf_op jit(solution)/shard_map/ppermute | solution.py:242
  116.5 15.9 %all-to-all-start.1 = ((bf16[8,192,128]{2,1,0:T(8,128)(2,1)}), bf16[8,192,128]{2,1,0:T(8,128)(2,1)S(1)}, u32[]{:S(2)}, u32[]{:S(2)}) async-start(bf16[8,192,128]{2,1,0:T(8,128)(2,1)} %shard_map.101), calls=%async_computation.1 | async-start | bytes 786432 | tf_op jit(solution)/shard_map/all_to_all | solution.py:296
  120.1 27.7 %collective-permute-start.6 = (bf16[1024,256]{1,0:T(8,128)(2,1)}, bf16[1024,256]{1,0:T(8,128)(2,1)}, u32[]{:S(2)}, u32[]{:S(2)}) collective-permute-start(bf16[1024,256]{1,0:T(8,128)(2,1)} %param.17), channel_id=1, source_target_pairs={{0,1},{1,0},{2,3},{3,2},{4,5},{5,4},{6,7},{7,6},{8,9},{9,8},{10,11... | collective-permute-start | bytes 1572872 | tf_op jit(solution)/shard_map/ppermute | solution.py:242
  133.4 10.4 %collective-permute-start.3 = (bf16[384,512]{0,1:T(8,128)(2,1)S(1)}, bf16[384,512]{0,1:T(8,128)(2,1)S(1)}, u32[]{:S(2)}, u32[]{:S(2)}) collective-permute-start(bf16[384,512]{0,1:T(8,128)(2,1)S(1)} %reshape.45), channel_id=1, source_target_pairs={{0,2},{2,0},{1,3},{3,1},{4,6},{6,4},{5,7},{7,5},{8,10},{10,8},{9,1... | collective-permute-start | bytes 1179656 | tf_op jit(solution)/shard_map/ppermute | solution.py:242
  143.8 1.2 copy-start.10
  145.7 3.5 %copy-start.3 = (f32[384,1024]{1,0:T(8,128)}, f32[384,1024]{1,0:T(8,128)S(1)}, u32[]{:S(2)}) copy-start(f32[384,1024]{1,0:T(8,128)S(1)} %get-tuple-element.18) | copy-start | bytes 4718596
  145.7 3.5 %copy-start.2 = (bf16[4096,512]{1,0:T(8,128)(2,1)S(1)}, bf16[4096,512]{1,0:T(8,128)(2,1)}, u32[]{:S(2)}) copy-start(bf16[4096,512]{1,0:T(8,128)(2,1)} %all-gather.2.cloned.1.call-done.keyval_ref) | copy-start | bytes 12582916
  170.6 8.4 %copy-start.4 = (f32[384,1024]{1,0:T(8,128)S(1)}, f32[384,1024]{1,0:T(8,128)}, u32[]{:S(2)}) copy-start(f32[384,1024]{1,0:T(8,128)} %copy-done.3) | copy-start | bytes 4718596
  171.4 6.0 %collective-permute-start.8 = (bf16[192,512]{1,0:T(8,128)(2,1)}, bf16[192,512]{1,0:T(8,128)(2,1)}, u32[]{:S(2)}, u32[]{:S(2)}) collective-permute-start(bf16[192,512]{1,0:T(8,128)(2,1)} %dynamic-slice_bitcast_fusion), channel_id=1, source_target_pairs={{0,2},{2,0},{1,3},{3,1},{4,6},{6,4},{5,7},{7,5},{8,10},{10,8},{9,1... | collective-permute-start | bytes 589832 | tf_op jit(solution)/shard_map/ppermute | solution.py:242
  172.0 7.1 %copy-start.6 = (bf16[256,1024]{1,0:T(8,128)(2,1)S(1)}, bf16[256,1024]{1,0:T(8,128)(2,1)}, u32[]{:S(2)}) copy-start(bf16[256,1024]{1,0:T(8,128)(2,1)} %param.19) | copy-start | bytes 1572868
  172.0 7.1 %copy-start.7 = (bf16[256,1024]{1,0:T(8,128)(2,1)S(1)}, bf16[256,1024]{1,0:T(8,128)(2,1)}, u32[]{:S(2)}) copy-start(bf16[256,1024]{1,0:T(8,128)(2,1)} %get-tuple-element.11) | copy-start | bytes 1572868
  (2 other events, 1.8 us)
Sparse Core Ops, SparseCore 0:
  10.1 94.1 all-gather.1

commit v3 on v2

--- a/solution.py
+++ b/solution.py
@@ -15,6 +15,9 @@
 VMEM_LIMIT = 48 * 1024 * 1024
 CORE_SWAP = ((0, 1), (1, 0), (2, 3), (3, 2))
 CHIP_SWAP = ((0, 2), (2, 0), (1, 3), (3, 1))
+SIDE_SWAP = tuple((i, i ^ 1) for i in range(8))
+NEXT_SWAP = tuple((i, i ^ 2) for i in range(8))
+SKIP_SWAP = tuple((i, i ^ 4) for i in range(8))
 
 
 def low_lanes(shape):
@@ -25,14 +28,61 @@
     return pltpu.roll(values, HD, 1)
 
 
-def project_kernel(core_ref, vox_ref, gain_ref, ids_ref, own_ref, other_ref, out_ref, normed_ref):
+def columns_of(row):
+    return jnp.transpose(jnp.broadcast_to(row, (LANES, LANES)))
+
+
+def one_hot(condition):
+    return jnp.where(condition, 1.0, 0.0).astype(jnp.bfloat16)
+
+
+def project_kernel(
+    core_ref, vox_ref, gain_ref, place_ref, own_ref, other_ref, out_ref, rank_ref, normed_ref, ids_ref
+):
     step = pl.program_id(0)
-    rows = vox_ref.shape[0]
+    rows = normed_ref.shape[0]
     packed = rows // 2
+    groups = place_ref.shape[0]
 
     @pl.when(step == 0)
     def _():
-        values = vox_ref[...].astype(jnp.float32)
+        places = place_ref[...].astype(jnp.float32)
+        place_rows = [places[g : g + 1] for g in range(groups)]
+        place_columns = [columns_of(row) for row in place_rows]
+        blank = jnp.zeros((8 - groups, LANES), jnp.float32)
+        lane = lax.broadcasted_iota(jnp.int32, (LANES, LANES), 1).astype(jnp.float32)
+        rank_rows = [
+            sum(
+                jnp.sum(jnp.where(column < row, 1.0, 0.0), axis=0, keepdims=True)
+                for column in place_columns
+            )
+            for row in place_rows
+        ]
+        rank_columns = [
+            jnp.sum(sum(jnp.where(row < column, 1.0, 0.0) for row in place_rows), axis=1, keepdims=True)
+            for column in place_columns
+        ]
+        window_rows = [
+            jnp.floor(
+                sum(
+                    jnp.sum(
+                        jnp.where(rank == lane + float(g * LANES), column, 0.0), axis=0, keepdims=True
+                    )
+                    for rank, column in zip(rank_columns, place_columns)
+                )
+                * (1.0 / WBLK)
+            )
+            for g in range(groups)
+        ]
+        windows = jnp.concatenate(window_rows + [blank], axis=0)
+        high = jnp.floor(windows * (1.0 / 256.0))
+        ids_ref[...] = jnp.concatenate([high, windows - 256.0 * high], axis=0).astype(jnp.bfloat16)
+        rank_ref[...] = jnp.concatenate(rank_rows + [blank], axis=0)
+        wanted = (lax.broadcasted_iota(jnp.int32, (rows, LANES), 0) + core_ref[0] * rows).astype(
+            jnp.float32
+        )
+        order = jnp.concatenate([one_hot(row == wanted) for row in rank_rows], axis=1)
+        values = jnp.dot(order, vox_ref[...], preferred_element_type=jnp.float32)
         spread = jnp.mean(values * values, axis=-1, keepdims=True)
         normed_ref[...] = (values * lax.rsqrt(spread + 1e-06) * gain_ref[...]).astype(jnp.bfloat16)
 
@@ -70,8 +120,9 @@
         emit(other_ref)
 
 
-def project(core, vox, gain, ids, own_weight, other_weight):
-    rows, width = vox.shape
+def project(core, vox, gain, places, own_weight, other_weight):
+    row_count, width = vox.shape
+    rows = row_count // 2
     local_width = own_weight.shape[2]
     heads = 2 * local_width // HD
     pair_steps = heads // 2
@@ -83,16 +134,22 @@
         absolute = jnp.where(side == 0, core_ref[0], 1 - core_ref[0])
         return (absolute * half_steps + step % half_steps, 0, 0)
 
+    def whole(step, core_ref):
+        return (0, 0)
+
     return pl.pallas_call(
         project_kernel,
-        out_shape=jax.ShapeDtypeStruct((heads, blob, LANES), jnp.bfloat16),
+        out_shape=(
+            jax.ShapeDtypeStruct((heads, blob, LANES), jnp.bfloat16),
+            jax.ShapeDtypeStruct((8, LANES), jnp.float32),
+        ),
         grid_spec=pltpu.PrefetchScalarGridSpec(
             num_scalar_prefetch=1,
             grid=(pair_steps,),
             in_specs=[
-                pl.BlockSpec((rows, width), lambda step, core_ref: (0, 0)),
-                pl.BlockSpec((1, width), lambda step, core_ref: (0, 0)),
-                pl.BlockSpec((ID_ROWS, LANES), lambda step, core_ref: (0, 0)),
+                pl.BlockSpec((row_count, width), whole),
+                pl.BlockSpec((1, width), whole),
+                pl.BlockSpec(places.shape, whole),
                 pl.BlockSpec(
                     (3, width, LANES),
                     lambda step, core_ref: (0, 0, jnp.minimum(step, half_steps - 1)),
@@ -102,88 +159,283 @@
                     lambda step, core_ref: (0, 0, jnp.maximum(step - half_steps, 0)),
                 ),
             ],
-            out_specs=pl.BlockSpec((2, blob, LANES), out_map),
-            scratch_shapes=[pltpu.VMEM((rows, width), jnp.bfloat16)],
+            out_specs=(pl.BlockSpec((2, blob, LANES), out_map), pl.BlockSpec((8, LANES), whole)),
+            scratch_shapes=[
+                pltpu.VMEM((rows, width), jnp.bfloat16),
+                pltpu.VMEM((ID_ROWS, LANES), jnp.bfloat16),
+            ],
         ),
         compiler_params=pltpu.CompilerParams(vmem_limit_bytes=VMEM_LIMIT),
-    )(core, vox, gain, ids, own_weight, other_weight)
-
-
-def read_ids(ref, index, rows):
-    tile = ref[index, rows : rows + ID_ROWS].astype(jnp.float32)
-    return tile[:8] * 256.0 + tile[8:]
-
-
-def window_kernel(mine_ref, theirs_ref, out_ref):
+    )(core, vox, gain, places, own_weight, other_weight)
+
+
+def window_kernel(
+    core_ref,
+    first_ref,
+    round_ref,
+    mine_ref,
+    theirs_ref,
+    out_ref,
+    key_ref,
+    window_ref,
+    sum_ref,
+    total_ref,
+    column_ref,
+    query_ref,
+):
     source = pl.program_id(0)
     sources = mine_ref.shape[0]
     packed = out_ref.shape[1]
     rows = 2 * packed
-    groups = rows // LANES
+    blocks = rows // LANES
+    last = 2 * rows // WBLK
     low_packed = low_lanes((packed, LANES))
+    core = core_ref[0]
+
+    @pl.when(source == 0)
+    def _():
+        low = low_lanes((8, LANES))
+        real = lax.broadcasted_iota(jnp.int32, (8, LANES), 0) < 2 * blocks
+        for index in range(sources):
+            key_ref[index, pl.ds(pl.multiple_of(core * rows, LANES), rows)] = mine_ref[index, :rows]
+            key_ref[index, pl.ds(pl.multiple_of((1 - core) * rows, LANES), rows)] = theirs_ref[index, :rows]
+            key_ref[index, 2 * rows :] = jnp.zeros((2 * LANES, LANES), jnp.bfloat16)
+            tile = mine_ref[index, rows : rows + ID_ROWS].astype(jnp.float32)
+            even = jnp.where(real, tile[:8] * 256.0 + tile[8:], -1.0)
+            window_ref[index, 0] = even
+            window_ref[index, 1] = jnp.where(
+                low, swap_halves(even), swap_halves(pltpu.roll(even, 7, 0))
+            )
+
     wire = mine_ref[source, rows + ID_ROWS :].astype(jnp.float32)
     query = jnp.concatenate(
         [jnp.where(low_packed, wire, 0.0), jnp.where(low_packed, swap_halves(wire), 0.0)], axis=0
     ).astype(jnp.bfloat16)
-    columns = jnp.transpose(read_ids(mine_ref, source, rows))
-    query_ids = jnp.concatenate([columns[:, g : g + 1] for g in range(groups)], axis=0)
-
-    def fold(ref, index, state):
-        sums, total = state
-        keyval = ref[index, :rows]
-        key_ids = read_ids(ref, index, rows)
+
+    def fold(block, other, turn, query_part, query_ids, sums, total):
+        first = first_ref[(source * blocks + block) * sources + other]
+        start = jnp.minimum(first + 4 * turn, last)
+        keyval = key_ref[other, pl.ds(pl.multiple_of(start * WBLK, WBLK), 2 * LANES)]
         scores = lax.dot_general(
-            query, keyval, (((1,), (1,)), ((), ())), preferred_element_type=jnp.float32
+            query_part, keyval, (((1,), (1,)), ((), ())), preferred_element_type=jnp.float32
         )
         weights = [
             jnp.where(
-                query_ids == key_ids[g : g + 1],
+                query_ids == window_ref[other, start % 2, pl.ds(start // 2 + g, 1)],
                 jnp.exp(scores[:, g * LANES : (g + 1) * LANES]),
                 0.0,
             )
-            for g in range(groups)
+            for g in range(2)
         ]
-        sums = functools.reduce(jnp.add, weights, sums)
         rounded = jnp.concatenate([part.astype(jnp.bfloat16) for part in weights], axis=1)
-        return sums, total + jnp.dot(rounded, keyval, preferred_element_type=jnp.float32)
-
-    def body(index, state):
-        return fold(theirs_ref, index, fold(mine_ref, index, state))
-
-    nothing = jnp.zeros((rows, LANES), jnp.float32)
-    sums, total = lax.fori_loop(0, sources, body, (nothing, nothing))
-    mixed = total / jnp.sum(sums, axis=-1, keepdims=True)
+        return (
+            sums + weights[0] + weights[1],
+            total + jnp.dot(rounded, keyval, preferred_element_type=jnp.float32),
+        )
+
+    for block in range(blocks):
+        query_part = query[block * LANES : (block + 1) * LANES]
+        query_ids = columns_of(window_ref[source, 0, pl.ds(core * blocks + block, 1)])
+        query_ref[block] = query_part
+        column_ref[block] = query_ids
+        sums = jnp.zeros((LANES, LANES), jnp.float32)
+        total = jnp.zeros((LANES, LANES), jnp.float32)
+        for other in range(sources):
+            sums, total = fold(block, other, 0, query_part, query_ids, sums, total)
+        sum_ref[block] = sums
+        total_ref[block] = total
+
+    def visit(index, carry):
+        block, other = index // sources, index % sources
+
+        def more(turn, carry):
+            sum_ref[block], total_ref[block] = fold(
+                block,
+                other,
+                turn,
+                query_ref[block],
+                column_ref[block],
+                sum_ref[block],
+                total_ref[block],
+            )
+            return carry
+
+        return lax.fori_loop(1, round_ref[source * blocks * sources + index], more, carry)
+
+    lax.fori_loop(0, blocks * sources, visit, 0)
+    mixed = jnp.concatenate(
+        [
+            total_ref[block] / jnp.sum(sum_ref[block], axis=-1, keepdims=True)
+            for block in range(blocks)
+        ],
+        axis=0,
+    )
     out_ref[0] = jnp.where(low_packed, swap_halves(mixed[:packed]), mixed[packed:]).astype(
         jnp.bfloat16
     )
 
 
-def window_mixing(mine, theirs, packed):
-    sources, blob, _ = mine.shape
+def window_mixing(core, mine, theirs, packed):
+    sources = mine.shape[0]
+    rows = 2 * packed
+    blocks = rows // LANES
+    tiles = mine[:, rows : rows + ID_ROWS].astype(jnp.float32)
+    windows = tiles[:, : 2 * blocks] * 256.0 + tiles[:, 8 : 8 + 2 * blocks]
+    key_low, key_high = windows[:, :, ::WBLK], windows[:, :, WBLK - 1 :: WBLK]
+    own = lax.dynamic_slice_in_dim(windows, core[0] * blocks, blocks, 1)
+    query_low, query_high = (own[:, :, at, None, None, None] for at in (0, LANES - 1))
+    first = jnp.sum((key_high < query_low).astype(jnp.int32), axis=(-2, -1))
+    beyond = jnp.sum((key_low <= query_high).astype(jnp.int32), axis=(-2, -1))
+    rounds = (beyond - first + 3) // 4
     return pl.pallas_call(
         window_kernel,
         out_shape=jax.ShapeDtypeStruct((sources, packed, LANES), jnp.bfloat16),
-        grid=(sources,),
-        in_specs=[
-            pl.BlockSpec(mine.shape, lambda source: (0, 0, 0)),
-            pl.BlockSpec(theirs.shape, lambda source: (0, 0, 0)),
-        ],
-        out_specs=pl.BlockSpec((1, packed, LANES), lambda source: (source, 0, 0)),
+        grid_spec=pltpu.PrefetchScalarGridSpec(
+            num_scalar_prefetch=3,
+            grid=(sources,),
+            in_specs=[
+                pl.BlockSpec(mine.shape, lambda source, *refs: (0, 0, 0)),
+                pl.BlockSpec(theirs.shape, lambda source, *refs: (0, 0, 0)),
+            ],
+            out_specs=pl.BlockSpec((1, packed, LANES), lambda source, *refs: (source, 0, 0)),
+            scratch_shapes=[
+                pltpu.VMEM((sources, 2 * rows + 2 * LANES, LANES), jnp.bfloat16),
+                pltpu.VMEM((sources, 2, 8, LANES), jnp.float32),
+                pltpu.VMEM((blocks, LANES, LANES), jnp.float32),
+                pltpu.VMEM((blocks, LANES, LANES), jnp.float32),
+                pltpu.VMEM((blocks, LANES, LANES), jnp.float32),
+                pltpu.VMEM((blocks, LANES, LANES), jnp.bfloat16),
+            ],
+        ),
         compiler_params=pltpu.CompilerParams(vmem_limit_bytes=VMEM_LIMIT),
         cost_estimate=pl.CostEstimate(
-            flops=32 * LANES * (sources * packed) ** 2,
-            transcendentals=8 * (sources * packed) ** 2,
+            flops=12 * LANES * (sources * packed) ** 2,
+            transcendentals=2 * (sources * packed) ** 2,
             bytes_accessed=2 * (mine.size + theirs.size),
         ),
-    )(mine, theirs)
-
-
-def cross_kernel(query_ref, keyval_ref, out_ref, score_ref):
+    )(core, first.reshape(-1), rounds.reshape(-1), mine, theirs)
+
+
+def bridge_kernel(
+    core_ref,
+    chip_ref,
+    rank_ref,
+    vox_ref,
+    gain_ref,
+    near_ref,
+    near_other_ref,
+    far_ref,
+    far_other_ref,
+    weight_ref,
+    other_weight_ref,
+    chip_weight_ref,
+    chip_other_weight_ref,
+    query_weight_ref,
+    other_query_weight_ref,
+    hidden_ref,
+    query_ref,
+    other_query_ref,
+    mix_ref,
+    column_ref,
+    kept_ref,
+):
+    share = hidden_ref.shape[0]
+    rows = 2 * share
+    core, chip = core_ref[0], chip_ref[0]
+    low = low_lanes((share, LANES))
+    heads = near_ref.shape[0]
+    groups = 2 * rows // LANES
+    for side, (own, other) in enumerate(((near_ref, near_other_ref), (far_ref, far_other_ref))):
+        for half, ref in enumerate((own, other)):
+            offset = pl.multiple_of((core if half == 0 else 1 - core) * rows, LANES)
+            for pair in range(heads // 2):
+                holder = core if pair < heads // 4 else 1 - core
+                head = holder * (heads // 2) + (pair % (heads // 4)) * 2
+                first, second = ref[head].astype(jnp.float32), ref[head + 1].astype(jnp.float32)
+                at = (side * heads // 2 + pair) * LANES
+                mix_ref[pl.ds(offset, share), at : at + LANES] = jnp.where(
+                    low, first, swap_halves(second)
+                ).astype(jnp.bfloat16)
+                mix_ref[pl.ds(offset + share, share), at : at + LANES] = jnp.where(
+                    low, swap_halves(first), second
+                ).astype(jnp.bfloat16)
+    for group in range(groups):
+        column_ref[group * LANES : (group + 1) * LANES] = columns_of(rank_ref[group : group + 1])
+    begin = pl.multiple_of(core * share, 64)
+    ranks = jnp.concatenate(
+        [column_ref[pl.ds(begin, share)], column_ref[pl.ds(begin + rows, share)]], axis=0
+    )
+    lane = lax.broadcasted_iota(jnp.int32, (rows, LANES), 1).astype(jnp.float32)
+    order = jnp.concatenate(
+        [one_hot(ranks == lane + float(group * LANES)) for group in range(groups)], axis=1
+    )
+    mix = jnp.dot(order, mix_ref[...], preferred_element_type=jnp.float32).astype(jnp.bfloat16)
+    hidden = jnp.concatenate(
+        [vox_ref[pl.ds(begin, share)], vox_ref[pl.ds(begin + rows, share)]], axis=0
+    ).astype(jnp.float32)
+    depth = weight_ref.shape[0]
+    refs = (weight_ref, other_weight_ref, chip_weight_ref, chip_other_weight_ref)
+    summed = sum(
+        jnp.dot(mix[:, i * depth : (i + 1) * depth], ref[...], preferred_element_type=jnp.float32)
+        for i, ref in enumerate(refs)
+    )
+    hidden = hidden + summed
+    kept_ref[...] = hidden
+    hidden_ref[...] = kept_ref[pl.ds(pl.multiple_of(chip * share, 64), share)]
+    spread = jnp.mean(hidden * hidden, axis=-1, keepdims=True)
+    normed = (hidden * lax.rsqrt(spread + 1e-06) * gain_ref[...]).astype(jnp.bfloat16)
+    for ref, out in (
+        (query_weight_ref, query_ref),
+        (other_query_weight_ref, other_query_ref),
+    ):
+        queries = jnp.dot(normed, ref[...], preferred_element_type=jnp.float32)
+        out[...] = (queries.astype(jnp.bfloat16).astype(jnp.float32) * HD ** (-0.5)).astype(
+            jnp.bfloat16
+        )
+
+
+def bridge(core, chip, ranks, voxels, gain, mixes, weights, query_weights):
+    row_count, width = voxels.shape
+    rows = row_count // 2
+    share = rows // 2
+    local_width = query_weights[0].shape[1]
+    scalar = pl.BlockSpec(memory_space=pltpu.SMEM)
+
+    def whole(array):
+        return pl.BlockSpec(array.shape, lambda step: (0,) * array.ndim)
+
+    operands = (ranks, voxels, gain, *mixes, *weights, *query_weights)
+    specs = [whole(array) for array in operands]
+    specs[7:11] = [pl.BlockSpec((width // 4, width), lambda step: (0, 0))] * 4
+    outs = (
+        jax.ShapeDtypeStruct((share, width), jnp.float32),
+        jax.ShapeDtypeStruct((rows, local_width), jnp.bfloat16),
+        jax.ShapeDtypeStruct((rows, local_width), jnp.bfloat16),
+    )
+    return pl.pallas_call(
+        bridge_kernel,
+        out_shape=outs,
+        grid=(1,),
+        in_specs=[scalar, scalar] + specs,
+        out_specs=tuple(whole(out) for out in outs),
+        scratch_shapes=[
+            pltpu.VMEM((row_count, width), jnp.bfloat16),
+            pltpu.VMEM((row_count, LANES), jnp.float32),
+            pltpu.VMEM((rows, width), jnp.float32),
+        ],
+        compiler_params=pltpu.CompilerParams(vmem_limit_bytes=VMEM_LIMIT),
+        cost_estimate=pl.CostEstimate(
+            flops=8 * rows * width * width, transcendentals=rows, bytes_accessed=8 * width * width
+        ),
+    )(core, chip, *operands)
+
+
+def cross_kernel(query_ref, *refs):
+    piece_refs, out_ref, score_ref = refs[:-2], refs[-2], refs[-1]
     rows, local_width = query_ref.shape
-    tokens = keyval_ref.shape[0]
-    chunk = math.gcd(tokens, 512)
     low = low_lanes((rows, LANES))
     zero = jnp.zeros((), jnp.bfloat16)
+    chunk = piece_refs[0].shape[0]
 
     def lane_groups(values):
         return [values[:, g : g + LANES] for g in range(0, chunk, LANES)]
@@ -193,53 +445,81 @@
         for head in range(2):
             query = jnp.where(low == (head == 0), query_ref[:, pair : pair + LANES], zero)
             peak = jnp.full((rows, LANES), -jnp.inf, jnp.float32)
-            for start in range(0, tokens, chunk):
+            for index, ref in enumerate(piece_refs):
                 scores = lax.dot_general(
                     query,
-                    keyval_ref[start : start + chunk, pair : pair + LANES],
+                    ref[:, pair : pair + LANES],
                     (((1,), (1,)), ((), ())),
                     preferred_element_type=jnp.float32,
                 )
-                score_ref[head, :, start : start + chunk] = scores
+                score_ref[head, :, index * chunk : (index + 1) * chunk] = scores
                 peak = functools.reduce(jnp.maximum, lane_groups(scores), peak)
             row_max = jnp.max(peak, axis=-1, keepdims=True)
             sums = jnp.zeros((rows, LANES), jnp.float32)
             total = jnp.zeros((rows, LANES), jnp.float32)
-            for start in range(0, tokens, chunk):
-                weights = jnp.exp(score_ref[head, :, start : start + chunk] - row_max)
+            for index, ref in enumerate(piece_refs):
+                weights = jnp.exp(
+                    score_ref[head, :, index * chunk : (index + 1) * chunk] - row_max
+                )
                 sums = functools.reduce(jnp.add, lane_groups(weights), sums)
                 total = total + jnp.dot(
                     weights.astype(jnp.bfloat16),
-                    keyval_ref[
-                        start : start + chunk, local_width + pair : local_width + pair + LANES
-                    ],
+                    ref[:, local_width + pair : local_width + pair + LANES],
                     preferred_element_type=jnp.float32,
                 )
             mixes.append(total / jnp.sum(sums, axis=-1, keepdims=True))
         out_ref[:, pair : pair + LANES] = jnp.where(low, mixes[0], mixes[1]).astype(jnp.bfloat16)
 
 
-def cross_mixing(queries, keyval):
+def cross_mixing(queries, pieces):
     rows, local_width = queries.shape
-    tokens = keyval.shape[0]
+    tokens = sum(piece.shape[0] for piece in pieces)
     scored = rows * tokens * local_width // HD
     return pl.pallas_call(
         cross_kernel,
         out_shape=jax.ShapeDtypeStruct((rows, local_width), jnp.bfloat16),
-        in_specs=[pl.BlockSpec(memory_space=pltpu.VMEM)] * 2,
+        in_specs=[pl.BlockSpec(memory_space=pltpu.VMEM)] * (1 + len(pieces)),
         out_specs=pl.BlockSpec(memory_space=pltpu.VMEM),
         scratch_shapes=[pltpu.VMEM((2, rows, tokens), jnp.float32)],
         compiler_params=pltpu.CompilerParams(vmem_limit_bytes=VMEM_LIMIT),
         cost_estimate=pl.CostEstimate(
             flops=8 * LANES * scored,
             transcendentals=scored,
-            bytes_accessed=2 * (keyval.size + 2 * queries.size),
+            bytes_accessed=4 * (tokens * local_width + queries.size),
         ),
-    )(queries, keyval)
+    )(queries, *pieces)
+
+
+def finish_kernel(base_ref, mix_ref, weight_ref, out_ref):
+    out_ref[...] = (
+        base_ref[...] + jnp.dot(mix_ref[...], weight_ref[...], preferred_element_type=jnp.float32)
+    ).astype(jnp.bfloat16)
+
+
+def finish(base, mix, pair):
+    def whole(array):
+        return pl.BlockSpec(array.shape, lambda step: (0, 0))
+
+    return pl.pallas_call(
+        finish_kernel,
+        out_shape=jax.ShapeDtypeStruct(base.shape, jnp.bfloat16),
+        grid=(1,),
+        in_specs=[
+            whole(base),
+            whole(mix),
+            pl.BlockSpec((pair.shape[0] // 2, pair.shape[1]), lambda step: (1, 0)),
+        ],
+        out_specs=whole(base),
+        compiler_params=pltpu.CompilerParams(vmem_limit_bytes=VMEM_LIMIT),
+    )(base, mix, pair)
 
 
 def swap(array, pairs):
     return lax.ppermute(array, "mp", pairs)
+
+
+def across(array, pairs):
+    return lax.ppermute(array, "seq", pairs)
 
 
 def by_head(
@@ -254,90 +534,98 @@
     cond_kv_weight,
     cross_out_weight,
 ):
-    model_index = lax.axis_index("mp")
-    core = model_index % 2
-    chip = model_index // 2
+    model_index = lax.axis_index("mp").astype(jnp.int32)
+    core = (model_index % 2).reshape(1)
+    chip = (model_index // 2).reshape(1)
     row_count, width = voxels.shape
-    local_width = qkv_weight.shape[2]
-    share = row_count // 4
-    rows = 2 * share
-    head_count = 2 * local_width // HD
+    rows = row_count // 2
+    share = rows // 2
+    depth = self_out_weight.shape[0]
 
     other_qkv = swap(qkv_weight, CORE_SWAP)
     cond_pair = [
         jnp.dot(cond, cond_kv_weight[part], preferred_element_type=jnp.float32).astype(jnp.bfloat16)
         for part in range(2)
     ]
-    own_keyval = lax.all_gather(jnp.concatenate(cond_pair, axis=1), "seq", axis=0, tiled=True)
-
-    vox = lax.dynamic_index_in_dim(
-        voxels.reshape(2, 2, share, width), core, axis=1, keepdims=False
-    ).reshape(rows, width)
-    window_ids = (
-        lax.dynamic_index_in_dim(
-            destination.reshape(2, 2, share), core, axis=1, keepdims=False
-        ).reshape(rows // LANES, LANES)
-        // WBLK
-    )
-    blank = jnp.zeros((8 - rows // LANES, LANES), jnp.int32)
-    ids = jnp.concatenate([window_ids // 256, blank, window_ids % 256, blank], axis=0).astype(
-        jnp.bfloat16
-    )
-    sent = project(
-        core.reshape(1).astype(jnp.int32), vox, norm_gain.reshape(1, width), ids, qkv_weight, other_qkv
-    )
-
-    chip_out = swap(jnp.concatenate([self_out_weight, cross_out_weight], axis=0), CHIP_SWAP)
-    other_q = swap(cross_q_weight, CORE_SWAP)
-
+    own_piece = jnp.concatenate(cond_pair, axis=1)
+    voxels, own_piece = lax.optimization_barrier((voxels, own_piece))
+    sent, ranks = project(
+        core,
+        voxels,
+        norm_gain.reshape(1, width),
+        destination.reshape(row_count // LANES, LANES),
+        qkv_weight,
+        other_qkv,
+    )
+
+    out_pair = jnp.concatenate([self_out_weight, cross_out_weight], axis=0)
+    chip_pair = swap(out_pair, CHIP_SWAP)
+    other_pair = swap(out_pair, CORE_SWAP)
+    other_query_weight = swap(cross_q_weight, CORE_SWAP)
+    side_piece = across(own_piece, SIDE_SWAP)
+    next_piece = across(own_piece, NEXT_SWAP)
+
+    sent, side_piece, next_piece = lax.optimization_barrier((sent, side_piece, next_piece))
     mine = lax.all_to_all(sent, "seq", split_axis=0, concat_axis=0, tiled=True)
-    theirs = swap(mine[:, : rows + ID_ROWS], CORE_SWAP)
-    mixed = window_mixing(mine, theirs, share)
-    returned = lax.all_to_all(mixed, "seq", split_axis=0, concat_axis=0, tiled=True)
-    near_mix = (
-        returned.reshape(head_count, share, 2, HD).transpose(2, 1, 0, 3).reshape(rows, head_count * HD)
-    )
-    far_mix = swap(near_mix, CHIP_SWAP)
-    own_keyval, chip_out, _ = lax.optimization_barrier((own_keyval, chip_out, mixed))
-
-    own_out = jnp.concatenate([self_out_weight, cross_out_weight], axis=0)
-    own_other_out = swap(own_out, CORE_SWAP)
-    chip_other_out = swap(chip_out, CORE_SWAP)
-    split = self_out_weight.shape[0]
-
-    def in_order(first, second):
-        return jnp.where(
-            core == 0,
-            jnp.concatenate([first[:split], second[:split]], axis=0),
-            jnp.concatenate([second[:split], first[:split]], axis=0),
+    theirs = swap(mine, CORE_SWAP)
+    late_piece, _ = lax.optimization_barrier((own_piece, mine))
+    skip_piece = across(late_piece, SKIP_SWAP)
+    next_side_piece = across(next_piece, SIDE_SWAP)
+    mixed = window_mixing(core, mine, theirs, share)
+    mixed, skip_piece, next_side_piece, chip_pair = lax.optimization_barrier(
+        (mixed, skip_piece, next_side_piece, chip_pair)
+    )
+    chip_other_pair = swap(chip_pair, CORE_SWAP)
+    last_piece = across(skip_piece, NEXT_SWAP)
+    skip_side_piece = across(skip_piece, SIDE_SWAP)
+    near = lax.all_to_all(mixed, "seq", split_axis=0, concat_axis=0, tiled=True)
+    far = swap(near, CHIP_SWAP)
+    near_other = swap(near, CORE_SWAP)
+    far, last_piece, skip_side_piece = lax.optimization_barrier((far, last_piece, skip_side_piece))
+    last_side_piece = across(last_piece, SIDE_SWAP)
+    far_other = swap(far, CORE_SWAP)
+    pieces = [
+        own_piece,
+        side_piece,
+        next_piece,
+        next_side_piece,
+        skip_piece,
+        skip_side_piece,
+        last_piece,
+        last_side_piece,
+    ]
+    pairs = (out_pair, other_pair, chip_pair, chip_other_pair)
+    own_hidden, own_query, other_query = bridge(
+        core,
+        chip,
+        ranks,
+        voxels,
+        cross_norm_gain.reshape(1, width),
+        (near, near_other, far, far_other),
+        pairs,
+        (cross_q_weight, other_query_weight),
+    )
+
+    asked = swap(other_query, CORE_SWAP)
+    answered = swap(cross_mixing(asked, pieces), CORE_SWAP)
+
+    def exchanged(mix):
+        halves = mix.reshape(2, share, mix.shape[1])
+        kept, leaving = (
+            lax.dynamic_index_in_dim(halves, at, 0, keepdims=False) for at in (chip[0], 1 - chip[0])
         )
-
-    summed = jnp.dot(
-        near_mix, in_order(own_out, own_other_out), preferred_element_type=jnp.float32
-    ) + jnp.dot(far_mix, in_order(chip_out, chip_other_out), preferred_element_type=jnp.float32)
-    hidden = vox.astype(jnp.float32) + summed
-    spread = jnp.mean(hidden * hidden, axis=-1, keepdims=True)
-    normed = (hidden * lax.rsqrt(spread + 1e-06) * cross_norm_gain).astype(jnp.bfloat16)
-    own_hidden = lax.dynamic_slice_in_dim(hidden, chip * share, share, 0)
-
-    def queries_of(weight):
-        return (
-            jnp.dot(normed, weight, preferred_element_type=jnp.float32).astype(jnp.bfloat16)
-            * HD ** (-0.5)
-        ).astype(jnp.bfloat16)
-
-    other_keyval = swap(own_keyval, CORE_SWAP)
-    own_cross = cross_mixing(queries_of(cross_q_weight), own_keyval)
-    other_cross = cross_mixing(queries_of(other_q), other_keyval)
-    both = jnp.concatenate([own_cross, other_cross], axis=1).reshape(2, share, 2 * local_width)
-    kept = lax.dynamic_index_in_dim(both, chip, axis=0, keepdims=False)
-    arrived = swap(lax.dynamic_index_in_dim(both, 1 - chip, axis=0, keepdims=False), CHIP_SWAP)
-    near_out = jnp.concatenate([own_out[split:], own_other_out[split:]], axis=0)
-    far_out = jnp.concatenate([chip_out[split:], chip_other_out[split:]], axis=0)
-    crossed = jnp.dot(kept, near_out, preferred_element_type=jnp.float32) + jnp.dot(
-        arrived, far_out, preferred_element_type=jnp.float32
-    )
-    return (own_hidden + crossed).astype(jnp.bfloat16)
+        return kept, swap(leaving, CHIP_SWAP)
+
+    other_kept, other_arrived = exchanged(answered)
+    own_kept, own_arrived = exchanged(cross_mixing(own_query, pieces))
+    crossed = own_hidden
+    for part, pair in (
+        (other_kept, other_pair),
+        (other_arrived, chip_other_pair),
+        (own_kept, out_pair),
+    ):
+        crossed = crossed + jnp.dot(part, pair[depth:], preferred_element_type=jnp.float32)
+    return finish(crossed, own_arrived, chip_pair)
 
 
 def rms_norm(matrix, gain):

time: 188 us -> 162 us (0.86); the launches traced: 187 us -> 163 us
  blocking collectives: 48.7 us -> 33.2 us
  between operations: 13.7 us -> 0.31 us
  starting transfers between devices: 8.02 us -> 20.7 us
  Pallas kernels: 71.2 us -> 61.1 us
  waiting for transfers between devices: 23.5 us -> 29.8 us
  matrix products: 10 us -> 3.76 us
  local copies, waits for them, and re-layouts: 11 us -> 14 us
    pallas_call x1, Pallas kernels: 44.4 us -> 24.2 us  [window_mixing(): pl.pallas_call(window_kernel, out_shape=jax.ShapeDtypeStruct((sources, pa...]
    all_to_all x1, blocking collectives: 48.7 us -> 33.2 us  [by_head(): mine = lax.all_to_all(sent, 'seq', split_axis=0, concat_axis=0, tiled=True)]
    ppermute x0 -> x7, waiting for transfers between devices: none -> 13 us  [across(): return lax.ppermute(array, 'seq', pairs)]
    ppermute x9 -> x13, waiting for transfers between devices: 18.2 us -> 7.39 us  [swap(): return lax.ppermute(array, 'mp', pairs)]
    ppermute x0 -> x7, starting transfers between devices: none -> 10.8 us  [across(): return lax.ppermute(array, 'seq', pairs)]
    unnamed x31 -> x51, local copies, waits for them, and re-layouts: 1.68 us -> 12.3 us
    pallas_call x1 -> x3, Pallas kernels: 5.45 us -> 13.7 us  [the longest x1 6.75 us: project(): pl.pallas_call(project_kernel, out_shape=(jax.ShapeDtypeStruct((heads, bl...]
    dot_general x6 -> x3, matrix products: 7.67 us -> 1.85 us  [by_head(): jnp.dot(part, pair[depth:], preferred_element_type=jnp.float32)]
  transfers between devices with their start and end apart: 11 -> 21, of which waited for: 5 -> 10; matrix products, arithmetic and copies ran while one was open for 8% -> 4% of each run, Pallas kernels for 32% -> 30%
where the time goes in v3:
time: 162 us; the launch traced here: 163 us
  Pallas kernels  61.1 us (38%)
  blocking collectives  33.2 us (20%)
  waiting for transfers between devices  29.8 us (18%)
  starting transfers between devices  20.7 us (13%)
  local copies, waits for them, and re-layouts  14 us (9%)
  matrix products  3.76 us (2%)
    all_to_all x1, blocking collectives, by_head(): mine = lax.all_to_all(sent, 'seq', split_axis=0, concat_axis=0, tiled=True)  33.2 us
    pallas_call x1, Pallas kernels, window_mixing(): pl.pallas_call(window_kernel, out_shape=jax.ShapeDtypeStruct((sources, pa...  24.2 us
    pallas_call x2, Pallas kernels, cross_mixing(): pl.pallas_call(cross_kernel, out_shape=jax.ShapeDtypeStruct((rows, local_...  23.2 us
    ppermute x7, waiting for transfers between devices, across(): return lax.ppermute(array, 'seq', pairs)  13 us
    unnamed x51, local copies, waits for them, and re-layouts  12.3 us
    ppermute x7, starting transfers between devices, across(): return lax.ppermute(array, 'seq', pairs)  10.8 us
    all_to_all x1, waiting for transfers between devices, by_head(): near = lax.all_to_all(mixed, 'seq', split_axis=0, concat_axis=0, tiled=True)  9.34 us
    ppermute x13, waiting for transfers between devices, swap(): return lax.ppermute(array, 'mp', pairs)  7.39 us
  transfers between devices with their start and end apart: 21, of which 10 were waited for; matrix products, arithmetic and copies ran while one was open for 4% of the time, Pallas kernels for 30%

profile of v3, /device:TPU:0, one launch (start us, length us, event | category | flops | bytes accessed | tf_op | source)
XLA Modules:
  0.0 163.1 jit_solution(8247302851803026086)
XLA Ops:
  1.2 1.5 convolution_convert_fusion
  3.3 3.0 %collective-permute-start.1 = (bf16[512,512]{1,0:T(8,128)(2,1)S(1)}, bf16[512,512]{1,0:T(8,128)(2,1)}, u32[]{:S(2)}, u32[]{:S(2)}) collective-permute-start(bf16[512,512]{1,0:T(8,128)(2,1)S(1)} %pad_maximum_fusion.refs_0_), channel_id=1, source_target_pairs={{0,4},{4,0},{8,12},{12,8},{16,20},{20,16},{24,28},{28,24},{1,5},{5... | collective-permute-start | bytes 1572872 | tf_op jit(solution)/shard_map/ppermute | solution.py:522
  6.3 1.6 collective-permute-start.2
  7.9 1.4 copy-done.2
  9.3 6.8 %shard_map.100 = (bf16[8,592,128]{2,1,0:T(8,128)(2,1)S(1)}, f32[8,128]{1,0:T(8,128)S(1)}) custom-call(s32[1]{0:T(128)} %bitcast.core_ref, bf16[768,1024]{1,0:T(8,128)(2,1)S(1)} %copy-done.2, f32[1,1024]{1,0:T(1,128)S(1)} %bitcast.33, s32[6,128]{1,0:T(8,128)S(1)} %bitcast.34, bf16[3,1024,256]{2,1,0:T(8,128)(2,1)S(1)} %copy-done.1, ...), custom_call_target="tpu_custom_call" | custom-call | tf_op jit(solution)/shard_map/pallas_call | solution.py:140
  16.0 2.2 %collective-permute-done.1.refs_1_ = bf16[512,512]{1,0:T(8,128)(2,1)} collective-permute-done((bf16[512,512]{1,0:T(8,128)(2,1)S(1)}, bf16[512,512]{1,0:T(8,128)(2,1)}, u32[]{:S(2)}, u32[]{:S(2)}) %collective-permute-start.1) | collective-permute-done | bytes 524320 | tf_op jit(solution)/shard_map/ppermute | solution.py:522
  18.3 1.5 collective-permute-done.2.refs_2_
  19.8 33.2 %all_to_all.10.mine_ref = bf16[8,592,128]{2,1,0:T(8,128)(2,1)S(1)} all-to-all(bf16[8,592,128]{2,1,0:T(8,128)(2,1)S(1)} %get-tuple-element.27), channel_id=1, replica_groups=mesh['seq'=8,'mp'=4] {'seq'}, dimensions={0} | all-to-all | bytes 2424832 | tf_op jit(solution)/shard_map/all_to_all | solution.py:569
  54.6 1.5 collective-permute-start.6
  58.7 24.2 %shard_map.101 = bf16[8,192,128]{2,1,0:T(8,128)(2,1)S(1)} custom-call(s32[1]{0:T(128)} %bitcast.core_ref, s32[192]{0:T(256)S(1)} %reshape.36.first_ref, s32[192]{0:T(256)S(1)} %and_select_fusion.round_ref, bf16[8,592,128]{2,1,0:T(8,128)(2,1)S(1)} %all_to_all.10.mine_ref, bf16[8,592,128]{2,1,0:T(8,128)(2,1)} %collective-permute-done.3.theirs_ref), custom_call_target="tpu_custom_call" | custom-call | flops 3623878656 | bytes 2424832 | tf_op jit(solution)/shard_map/pallas_call | solution.py:290
  84.3 4.2 %all-to-all-start.1 = ((bf16[8,192,128]{2,1,0:T(8,128)(2,1)}), bf16[8,192,128]{2,1,0:T(8,128)(2,1)S(1)}, u32[]{:S(2)}, u32[]{:S(2)}) async-start(bf16[8,192,128]{2,1,0:T(8,128)(2,1)} %copy-done.9), calls=%async_computation.1 | async-start | bytes 786432 | tf_op jit(solution)/shard_map/all_to_all | solution.py:581
  88.5 2.0 %collective-permute-start.10 = (bf16[512,512]{1,0:T(8,128)(2,1)}, bf16[512,512]{1,0:T(8,128)(2,1)}, u32[]{:S(2)}, u32[]{:S(2)}) collective-permute-start(bf16[512,512]{1,0:T(8,128)(2,1)} %collective-permute-done.4.refs_4_), channel_id=1, source_target_pairs={{0,4},{4,0},{8,12},{12,8},{16,20},{20,16},{24,28},{28,24},{1,5},{5... | collective-permute-start | bytes 1572872 | tf_op jit(solution)/shard_map/ppermute | solution.py:522
  91.0 1.5 collective-permute-start.9
  92.5 9.3 %all-to-all-done.1.near_ref = bf16[8,192,128]{2,1,0:T(8,128)(2,1)S(1)} async-done(((bf16[8,192,128]{2,1,0:T(8,128)(2,1)}), bf16[8,192,128]{2,1,0:T(8,128)(2,1)S(1)}, u32[]{:S(2)}, u32[]{:S(2)}) %all-to-all-start.1) | async-done | bytes 393248 | tf_op jit(solution)/shard_map/all_to_all | solution.py:581
  102.3 5.6 %collective-permute-done.10.refs_5_ = bf16[512,512]{1,0:T(8,128)(2,1)} collective-permute-done((bf16[512,512]{1,0:T(8,128)(2,1)}, bf16[512,512]{1,0:T(8,128)(2,1)}, u32[]{:S(2)}, u32[]{:S(2)}) %collective-permute-start.10) | collective-permute-done | bytes 524320 | tf_op jit(solution)/shard_map/ppermute | solution.py:522
  107.9 2.0 %collective-permute-done.9.refs_6_ = bf16[512,512]{1,0:T(8,128)(2,1)} collective-permute-done((bf16[512,512]{1,0:T(8,128)(2,1)}, bf16[512,512]{1,0:T(8,128)(2,1)}, u32[]{:S(2)}, u32[]{:S(2)}) %collective-permute-start.9) | collective-permute-done | bytes 524320 | tf_op jit(solution)/shard_map/ppermute | solution.py:522
  110.7 2.3 %collective-permute-done.8.far_ref = bf16[8,192,128]{2,1,0:T(8,128)(2,1)} collective-permute-done((bf16[8,192,128]{2,1,0:T(8,128)(2,1)S(1)}, bf16[8,192,128]{2,1,0:T(8,128)(2,1)}, u32[]{:S(2)}, u32[]{:S(2)}) %collective-permute-start.8) | collective-permute-done | bytes 393248 | tf_op jit(solution)/shard_map/ppermute | solution.py:518
  113.8 1.4 collective-permute-start.16
  120.6 5.9 %shard_map.102 = (f32[192,1024]{1,0:T(8,128)S(1)}, bf16[384,256]{1,0:T(8,128)(2,1)S(1)}, bf16[384,256]{1,0:T(8,128)(2,1)}) custom-call(s32[1]{0:T(128)} %bitcast.core_ref, s32[1]{0:T(128)} %bitcast.1.chip_ref, f32[8,128]{1,0:T(8,128)S(1)} %get-tuple-element.24.rank_ref, bf16[768,1024]{1,0:T(8,128)(2,1)} %vox_ref.1, f32[1,1024]{1,0:T(1,128)S(1)} %bitcast.35, ...), custom_call_target="tpu_custom_call" | custom-call | flops 3221225472 | bytes 8388608 | tf_op jit(solution)/shard_map/pallas_call | solution.py:415
  128.8 11.7 %shard_map.103 = bf16[384,256]{1,0:T(8,128)(2,1)S(1)} custom-call(bf16[384,256]{1,0:T(8,128)(2,1)S(1)} %collective-permute-done.15.query_ref, bf16[512,512]{1,0:T(8,128)(2,1)S(1)} %copy-done.6, bf16[512,512]{1,0:T(8,128)(2,1)} %collective-permute-done.1.refs_1_, bf16[512,512]{1,0:T(8,128)(2,1)} %collective-permute-done.2.refs_2_, ...), custom_call_target="tpu_custom_call" | custom-call | flops 6442450944 | bytes 4587520 | tf_op jit(solution)/shard_map/pallas_call | solution.py:478
  140.8 11.5 %shard_map.104 = bf16[384,256]{1,0:T(8,128)(2,1)S(1)} custom-call(bf16[384,256]{1,0:T(8,128)(2,1)S(1)} %copy-done.20, bf16[512,512]{1,0:T(8,128)(2,1)S(1)} %copy-done.6, bf16[512,512]{1,0:T(8,128)(2,1)} %collective-permute-done.1.refs_1_, bf16[512,512]{1,0:T(8,128)(2,1)} %collective-permute-done.2.refs_2_, bf16[512,512]{1,0:T(8,128)(2,1)} %collective-permute-done.5.refs_3_, ...), custom_call_target="tpu_custom_call" | custom-call | flops 6442450944 | bytes 4587520 | tf_op jit(solution)/shard_map/pallas_call | solution.py:478
  152.9 1.7 %collective-permute-start.18 = (bf16[192,256]{1,0:T(8,128)(2,1)S(1)}, bf16[192,256]{1,0:T(8,128)(2,1)S(1)}, u32[]{:S(2)}, u32[]{:S(2)}) collective-permute-start(bf16[192,256]{1,0:T(8,128)(2,1)S(1)} %dynamic-slice_bitcast_fusion.1), channel_id=1, source_target_pairs={{0,2},{2,0},{1,3},{3,1},{4,6},{6,4},{5,7},{7,5},{8,10},{10,8},{9,1... | collective-permute-start | bytes 294920 | tf_op jit(solution)/shard_map/ppermute | solution.py:518
  154.8 4.7 %collective-permute-done.18 = bf16[192,256]{1,0:T(8,128)(2,1)S(1)} collective-permute-done((bf16[192,256]{1,0:T(8,128)(2,1)S(1)}, bf16[192,256]{1,0:T(8,128)(2,1)S(1)}, u32[]{:S(2)}, u32[]{:S(2)}) %collective-permute-start.18) | collective-permute-done | bytes 98336 | tf_op jit(solution)/shard_map/ppermute | solution.py:518
  159.5 1.3 fusion
  (101 shorter events, 20.9 us)
Async XLA Ops:
  0.0 7.8 %collective-permute-start = (bf16[3,1024,256]{2,1,0:T(8,128)(2,1)}, bf16[3,1024,256]{2,1,0:T(8,128)(2,1)}, u32[]{:S(2)}, u32[]{:S(2)}) collective-permute-start(bf16[3,1024,256]{2,1,0:T(8,128)(2,1)} %own_ref.1), channel_id=1, source_target_pairs={{0,1},{1,0},{2,3},{3,2},{4,5},{5,4},{6,7},{7,6},{8,9},{9,8},{10,11... | collective-permute-start | bytes 4718600 | tf_op jit(solution)/shard_map/ppermute | solution.py:518
  3.3 15.0 %collective-permute-start.1 = (bf16[512,512]{1,0:T(8,128)(2,1)S(1)}, bf16[512,512]{1,0:T(8,128)(2,1)}, u32[]{:S(2)}, u32[]{:S(2)}) collective-permute-start(bf16[512,512]{1,0:T(8,128)(2,1)S(1)} %pad_maximum_fusion.refs_0_), channel_id=1, source_target_pairs={{0,4},{4,0},{8,12},{12,8},{16,20},{20,16},{24,28},{28,24},{1,5},{5... | collective-permute-start | bytes 1572872 | tf_op jit(solution)/shard_map/ppermute | solution.py:522
  6.3 13.5 %collective-permute-start.2 = (bf16[512,512]{1,0:T(8,128)(2,1)S(1)}, bf16[512,512]{1,0:T(8,128)(2,1)}, u32[]{:S(2)}, u32[]{:S(2)}) collective-permute-start(bf16[512,512]{1,0:T(8,128)(2,1)S(1)} %pad_maximum_fusion.refs_0_), channel_id=1, source_target_pairs={{0,8},{4,12},{8,0},{12,4},{16,24},{20,28},{24,16},{28,20},{1,9},{5... | collective-permute-start | bytes 1572872 | tf_op jit(solution)/shard_map/ppermute | solution.py:522
  19.7 33.2 %copy-start.23 = (bf16[256,1024]{1,0:T(8,128)(2,1)S(1)}, bf16[256,1024]{1,0:T(8,128)(2,1)}, u32[]{:S(2)}) copy-start(bf16[256,1024]{1,0:T(8,128)(2,1)} %param.15) | copy-start | bytes 1572868
  19.7 34.0 %copy-start.21 = (bf16[256,1024]{1,0:T(8,128)(2,1)S(1)}, bf16[256,1024]{1,0:T(8,128)(2,1)}, u32[]{:S(2)}) copy-start(bf16[256,1024]{1,0:T(8,128)(2,1)} %param.19) | copy-start | bytes 1572868
  52.9 5.7 %collective-permute-start.3 = (bf16[8,592,128]{2,1,0:T(8,128)(2,1)S(1)}, bf16[8,592,128]{2,1,0:T(8,128)(2,1)}, u32[]{:S(2)}, u32[]{:S(2)}) collective-permute-start(bf16[8,592,128]{2,1,0:T(8,128)(2,1)S(1)} %all_to_all.10.mine_ref), channel_id=1, source_target_pairs={{0,1},{1,0},{2,3},{3,2},{4,5},{5,4},{6,7},{7,6},{8,9},{9,8},{10,11... | collective-permute-start | bytes 3637256 | tf_op jit(solution)/shard_map/ppermute | solution.py:518
  54.6 29.0 %collective-permute-start.6 = (bf16[512,1024]{1,0:T(8,128)(2,1)}, bf16[512,1024]{1,0:T(8,128)(2,1)S(1)}, u32[]{:S(2)}, u32[]{:S(2)}) collective-permute-start(bf16[512,1024]{1,0:T(8,128)(2,1)} %constant_dynamic-update-slice_fusion.weight_ref), channel_id=1, source_target_pairs={{0,2},{2,0},{1,3},{3,1},{4,6},{6,4},{5,7},{7,5},{8,10},{10,8},{9,1... | collective-permute-start | bytes 3145736 | tf_op jit(solution)/shard_map/ppermute | solution.py:518
  56.1 27.5 %collective-permute-start.5 = (bf16[512,512]{1,0:T(8,128)(2,1)}, bf16[512,512]{1,0:T(8,128)(2,1)}, u32[]{:S(2)}, u32[]{:S(2)}) collective-permute-start(bf16[512,512]{1,0:T(8,128)(2,1)} %collective-permute-done.2.refs_2_), channel_id=1, source_target_pairs={{0,4},{4,0},{8,12},{12,8},{16,20},{20,16},{24,28},{28,24},{1,5},{5... | collective-permute-start | bytes 1572872 | tf_op jit(solution)/shard_map/ppermute | solution.py:522
  58.5 25.9 %collective-permute-start.4 = (bf16[512,512]{1,0:T(8,128)(2,1)}, bf16[512,512]{1,0:T(8,128)(2,1)}, u32[]{:S(2)}, u32[]{:S(2)}) collective-permute-start(bf16[512,512]{1,0:T(8,128)(2,1)} %copy-done.5), channel_id=1, source_target_pairs={{0,16},{4,20},{8,24},{12,28},{16,0},{20,4},{24,8},{28,12},{1,17},{... | collective-permute-start | bytes 1572872 | tf_op jit(solution)/shard_map/ppermute | solution.py:522
  58.6 57.6 %copy-start.18 = (f32[1024]{0:T(1024)S(1)}, f32[1024]{0:T(1024)}, u32[]{:S(2)}) copy-start(f32[1024]{0:T(1024)} %param.16) | copy-start | bytes 12292
  84.3 17.5 %all-to-all-start.1 = ((bf16[8,192,128]{2,1,0:T(8,128)(2,1)}), bf16[8,192,128]{2,1,0:T(8,128)(2,1)S(1)}, u32[]{:S(2)}, u32[]{:S(2)}) async-start(bf16[8,192,128]{2,1,0:T(8,128)(2,1)} %copy-done.9), calls=%async_computation.1 | async-start | bytes 786432 | tf_op jit(solution)/shard_map/all_to_all | solution.py:581
  88.5 19.3 %collective-permute-start.10 = (bf16[512,512]{1,0:T(8,128)(2,1)}, bf16[512,512]{1,0:T(8,128)(2,1)}, u32[]{:S(2)}, u32[]{:S(2)}) collective-permute-start(bf16[512,512]{1,0:T(8,128)(2,1)} %collective-permute-done.4.refs_4_), channel_id=1, source_target_pairs={{0,4},{4,0},{8,12},{12,8},{16,20},{20,16},{24,28},{28,24},{1,5},{5... | collective-permute-start | bytes 1572872 | tf_op jit(solution)/shard_map/ppermute | solution.py:522
  90.5 24.7 %collective-permute-start.12 = (bf16[512,1024]{1,0:T(8,128)(2,1)}, bf16[512,1024]{1,0:T(8,128)(2,1)S(1)}, u32[]{:S(2)}, u32[]{:S(2)}) collective-permute-start(bf16[512,1024]{1,0:T(8,128)(2,1)} %constant_dynamic-update-slice_fusion.weight_ref), channel_id=1, source_target_pairs={{0,1},{1,0},{2,3},{3,2},{4,5},{5,4},{6,7},{7,6},{8,9},{9,8},{10,11... | collective-permute-start | bytes 3145736 | tf_op jit(solution)/shard_map/ppermute | solution.py:518
  90.9 25.3 %collective-permute-start.13 = (bf16[512,1024]{1,0:T(8,128)(2,1)S(1)}, bf16[512,1024]{1,0:T(8,128)(2,1)}, u32[]{:S(2)}, u32[]{:S(2)}) collective-permute-start(bf16[512,1024]{1,0:T(8,128)(2,1)S(1)} %collective-permute-done.6.chip_weight_ref.weight_ref), channel_id=1, source_target_pairs={{0,1},{1,0},{2,3},{3,2},{4,5},{5,4},{6,7},{7,6},{8,9},{9,8},{10,11... | collective-permute-start | bytes 3145736 | tf_op jit(solution)/shard_map/ppermute | solution.py:518
  91.0 18.9 %collective-permute-start.9 = (bf16[512,512]{1,0:T(8,128)(2,1)}, bf16[512,512]{1,0:T(8,128)(2,1)}, u32[]{:S(2)}, u32[]{:S(2)}) collective-permute-start(bf16[512,512]{1,0:T(8,128)(2,1)} %collective-permute-done.4.refs_4_), channel_id=1, source_target_pairs={{0,8},{4,12},{8,0},{12,4},{16,24},{20,28},{24,16},{28,20},{1,9},{5... | collective-permute-start | bytes 1572872 | tf_op jit(solution)/shard_map/ppermute | solution.py:522
  101.8 11.2 %collective-permute-start.8 = (bf16[8,192,128]{2,1,0:T(8,128)(2,1)S(1)}, bf16[8,192,128]{2,1,0:T(8,128)(2,1)}, u32[]{:S(2)}, u32[]{:S(2)}) collective-permute-start(bf16[8,192,128]{2,1,0:T(8,128)(2,1)S(1)} %all-to-all-done.1.near_ref), channel_id=1, source_target_pairs={{0,2},{2,0},{1,3},{3,1},{4,6},{6,4},{5,7},{7,5},{8,10},{10,8},{9,1... | collective-permute-start | bytes 1179656 | tf_op jit(solution)/shard_map/ppermute | solution.py:518
  107.8 5.2 %collective-permute-start.14 = (bf16[1024,256]{1,0:T(8,128)(2,1)}, bf16[1024,256]{1,0:T(8,128)(2,1)S(1)}, u32[]{:S(2)}, u32[]{:S(2)}) collective-permute-start(bf16[1024,256]{1,0:T(8,128)(2,1)} %query_weight_ref.1), channel_id=1, source_target_pairs={{0,1},{1,0},{2,3},{3,2},{4,5},{5,4},{6,7},{7,6},{8,9},{9,8},{10,11... | collective-permute-start | bytes 1572872 | tf_op jit(solution)/shard_map/ppermute | solution.py:518
  109.9 6.3 %collective-permute-start.7 = (bf16[8,192,128]{2,1,0:T(8,128)(2,1)S(1)}, bf16[8,192,128]{2,1,0:T(8,128)(2,1)}, u32[]{:S(2)}, u32[]{:S(2)}) collective-permute-start(bf16[8,192,128]{2,1,0:T(8,128)(2,1)S(1)} %all-to-all-done.1.near_ref), channel_id=1, source_target_pairs={{0,1},{1,0},{2,3},{3,2},{4,5},{5,4},{6,7},{7,6},{8,9},{9,8},{10,11... | collective-permute-start | bytes 1179656 | tf_op jit(solution)/shard_map/ppermute | solution.py:518
  113.0 3.2 %collective-permute-start.11 = (bf16[8,192,128]{2,1,0:T(8,128)(2,1)}, bf16[8,192,128]{2,1,0:T(8,128)(2,1)}, u32[]{:S(2)}, u32[]{:S(2)}) collective-permute-start(bf16[8,192,128]{2,1,0:T(8,128)(2,1)} %collective-permute-done.8.far_ref), channel_id=1, source_target_pairs={{0,1},{1,0},{2,3},{3,2},{4,5},{5,4},{6,7},{7,6},{8,9},{9,8},{10,11... | collective-permute-start | bytes 1179656 | tf_op jit(solution)/shard_map/ppermute | solution.py:518
  113.8 14.7 %collective-permute-start.16 = (bf16[512,512]{1,0:T(8,128)(2,1)}, bf16[512,512]{1,0:T(8,128)(2,1)}, u32[]{:S(2)}, u32[]{:S(2)}) collective-permute-start(bf16[512,512]{1,0:T(8,128)(2,1)} %collective-permute-done.9.refs_6_), channel_id=1, source_target_pairs={{0,4},{4,0},{8,12},{12,8},{16,20},{20,16},{24,28},{28,24},{1,5},{5... | collective-permute-start | bytes 1572872 | tf_op jit(solution)/shard_map/ppermute | solution.py:522
  127.2 1.7 %collective-permute-start.15 = (bf16[384,256]{1,0:T(8,128)(2,1)}, bf16[384,256]{1,0:T(8,128)(2,1)S(1)}, u32[]{:S(2)}, u32[]{:S(2)}) collective-permute-start(bf16[384,256]{1,0:T(8,128)(2,1)} %get-tuple-element.35), channel_id=1, source_target_pairs={{0,1},{1,0},{2,3},{3,2},{4,5},{5,4},{6,7},{7,6},{8,9},{9,8},{10,11... | collective-permute-start | bytes 589832 | tf_op jit(solution)/shard_map/ppermute | solution.py:518
  140.5 12.4 %collective-permute-start.17 = (bf16[384,256]{1,0:T(8,128)(2,1)S(1)}, bf16[384,256]{1,0:T(8,128)(2,1)S(1)}, u32[]{:S(2)}, u32[]{:S(2)}) collective-permute-start(bf16[384,256]{1,0:T(8,128)(2,1)S(1)} %shard_map.103), channel_id=1, source_target_pairs={{0,1},{1,0},{2,3},{3,2},{4,5},{5,4},{6,7},{7,6},{8,9},{9,8},{10,11... | collective-permute-start | bytes 589832 | tf_op jit(solution)/shard_map/ppermute | solution.py:518
  152.4 8.8 %collective-permute-start.19 = (bf16[192,256]{1,0:T(8,128)(2,1)S(1)}, bf16[192,256]{1,0:T(8,128)(2,1)S(1)}, u32[]{:S(2)}, u32[]{:S(2)}) collective-permute-start(bf16[192,256]{1,0:T(8,128)(2,1)S(1)} %dynamic-slice_bitcast_fusion), channel_id=1, source_target_pairs={{0,2},{2,0},{1,3},{3,1},{4,6},{6,4},{5,7},{7,5},{8,10},{10,8},{9,1... | collective-permute-start | bytes 294920 | tf_op jit(solution)/shard_map/ppermute | solution.py:518
  152.9 6.6 %collective-permute-start.18 = (bf16[192,256]{1,0:T(8,128)(2,1)S(1)}, bf16[192,256]{1,0:T(8,128)(2,1)S(1)}, u32[]{:S(2)}, u32[]{:S(2)}) collective-permute-start(bf16[192,256]{1,0:T(8,128)(2,1)S(1)} %dynamic-slice_bitcast_fusion.1), channel_id=1, source_target_pairs={{0,2},{2,0},{1,3},{3,1},{4,6},{6,4},{5,7},{7,5},{8,10},{10,8},{9,1... | collective-permute-start | bytes 294920 | tf_op jit(solution)/shard_map/ppermute | solution.py:518
  (22 other events, 119.0 us)

commit v4 on v3

v4 whole, which is shorter than its diff:
```python
import functools
import math

import jax
import jax.numpy as jnp
from jax import lax
from jax.experimental import pallas as pl
from jax.experimental.pallas import tpu as pltpu
from jax.sharding import PartitionSpec as P

HD = 64
WBLK = 64
LANES = 128
ID_ROWS = 16
MEGA = 1024 * 1024
BATCH = 4
CORE_SWAP = ((0, 1), (1, 0), (2, 3), (3, 2))
CHIP_SWAP = ((0, 2), (2, 0), (1, 3), (3, 1))
SIDE_SWAP = tuple((i, i ^ 1) for i in range(8))
NEXT_SWAP = tuple((i, i ^ 2) for i in range(8))
SKIP_SWAP = tuple((i, i ^ 4) for i in range(8))


def low_lanes(shape):
    return lax.broadcasted_iota(jnp.int32, shape, 1) < HD


def swap_halves(values):
    return pltpu.roll(values, HD, 1)


def columns_of(row):
    return jnp.transpose(jnp.broadcast_to(row, (LANES, LANES)))


def one_hot(condition):
    return jnp.where(condition, 1.0, 0.0).astype(jnp.bfloat16)


def project_kernel(
    core_ref, vox_ref, gain_ref, place_ref, own_ref, other_ref, out_ref, rank_ref, normed_ref, ids_ref
):
    step = pl.program_id(0)
    rows = normed_ref.shape[0]
    packed = rows // 2
    groups = place_ref.shape[0]

    @pl.when(step == 0)
    def _():
        places = place_ref[...].astype(jnp.float32)
        place_rows = [places[g : g + 1] for g in range(groups)]
        place_columns = [columns_of(row) for row in place_rows]
        blank = jnp.zeros((8 - groups, LANES), jnp.float32)
        lane = lax.broadcasted_iota(jnp.int32, (LANES, LANES), 1).astype(jnp.float32)
        rank_rows = [
            sum(
                jnp.sum(jnp.where(column < row, 1.0, 0.0), axis=0, keepdims=True)
                for column in place_columns
            )
            for row in place_rows
        ]
        rank_columns = [
            jnp.sum(sum(jnp.where(row < column, 1.0, 0.0) for row in place_rows), axis=1, keepdims=True)
            for column in place_columns
        ]
        window_rows = [
            jnp.floor(
                sum(
                    jnp.sum(
                        jnp.where(rank == lane + float(g * LANES), column, 0.0), axis=0, keepdims=True
                    )
                    for rank, column in zip(rank_columns, place_columns)
                )
                * (1.0 / WBLK)
            )
            for g in range(groups)
        ]
        slot = lax.broadcasted_iota(jnp.int32, (1, LANES), 1)
        bounds = jnp.zeros((1, LANES), jnp.float32)
        for block in range(2 * groups):
            begin = (block % 2) * WBLK
            row = window_rows[block // 2]
            bounds = jnp.where(slot == block, row[:, begin : begin + 1], bounds)
            bounds = jnp.where(
                slot == block + 2 * groups, row[:, begin + WBLK - 1 : begin + WBLK], bounds
            )
        windows = jnp.concatenate(
            window_rows + [bounds] + [jnp.zeros_like(bounds)] * (7 - groups), axis=0
        )
        high = jnp.floor(windows * (1.0 / 256.0))
        ids_ref[...] = jnp.concatenate([high, windows - 256.0 * high], axis=0).astype(jnp.bfloat16)
        rank_ref[...] = jnp.concatenate(rank_rows + [blank], axis=0)
        wanted = (lax.broadcasted_iota(jnp.int32, (rows, LANES), 0) + core_ref[0] * rows).astype(
            jnp.float32
        )
        order = jnp.concatenate([one_hot(row == wanted) for row in rank_rows], axis=1)
        values = jnp.dot(order, vox_ref[...], preferred_element_type=jnp.float32)
        spread = jnp.mean(values * values, axis=-1, keepdims=True)
        normed_ref[...] = (values * lax.rsqrt(spread + 1e-06) * gain_ref[...]).astype(jnp.bfloat16)

    def emit(weight_ref):
        normed = normed_ref[...]
        low = low_lanes((rows, LANES))
        low_packed = low_lanes((packed, LANES))
        query, key, value = (
            jnp.dot(normed, weight_ref[part], preferred_element_type=jnp.float32)
            for part in range(3)
        )
        query = query * HD ** (-0.5)
        for at in range(0, weight_ref.shape[2], LANES):
            keys, values = key[:, at : at + LANES], value[:, at : at + LANES]
            first, second = query[:packed, at : at + LANES], query[packed:, at : at + LANES]
            pairs = (
                (
                    jnp.where(low, keys, swap_halves(values)),
                    jnp.where(low_packed, first, swap_halves(second)),
                ),
                (
                    jnp.where(low, swap_halves(keys), values),
                    jnp.where(low_packed, swap_halves(first), second),
                ),
            )
            for side, (keyval, queries) in enumerate(pairs):
                head = at // HD + side
                out_ref[head, :rows] = keyval.astype(jnp.bfloat16)
                out_ref[head, rows : rows + ID_ROWS] = ids_ref[...]
                out_ref[head, rows + ID_ROWS :] = queries.astype(jnp.bfloat16)

    @pl.when(step == 0)
    def _():
        emit(own_ref)

    @pl.when(step == 1)
    def _():
        emit(other_ref)


def project(core, vox, gain, places, own_weight, other_weight):
    row_count, width = vox.shape
    rows = row_count // 2
    local_width = own_weight.shape[2]
    heads = 2 * local_width // HD
    blob = rows + ID_ROWS + rows // 2

    def out_map(step, core_ref):
        return (jnp.where(step == 0, core_ref[0], 1 - core_ref[0]), 0, 0)

    def whole(step, core_ref):
        return (0, 0)

    return pl.pallas_call(
        project_kernel,
        out_shape=(
            jax.ShapeDtypeStruct((heads, blob, LANES), jnp.bfloat16),
            jax.ShapeDtypeStruct((8, LANES), jnp.float32),
        ),
        grid_spec=pltpu.PrefetchScalarGridSpec(
            num_scalar_prefetch=1,
            grid=(2,),
            in_specs=[
                pl.BlockSpec((row_count, width), whole),
                pl.BlockSpec((1, width), whole),
                pl.BlockSpec(places.shape, whole),
                pl.BlockSpec(own_weight.shape, lambda step, core_ref: (0, 0, 0)),
                pl.BlockSpec(own_weight.shape, lambda step, core_ref: (0, 0, 0)),
            ],
            out_specs=(pl.BlockSpec((heads // 2, blob, LANES), out_map), pl.BlockSpec((8, LANES), whole)),
            scratch_shapes=[
                pltpu.VMEM((rows, width), jnp.bfloat16),
                pltpu.VMEM((ID_ROWS, LANES), jnp.bfloat16),
            ],
        ),
        compiler_params=pltpu.CompilerParams(vmem_limit_bytes=28 * MEGA),
    )(core, vox, gain, places, own_weight, other_weight)


def window_kernel(
    core_ref,
    mine_ref,
    theirs_ref,
    out_ref,
    wire_ref,
    key_ref,
    window_ref,
    query_ref,
    column_ref,
    sum_ref,
    total_ref,
    plan_ref,
    plan_smem,
    late_smem,
    copy_sem,
):
    sources, packed, _ = out_ref.shape
    rows = 2 * packed
    blocks = rows // LANES
    last = 2 * rows // WBLK
    low_packed = low_lanes((packed, LANES))
    core = core_ref[0]

    low = low_lanes((8, LANES))
    real = lax.broadcasted_iota(jnp.int32, (8, LANES), 0) < 2 * blocks
    copies = [
        pltpu.make_async_copy(source, target, copy_sem.at[index])
        for index, (source, target) in enumerate(
            (
                (mine_ref.at[:, pl.ds(rows, ID_ROWS + packed)], wire_ref),
                (
                    mine_ref.at[:, pl.ds(0, rows)],
                    key_ref.at[:, pl.ds(pl.multiple_of(core * rows, LANES), rows)],
                ),
                (
                    theirs_ref.at[:, pl.ds(0, rows)],
                    key_ref.at[:, pl.ds(pl.multiple_of((1 - core) * rows, LANES), rows)],
                ),
            )
        )
    ]
    for copy in copies:
        copy.start()
    key_ref[:, 2 * rows :] = jnp.zeros((sources, 2 * LANES, LANES), jnp.bfloat16)
    copies[0].wait()
    bounds = []
    for index in range(sources):
        tile = wire_ref[index, :ID_ROWS].astype(jnp.float32)
        ids = tile[:8] * 256.0 + tile[8:]
        bounds.append(ids[2 * blocks : 2 * blocks + 1])
        even = jnp.where(real, ids, -1.0)
        window_ref[index, 0] = even
        window_ref[index, 1] = jnp.where(
            low, swap_halves(even), swap_halves(pltpu.roll(even, 7, 0))
        )

    bounds = jnp.concatenate(bounds, axis=0)
    slot = lax.broadcasted_iota(jnp.int32, (sources, LANES), 1)
    lows = jnp.where(slot < last, bounds, jnp.inf)
    highs = jnp.where(slot < last, pltpu.roll(bounds, LANES - last, 1), jnp.inf)
    begins = [
        jnp.where(core == 0, bounds[:, at : at + 1], bounds[:, at + last // 2 : at + last // 2 + 1])
        for at in range(0, last // 2, 2)
    ]
    ends = [
        jnp.where(core == 0, bounds[:, at : at + 1], bounds[:, at + last // 2 : at + last // 2 + 1])
        for at in range(last + 1, last + last // 2, 2)
    ]
    first = jnp.full((sources, LANES), float(last), jnp.float32)
    beyond = first
    for source in range(sources):
        for block in range(blocks):
            here = slot == source * blocks + block
            begin, end = (edges[block][source : source + 1] for edges in (begins, ends))
            first = jnp.where(
                here, jnp.sum(jnp.where(highs < begin, 1.0, 0.0), axis=1, keepdims=True), first
            )
            beyond = jnp.where(
                here, jnp.sum(jnp.where(lows <= end, 1.0, 0.0), axis=1, keepdims=True), beyond
            )
    plan_ref[0] = first.astype(jnp.int32)
    plan_ref[1] = jnp.floor((beyond - first + 3.0) * 0.25).astype(jnp.int32)
    plan_copy = pltpu.make_async_copy(plan_ref, plan_smem, copy_sem.at[3])
    plan_copy.start()
    plan_copy.wait()
    copies[1].wait()
    copies[2].wait()

    def fold(pair, other, turn, query_part, query_ids, sums, total):
        start = jnp.minimum(plan_smem[0, other, pair] + 4 * turn, last)
        keyval = key_ref[other, pl.ds(pl.multiple_of(start * WBLK, WBLK), 2 * LANES)]
        scores = lax.dot_general(
            query_part, keyval, (((1,), (1,)), ((), ())), preferred_element_type=jnp.float32
        )
        weights = [
            jnp.where(
                query_ids == window_ref[other, start % 2, pl.ds(start // 2 + g, 1)],
                jnp.exp(scores[:, g * LANES : (g + 1) * LANES]),
                0.0,
            )
            for g in range(2)
        ]
        rounded = jnp.concatenate([part.astype(jnp.bfloat16) for part in weights], axis=1)
        return (
            sums + weights[0] + weights[1],
            total + jnp.dot(rounded, keyval, preferred_element_type=jnp.float32),
        )

    def sweep(source, carry):
        wire = wire_ref[source, ID_ROWS:].astype(jnp.float32)
        query = jnp.concatenate(
            [jnp.where(low_packed, wire, 0.0), jnp.where(low_packed, swap_halves(wire), 0.0)],
            axis=0,
        ).astype(jnp.bfloat16)
        for block in range(blocks):
            at = source * blocks + block
            query_part = query[block * LANES : (block + 1) * LANES]
            query_ids = columns_of(window_ref[source, 0, pl.ds(core * blocks + block, 1)])
            query_ref[at] = query_part
            column_ref[at] = query_ids
            sums = jnp.zeros((LANES, LANES), jnp.float32)
            total = jnp.zeros((LANES, LANES), jnp.float32)
            for other in range(sources):
                sums, total = fold(at, other, 0, query_part, query_ids, sums, total)
            sum_ref[at] = sums
            total_ref[at] = total
        return carry

    lax.fori_loop(0, sources, sweep, 0)
    spare = sources * blocks
    query_ref[spare] = jnp.zeros((LANES, LANES), jnp.bfloat16)
    column_ref[spare] = jnp.zeros((LANES, LANES), jnp.float32)
    sum_ref[spare] = jnp.zeros((LANES, LANES), jnp.float32)
    total_ref[spare] = jnp.zeros((LANES, LANES), jnp.float32)

    count = jnp.int32(0)
    for other in range(sources):
        for at in range(sources * blocks):
            late_smem[count] = other * LANES + at
            count = count + jnp.where(plan_smem[1, other, at] > 1, 1, 0)
    for i in range(BATCH):
        late_smem[count + i] = spare

    def visit(index, carry):
        pairs = [late_smem[index * BATCH + i] for i in range(BATCH)]
        pairs = [(pair // LANES, pair % LANES) for pair in pairs]
        turns = functools.reduce(jnp.maximum, [plan_smem[1, other, at] for other, at in pairs])

        def more(turn, carry):
            for other, at in pairs:
                sum_ref[at], total_ref[at] = fold(
                    at, other, turn, query_ref[at], column_ref[at], sum_ref[at], total_ref[at]
                )
            return carry

        return lax.fori_loop(1, turns, more, carry)

    lax.fori_loop(0, (count + BATCH - 1) // BATCH, visit, 0)

    for source in range(sources):
        mixed = jnp.concatenate(
            [
                total_ref[at] / jnp.sum(sum_ref[at], axis=-1, keepdims=True)
                for at in range(source * blocks, (source + 1) * blocks)
            ],
            axis=0,
        )
        out_ref[source] = jnp.where(low_packed, swap_halves(mixed[:packed]), mixed[packed:]).astype(
            jnp.bfloat16
        )


def window_mixing(core, mine, theirs, packed):
    sources = mine.shape[0]
    rows = 2 * packed
    blocks = rows // LANES
    vmem = pl.BlockSpec(memory_space=pltpu.VMEM)
    smem = pl.BlockSpec(memory_space=pltpu.SMEM)
    return pl.pallas_call(
        window_kernel,
        out_shape=jax.ShapeDtypeStruct((sources, packed, LANES), jnp.bfloat16),
        in_specs=[smem] + [pl.BlockSpec(memory_space=pltpu.HBM)] * 2,
        out_specs=vmem,
        scratch_shapes=[
            pltpu.VMEM((sources, ID_ROWS + packed, LANES), jnp.bfloat16),
            pltpu.VMEM((sources, 2 * rows + 2 * LANES, LANES), jnp.bfloat16),
            pltpu.VMEM((sources, 2, 8, LANES), jnp.float32),
            pltpu.VMEM((sources * blocks + 1, LANES, LANES), jnp.bfloat16),
            pltpu.VMEM((sources * blocks + 1, LANES, LANES), jnp.float32),
            pltpu.VMEM((sources * blocks + 1, LANES, LANES), jnp.float32),
            pltpu.VMEM((sources * blocks + 1, LANES, LANES), jnp.float32),
            pltpu.VMEM((2, sources, LANES), jnp.int32),
            pltpu.SMEM((2, sources, LANES), jnp.int32),
            pltpu.SMEM((sources * sources * blocks + 2 * BATCH,), jnp.int32),
            pltpu.SemaphoreType.DMA((4,)),
        ],
        compiler_params=pltpu.CompilerParams(vmem_limit_bytes=24 * MEGA),
        cost_estimate=pl.CostEstimate(
            flops=80 * LANES * (sources * packed) ** 2,
            transcendentals=2 * (sources * packed) ** 2,
            bytes_accessed=2 * (mine.size + theirs.size),
        ),
    )(core, mine, theirs)


def fetch(refs, local_ref, copy_sem):
    copies = [
        pltpu.make_async_copy(ref, local_ref.at[index], copy_sem.at[index])
        for index, ref in enumerate(refs)
    ]
    for copy in copies:
        copy.start()
    return copies


def mix_heads(core, own_ref, other_ref, order, weight_ref, copies, mix_ref):
    heads, share, _ = own_ref.shape
    rows = 2 * share
    low = low_lanes((share, LANES))
    for half, ref in enumerate((own_ref, other_ref)):
        offset = pl.multiple_of((core if half == 0 else 1 - core) * rows, LANES)
        for pair in range(heads // 2):
            holder = core if pair < heads // 4 else 1 - core
            head = holder * (heads // 2) + (pair % (heads // 4)) * 2
            first, second = ref[head].astype(jnp.float32), ref[head + 1].astype(jnp.float32)
            at = pair * LANES
            mix_ref[pl.ds(offset, share), at : at + LANES] = jnp.where(
                low, first, swap_halves(second)
            ).astype(jnp.bfloat16)
            mix_ref[pl.ds(offset + share, share), at : at + LANES] = jnp.where(
                low, swap_halves(first), second
            ).astype(jnp.bfloat16)
    mix = jnp.dot(order, mix_ref[...], preferred_element_type=jnp.float32).astype(jnp.bfloat16)
    depth = weight_ref.shape[1]
    for copy in copies:
        copy.wait()
    return sum(
        jnp.dot(
            mix[:, i * depth : (i + 1) * depth], weight_ref[i], preferred_element_type=jnp.float32
        )
        for i in range(len(copies))
    )


def near_kernel(
    core_ref,
    rank_ref,
    vox_ref,
    own_ref,
    other_ref,
    weight_ref,
    other_weight_ref,
    hidden_ref,
    order_ref,
    token_ref,
    mix_ref,
    column_ref,
    local_ref,
    copy_sem,
):
    core = core_ref[0]
    copies = fetch((weight_ref, other_weight_ref), local_ref, copy_sem)
    token_ref[...] = jnp.zeros_like(token_ref)
    rows = hidden_ref.shape[0]
    share = rows // 2
    groups = 2 * rows // LANES
    for group in range(groups):
        column_ref[group * LANES : (group + 1) * LANES] = columns_of(rank_ref[group : group + 1])
    begin = pl.multiple_of(core * share, 64)
    ranks = jnp.concatenate(
        [column_ref[pl.ds(begin, share)], column_ref[pl.ds(begin + rows, share)]], axis=0
    )
    lane = lax.broadcasted_iota(jnp.int32, (rows, LANES), 1).astype(jnp.float32)
    order = jnp.concatenate(
        [one_hot(ranks == lane + float(group * LANES)) for group in range(groups)], axis=1
    )
    order_ref[...] = order
    values = jnp.concatenate(
        [vox_ref[pl.ds(begin, share)], vox_ref[pl.ds(begin + rows, share)]], axis=0
    ).astype(jnp.float32)
    hidden_ref[...] = values + mix_heads(
        core, own_ref, other_ref, order, local_ref, copies, mix_ref
    )


def far_kernel(
    core_ref,
    chip_ref,
    base_ref,
    order_ref,
    gain_ref,
    own_ref,
    other_ref,
    weight_ref,
    other_weight_ref,
    query_weight_ref,
    other_query_weight_ref,
    hidden_ref,
    query_ref,
    other_query_ref,
    mix_ref,
    kept_ref,
    local_ref,
    copy_sem,
    query_local_ref,
    query_sem,
):
    share = hidden_ref.shape[0]
    copies = fetch((weight_ref, other_weight_ref), local_ref, copy_sem)
    query_copies = fetch((query_weight_ref, other_query_weight_ref), query_local_ref, query_sem)
    hidden = base_ref[...] + mix_heads(
        core_ref[0], own_ref, other_ref, order_ref[...], local_ref, copies, mix_ref
    )
    kept_ref[...] = hidden
    hidden_ref[...] = kept_ref[pl.ds(pl.multiple_of(chip_ref[0] * share, 64), share)]
    spread = jnp.mean(hidden * hidden, axis=-1, keepdims=True)
    normed = (hidden * lax.rsqrt(spread + 1e-06) * gain_ref[...]).astype(jnp.bfloat16)
    for index, out in enumerate((query_ref, other_query_ref)):
        query_copies[index].wait()
        queries = jnp.dot(normed, query_local_ref[index], preferred_element_type=jnp.float32)
        out[...] = (queries.astype(jnp.bfloat16).astype(jnp.float32) * HD ** (-0.5)).astype(
            jnp.bfloat16
        )


def whole(array):
    return pl.BlockSpec(array.shape, lambda step: (0,) * array.ndim)


def near_part(core, ranks, voxels, mixes, weights):
    row_count, width = voxels.shape
    rows = row_count // 2
    heads = mixes[0].shape[0]
    outs = (
        jax.ShapeDtypeStruct((rows, width), jnp.float32),
        jax.ShapeDtypeStruct((rows, row_count), jnp.bfloat16),
        jax.ShapeDtypeStruct((8, LANES), jnp.float32),
    )
    return pl.pallas_call(
        near_kernel,
        out_shape=outs,
        grid=(1,),
        in_specs=[pl.BlockSpec(memory_space=pltpu.SMEM)]
        + [whole(array) for array in (ranks, voxels, *mixes)]
        + [pl.BlockSpec(memory_space=pltpu.HBM)] * len(weights),
        out_specs=tuple(whole(out) for out in outs),
        scratch_shapes=[
            pltpu.VMEM((row_count, heads * HD), jnp.bfloat16),
            pltpu.VMEM((row_count, LANES), jnp.float32),
            pltpu.VMEM((len(weights), *weights[0].shape), jnp.bfloat16),
            pltpu.SemaphoreType.DMA((len(weights),)),
        ],
        compiler_params=pltpu.CompilerParams(vmem_limit_bytes=24 * MEGA),
        cost_estimate=pl.CostEstimate(
            flops=10 * rows * width * width, transcendentals=0, bytes_accessed=8 * width * width
        ),
    )(core, ranks, voxels, *mixes, *weights)


def far_part(core, chip, base, order, gain, mixes, weights, query_weights):
    rows, width = base.shape
    share = rows // 2
    local_width = query_weights[0].shape[1]
    heads = mixes[0].shape[0]
    outs = (
        jax.ShapeDtypeStruct((share, width), jnp.float32),
        jax.ShapeDtypeStruct((rows, local_width), jnp.bfloat16),
        jax.ShapeDtypeStruct((rows, local_width), jnp.bfloat16),
    )
    return pl.pallas_call(
        far_kernel,
        out_shape=outs,
        grid=(1,),
        in_specs=[pl.BlockSpec(memory_space=pltpu.SMEM)] * 2
        + [whole(array) for array in (base, order, gain, *mixes)]
        + [pl.BlockSpec(memory_space=pltpu.HBM)] * (len(weights) + len(query_weights)),
        out_specs=tuple(whole(out) for out in outs),
        scratch_shapes=[
            pltpu.VMEM((2 * rows, heads * HD), jnp.bfloat16),
            pltpu.VMEM((rows, width), jnp.float32),
            pltpu.VMEM((len(weights), *weights[0].shape), jnp.bfloat16),
            pltpu.SemaphoreType.DMA((len(weights),)),
            pltpu.VMEM((len(query_weights), *query_weights[0].shape), jnp.bfloat16),
            pltpu.SemaphoreType.DMA((len(query_weights),)),
        ],
        compiler_params=pltpu.CompilerParams(vmem_limit_bytes=24 * MEGA),
        cost_estimate=pl.CostEstimate(
            flops=10 * rows * width * width, transcendentals=rows, bytes_accessed=8 * width * width
        ),
    )(core, chip, base, order, gain, *mixes, *weights, *query_weights)


def cross_kernel(piece_count, merging, query_ref, *refs):
    piece_refs, refs = refs[:piece_count], refs[piece_count:]
    if merging:
        *old_refs, out_ref, score_ref, local_ref, copy_sem = refs
    else:
        *out_refs, score_ref, local_ref, copy_sem = refs
    rows, local_width = query_ref.shape
    low = low_lanes((rows, LANES))
    zero = jnp.zeros((), jnp.bfloat16)
    chunk = piece_refs[0].shape[0]
    copies = [
        pltpu.make_async_copy(ref, local_ref.at[index], copy_sem.at[index])
        for index, ref in enumerate(piece_refs)
    ]
    for copy in copies:
        copy.start()

    def lane_groups(values):
        return [values[:, g : g + LANES] for g in range(0, chunk, LANES)]

    for pair in range(0, local_width, LANES):
        if merging:
            old_peak, old_sums, old_total = (ref[:, pair : pair + LANES] for ref in old_refs)
        results = []
        for head in range(2):
            query = jnp.where(low == (head == 0), query_ref[:, pair : pair + LANES], zero)
            peak = jnp.full((rows, LANES), -jnp.inf, jnp.float32)
            for index in range(piece_count):
                if pair + head == 0:
                    copies[index].wait()
                scores = lax.dot_general(
                    query,
                    local_ref[index, :, pair : pair + LANES],
                    (((1,), (1,)), ((), ())),
                    preferred_element_type=jnp.float32,
                )
                score_ref[head, :, index * chunk : (index + 1) * chunk] = scores
                peak = functools.reduce(jnp.maximum, lane_groups(scores), peak)
            row_max = jnp.max(peak, axis=-1, keepdims=True)
            if merging:
                row_max = jnp.maximum(row_max, old_peak[:, head * HD : head * HD + 1])
            sums = jnp.zeros((rows, LANES), jnp.float32)
            total = jnp.zeros((rows, LANES), jnp.float32)
            for index in range(piece_count):
                weights = jnp.exp(
                    score_ref[head, :, index * chunk : (index + 1) * chunk] - row_max
                )
                sums = functools.reduce(jnp.add, lane_groups(weights), sums)
                total = total + jnp.dot(
                    weights.astype(jnp.bfloat16),
                    local_ref[index, :, local_width + pair : local_width + pair + LANES],
                    preferred_element_type=jnp.float32,
                )
            results.append((row_max, jnp.sum(sums, axis=-1, keepdims=True), total))
        new_peak, new_sums, new_total = (
            jnp.where(low, first, second) for first, second in zip(*results)
        )
        if merging:
            scale = jnp.exp(old_peak - new_peak)
            out_ref[:, pair : pair + LANES] = (
                (new_total + old_total * scale) / (new_sums + old_sums * scale)
            ).astype(jnp.bfloat16)
        else:
            for ref, values in zip(out_refs, (new_peak, new_sums, new_total)):
                ref[:, pair : pair + LANES] = values


def cross_mixing(queries, pieces, state=()):
    rows, local_width = queries.shape
    tokens = sum(piece.shape[0] for piece in pieces)
    scored = rows * tokens * local_width // HD
    block = pl.BlockSpec(memory_space=pltpu.VMEM)
    if state:
        outs = jax.ShapeDtypeStruct((rows, local_width), jnp.bfloat16)
    else:
        outs = (jax.ShapeDtypeStruct((rows, local_width), jnp.float32),) * 3
    return pl.pallas_call(
        functools.partial(cross_kernel, len(pieces), bool(state)),
        out_shape=outs,
        in_specs=[block]
        + [pl.BlockSpec(memory_space=pltpu.HBM)] * len(pieces)
        + [block] * len(state),
        out_specs=block if state else (block,) * 3,
        scratch_shapes=[
            pltpu.VMEM((2, rows, tokens), jnp.float32),
            pltpu.VMEM((len(pieces), *pieces[0].shape), jnp.bfloat16),
            pltpu.SemaphoreType.DMA((len(pieces),)),
        ],
        compiler_params=pltpu.CompilerParams(vmem_limit_bytes=20 * MEGA),
        cost_estimate=pl.CostEstimate(
            flops=16 * LANES * scored,
            transcendentals=scored,
            bytes_accessed=4 * (tokens * local_width + queries.size),
        ),
    )(queries, *pieces, *state)


def finish_kernel(base_ref, mix_ref, weight_ref, out_ref):
    out_ref[...] = (
        base_ref[...] + jnp.dot(mix_ref[...], weight_ref[...], preferred_element_type=jnp.float32)
    ).astype(jnp.bfloat16)


def finish(base, mix, weight):
    return pl.pallas_call(
        finish_kernel,
        out_shape=jax.ShapeDtypeStruct(base.shape, jnp.bfloat16),
        grid=(1,),
        in_specs=[whole(base), whole(mix), whole(weight)],
        out_specs=whole(base),
        compiler_params=pltpu.CompilerParams(vmem_limit_bytes=8 * MEGA),
    )(base, mix, weight)


def swap(array, pairs):
    return lax.ppermute(array, "mp", pairs)


def across(array, pairs):
    return lax.ppermute(array, "seq", pairs)


def by_head(
    voxels,
    destination,
    cond,
    norm_gain,
    qkv_weight,
    self_out_weight,
    cross_norm_gain,
    cross_q_weight,
    cond_kv_weight,
    cross_out_weight,
):
    model_index = lax.axis_index("mp").astype(jnp.int32)
    core = (model_index % 2).reshape(1)
    chip = (model_index // 2).reshape(1)
    row_count, width = voxels.shape
    rows = row_count // 2
    share = rows // 2

    other_qkv = swap(qkv_weight, CORE_SWAP)
    cond_pair = [
        jnp.dot(cond, cond_kv_weight[part], preferred_element_type=jnp.float32).astype(jnp.bfloat16)
        for part in range(2)
    ]
    own_piece = jnp.concatenate(cond_pair, axis=1)
    voxels, own_piece = lax.optimization_barrier((voxels, own_piece))
    sent, ranks = project(
        core,
        voxels,
        norm_gain.reshape(1, width),
        destination.reshape(row_count // LANES, LANES),
        qkv_weight,
        other_qkv,
    )

    mine = lax.all_to_all(sent, "seq", split_axis=0, concat_axis=0, tiled=True)
    theirs = swap(mine, CORE_SWAP)
    side_piece = across(own_piece, SIDE_SWAP)
    next_piece = across(own_piece, NEXT_SWAP)
    chip_self = swap(self_out_weight, CHIP_SWAP)
    late_piece, _ = lax.optimization_barrier((own_piece, mine))
    skip_piece = across(late_piece, SKIP_SWAP)
    mixed = window_mixing(core, mine, theirs, share)
    mixed, side_piece, next_piece, skip_piece, chip_self = lax.optimization_barrier(
        (mixed, side_piece, next_piece, skip_piece, chip_self)
    )

    near = lax.all_to_all(mixed, "seq", split_axis=0, concat_axis=0, tiled=True)
    last_piece = across(skip_piece, NEXT_SWAP)
    next_side_piece = across(next_piece, SIDE_SWAP)
    skip_side_piece = across(skip_piece, SIDE_SWAP)
    chip_cross = swap(cross_out_weight, CHIP_SWAP)
    far = swap(near, CHIP_SWAP)
    near_other = swap(near, CORE_SWAP)
    base, order, token = near_part(
        core,
        ranks,
        voxels,
        (near, near_other),
        (self_out_weight, swap(self_out_weight, CORE_SWAP)),
    )
    far, last_piece, next_side_piece, chip_cross, _ = lax.optimization_barrier(
        (far, last_piece, next_side_piece, chip_cross, token)
    )
    last_side_piece = across(last_piece, SIDE_SWAP)
    far_other = swap(far, CORE_SWAP)
    own_hidden, own_query, other_query = far_part(
        core,
        chip,
        base,
        order,
        cross_norm_gain.reshape(1, width),
        (far, far_other),
        (chip_self, swap(chip_self, CORE_SWAP)),
        (cross_q_weight, swap(cross_q_weight, CORE_SWAP)),
    )

    asked = swap(other_query, CORE_SWAP)
    early = (own_piece, side_piece, next_piece, skip_piece)
    own_state = cross_mixing(own_query, early)
    asked, skip_side_piece, *own_state = lax.optimization_barrier(
        (asked, skip_side_piece, *own_state)
    )
    asked_state = cross_mixing(asked, early)
    last_side_piece, *asked_state = lax.optimization_barrier((last_side_piece, *asked_state))
    late = (next_side_piece, skip_side_piece, last_piece, last_side_piece)
    answered = swap(cross_mixing(asked, late, tuple(asked_state)), CORE_SWAP)

    def halved(mix):
        halves = mix.reshape(2, share, mix.shape[1])
        return (
            lax.dynamic_index_in_dim(halves, at, 0, keepdims=False) for at in (chip[0], 1 - chip[0])
        )

    other_kept, other_leaving = halved(answered)
    other_arrived = swap(other_leaving, CHIP_SWAP)
    own_mix = cross_mixing(own_query, late, tuple(own_state))
    own_mix, other_arrived, other_kept = lax.optimization_barrier(
        (own_mix, other_arrived, other_kept)
    )
    own_kept, own_leaving = halved(own_mix)
    own_arrived = swap(own_leaving, CHIP_SWAP)
    crossed = own_hidden
    for part, weight in (
        (other_kept, swap(cross_out_weight, CORE_SWAP)),
        (other_arrived, swap(chip_cross, CORE_SWAP)),
        (own_kept, cross_out_weight),
    ):
        crossed = crossed + jnp.dot(part, weight, preferred_element_type=jnp.float32)
    return finish(crossed, own_arrived, chip_cross)


def rms_norm(matrix, gain):
    values = matrix.astype(jnp.float32)
    spread = jnp.mean(values * values, axis=-1, keepdims=True)
    return (values * lax.rsqrt(spread + 1e-06) * gain).astype(jnp.bfloat16)


def window_attention(queries, keyset, valset, occupied, head_count):
    slot_count = queries.shape[0]
    window_count = slot_count // WBLK
    query_heads = queries.reshape(window_count, WBLK, head_count, HD)
    key_heads = keyset.reshape(window_count, WBLK, head_count, HD)
    value_heads = valset.reshape(window_count, WBLK, head_count, HD)
    scores = jnp.einsum(
        "wqhd,wkhd->whqk", query_heads, key_heads, preferred_element_type=jnp.float32
    ) * HD ** (-0.5)
    diagonal = (
        jnp.arange(WBLK, dtype=jnp.int32)[:, None] == jnp.arange(WBLK, dtype=jnp.int32)[None, :]
    )
    allowed = occupied.reshape(window_count, 1, WBLK) | diagonal[None]
    weights = jnp.where(allowed[:, None], jnp.exp(scores), 0.0)
    totals = jnp.sum(weights, axis=-1)
    mixed = jnp.einsum(
        "whqk,wkhd->wqhd",
        weights.astype(jnp.bfloat16),
        value_heads,
        preferred_element_type=jnp.float32,
    )
    mixed = mixed / jnp.transpose(totals, (0, 2, 1))[:, :, :, None]
    return mixed.astype(jnp.bfloat16).reshape(slot_count, head_count * HD)


def by_owner(
    voxels,
    destination,
    cond,
    norm_gain,
    qkv_weight,
    self_out_weight,
    cross_norm_gain,
    cross_q_weight,
    cond_kv_weight,
    cross_out_weight,
):
    peer_count = lax.axis_size("seq")
    part_count = lax.axis_size("mp")
    model_index = lax.axis_index("mp")
    row_count = voxels.shape[0]
    local_width = qkv_weight.shape[2]
    head_count = local_width // HD
    capacity = 2 * row_count // peer_count
    slot_count = peer_count * capacity
    owner_ids = destination // slot_count
    slot_ids = destination % slot_count
    matches = (owner_ids[:, None] == jnp.arange(peer_count, dtype=jnp.int32)[None, :]).astype(
        jnp.int32
    )
    within = jnp.sum(matches * (jnp.cumsum(matches, axis=0) - 1), axis=1)
    send_index = owner_ids * capacity + within
    normed = rms_norm(voxels, norm_gain)
    place_buffer = (
        jnp.full((slot_count,), slot_count, jnp.int32)
        .at[send_index]
        .set(slot_ids)
        .reshape(peer_count, capacity)
    )
    projected = jnp.einsum(
        "rd,cdh->rch", normed, qkv_weight, preferred_element_type=jnp.float32
    ).astype(jnp.bfloat16)
    send_buffer = (
        jnp.zeros((slot_count, 3 * local_width), jnp.bfloat16)
        .at[send_index]
        .set(projected.reshape(row_count, 3 * local_width))
    )
    received, places = (
        lax.all_to_all(
            send_buffer.reshape(peer_count, capacity, 3 * local_width),
            "seq",
            split_axis=0,
            concat_axis=0,
            tiled=True,
        ),
        lax.all_to_all(place_buffer, "seq", split_axis=0, concat_axis=0, tiled=True),
    )
    received = received.reshape(slot_count, 3 * local_width)
    places = places.reshape(slot_count)
    layout = (
        jnp.zeros((slot_count, 3 * local_width), jnp.bfloat16).at[places].set(received, mode="drop")
    )
    occupied = jnp.zeros((slot_count,), jnp.bool_).at[places].set(True, mode="drop")
    mixed = window_attention(
        layout[:, :local_width],
        layout[:, local_width : 2 * local_width],
        layout[:, 2 * local_width :],
        occupied,
        head_count,
    )
    outgoing = mixed[jnp.minimum(places, slot_count - 1)]
    returned = lax.all_to_all(
        outgoing.reshape(peer_count, capacity, local_width),
        "seq",
        split_axis=0,
        concat_axis=0,
        tiled=True,
    )
    window_mix = returned.reshape(slot_count, local_width)[send_index]
    row_share = row_count // part_count
    summed_out = lax.psum(
        jnp.dot(window_mix, self_out_weight, preferred_element_type=jnp.float32), "mp"
    )
    hidden = voxels.astype(jnp.float32) + summed_out
    normed2 = rms_norm(hidden, cross_norm_gain)
    own_hidden = lax.dynamic_slice_in_dim(hidden, model_index * row_share, row_share, 0)
    cross_query = (
        jnp.dot(normed2, cross_q_weight, preferred_element_type=jnp.float32)
        .astype(jnp.bfloat16)
        .reshape(row_count, head_count, HD)
    )
    cond_pair = jnp.einsum(
        "td,cdh->cth", cond, cond_kv_weight, preferred_element_type=jnp.float32
    ).astype(jnp.bfloat16)

    def fold_block(running, key_block, value_block):
        row_max, totals, mixed_sum = running
        scores = jnp.einsum(
            "qhd,khd->qhk", cross_query, key_block, preferred_element_type=jnp.float32
        ) * HD ** (-0.5)
        new_max = jnp.maximum(row_max, jnp.max(scores, axis=-1))
        rescale = jnp.exp(row_max - new_max)
        weights = jnp.exp(scores - new_max[:, :, None])
        totals = totals * rescale + jnp.sum(weights, axis=-1)
        update = jnp.einsum(
            "qhk,khd->qhd",
            weights.astype(jnp.bfloat16),
            value_block,
            preferred_element_type=jnp.float32,
        )
        return (new_max, totals, mixed_sum * rescale[:, :, None] + update)

    start_state = (
        jnp.full((row_count, head_count), -1e30, jnp.float32),
        jnp.zeros((row_count, head_count), jnp.float32),
        jnp.zeros((row_count, head_count, HD), jnp.float32),
    )
    key_piece = lax.all_gather(cond_pair[0], "seq", axis=0, tiled=True)
    value_piece = lax.all_gather(cond_pair[1], "seq", axis=0, tiled=True)
    token_count = key_piece.shape[0]
    sub_block = math.gcd(token_count, 512)
    key_blocks = key_piece.reshape(token_count // sub_block, sub_block, head_count, HD)
    value_blocks = value_piece.reshape(token_count // sub_block, sub_block, head_count, HD)

    def advance(state, operands):
        return (fold_block(state, operands[0], operands[1]), None)

    folded, unused = lax.scan(advance, start_state, (key_blocks, value_blocks))
    row_max, totals, mixed_sum = folded
    cross_mix = (
        (mixed_sum / totals[:, :, None]).astype(jnp.bfloat16).reshape(row_count, local_width)
    )
    cross_sum = lax.psum_scatter(
        jnp.dot(cross_mix, cross_out_weight, preferred_element_type=jnp.float32),
        "mp",
        scatter_dimension=0,
        tiled=True,
    )
    return (own_hidden + cross_sum).astype(jnp.bfloat16)


def solution(mesh):
    heads_match = mesh.shape["mp"] == 4 and mesh.shape["seq"] == 8
    return jax.shard_map(
        by_head if heads_match else by_owner,
        mesh=mesh,
        in_specs=(
            P("seq", None),
            P("seq"),
            P("seq", None),
            P(),
            P(None, None, "mp"),
            P("mp", None),
            P(),
            P(None, "mp"),
            P(None, None, "mp"),
            P("mp", None),
        ),
        out_specs=P(("seq", "mp"), None),
        check_vma=False,
    )
```

time: 162 us -> 153 us (0.944)
  waiting for transfers between devices: 29.8 us -> 24.8 us
  Pallas kernels: 61.1 us -> 56.6 us
  blocking collectives: 33.2 us -> 36.7 us
  local copies, waits for them, and re-layouts: 14 us -> 10.8 us
  starting transfers between devices: 20.7 us -> 18.3 us
    pallas_call x1, Pallas kernels: 24.2 us -> 18.6 us  [window_mixing(): pl.pallas_call(window_kernel, out_shape=jax.ShapeDtypeStruct((sources, pa...]
    all_to_all x1, blocking collectives: 33.2 us -> 36.7 us  [by_head(): mine = lax.all_to_all(sent, 'seq', split_axis=0, concat_axis=0, tiled=True)]
    pallas_call x3 -> x6, Pallas kernels: 29.1 us -> 32.1 us  [the longest x4 24.4 us: cross_mixing(): pl.pallas_call(functools.partial(cross_kernel, len(pieces), bool(state)),...]
    unnamed x51 -> x52, local copies, waits for them, and re-layouts: 12.3 us -> 9.87 us
    ppermute x7, waiting for transfers between devices: 13 us -> 10.8 us  [across(): return lax.ppermute(array, 'seq', pairs)]
    ppermute x7, starting transfers between devices: 10.8 us -> 8.66 us  [across(): return lax.ppermute(array, 'seq', pairs)]
    pallas_call x1, Pallas kernels: 6.75 us -> 4.89 us  [project(): pl.pallas_call(project_kernel, out_shape=(jax.ShapeDtypeStruct((heads, bl...]
    ppermute x13 -> x16, waiting for transfers between devices: 7.39 us -> 6.23 us  [swap(): return lax.ppermute(array, 'mp', pairs)]
  transfers between devices with their start and end apart: 21 -> 24, of which waited for: 10 -> 10; matrix products, arithmetic and copies ran while one was open for 4% -> 4% of each run, Pallas kernels for 30% -> 29%
where the time goes in v4:
time: 153 us
  Pallas kernels  56.6 us (37%)
  blocking collectives  36.7 us (24%)
  waiting for transfers between devices  24.8 us (16%)
  starting transfers between devices  18.3 us (12%)
  local copies, waits for them, and re-layouts  10.8 us (7%)
  matrix products  4.9 us (3%)
    all_to_all x1, blocking collectives, by_head(): mine = lax.all_to_all(sent, 'seq', split_axis=0, concat_axis=0, tiled=True)  36.7 us
    pallas_call x4, Pallas kernels, cross_mixing(): pl.pallas_call(functools.partial(cross_kernel, len(pieces), bool(state)),...  24.4 us
    pallas_call x1, Pallas kernels, window_mixing(): pl.pallas_call(window_kernel, out_shape=jax.ShapeDtypeStruct((sources, pa...  18.6 us
    ppermute x7, waiting for transfers between devices, across(): return lax.ppermute(array, 'seq', pairs)  10.8 us
    unnamed x52, local copies, waits for them, and re-layouts  9.87 us
    ppermute x7, starting transfers between devices, across(): return lax.ppermute(array, 'seq', pairs)  8.66 us
    all_to_all x1, waiting for transfers between devices, by_head(): near = lax.all_to_all(mixed, 'seq', split_axis=0, concat_axis=0, tiled=True)  7.84 us
    ppermute x16, waiting for transfers between devices, swap(): return lax.ppermute(array, 'mp', pairs)  6.23 us
  transfers between devices with their start and end apart: 24, of which 10 were waited for; matrix products, arithmetic and copies ran while one was open for 4% of the time, Pallas kernels for 29%

profile of v4, /device:TPU:0, one launch (start us, length us, event | category | flops | bytes accessed | tf_op | source)
XLA Modules:
  0.0 152.6 jit_solution(6923511385201579232)
XLA Ops:
  1.2 1.6 %convolution_convert_fusion = bf16[512,256]{1,0:T(8,128)(2,1)S(1)} fusion(bf16[512,1024]{1,0:T(8,128)(2,1)S(1)} %copy-done, bf16[2,1024,256]{2,1,0:T(8,128)(2,1)} %param.18), kind=kOutput, calls=%fused_computation | convolution fusion | flops 268566528 | bytes 1835008 | tf_op jit(solution)/shard_map/dot_general | solution.py:713
  4.2 1.4 copy-done.2
  5.6 4.9 %shard_map.100 = (bf16[8,592,128]{2,1,0:T(8,128)(2,1)S(1)}, f32[8,128]{1,0:T(8,128)S(1)}) custom-call(s32[1]{0:T(128)} %bitcast.core_ref, bf16[768,1024]{1,0:T(8,128)(2,1)S(1)} %copy-done.2, f32[1,1024]{1,0:T(1,128)S(1)} %bitcast.33, s32[6,128]{1,0:T(8,128)S(1)} %bitcast.34, bf16[3,1024,256]{2,1,0:T(8,128)(2,1)S(1)} %copy-done.1, ...), custom_call_target="tpu_custom_call" | custom-call | tf_op jit(solution)/shard_map/pallas_call | solution.py:151
  10.5 36.7 %all_to_all.10.mine_ref = bf16[8,592,128]{2,1,0:T(8,128)(2,1)S(1)} all-to-all(bf16[8,592,128]{2,1,0:T(8,128)(2,1)S(1)} %get-tuple-element.44), channel_id=1, replica_groups=mesh['seq'=8,'mp'=4] {'seq'}, dimensions={0} | all-to-all | bytes 2424832 | tf_op jit(solution)/shard_map/all_to_all | solution.py:727
  48.6 1.5 collective-permute-start.5
  50.1 1.9 %collective-permute-start.4 = (bf16[512,512]{1,0:T(8,128)(2,1)S(1)}, bf16[512,512]{1,0:T(8,128)(2,1)}, u32[]{:S(2)}, u32[]{:S(2)}) collective-permute-start(bf16[512,512]{1,0:T(8,128)(2,1)S(1)} %pad_maximum_fusion.refs_0_), channel_id=1, source_target_pairs={{0,16},{4,20},{8,24},{12,28},{16,0},{20,4},{24,8},{28,12},{1,17},{... | collective-permute-start | bytes 1572872 | tf_op jit(solution)/shard_map/ppermute | solution.py:689
  52.0 18.6 %shard_map.101 = bf16[8,192,128]{2,1,0:T(8,128)(2,1)S(1)} custom-call(s32[1]{0:T(128)} %bitcast.core_ref, bf16[8,592,128]{2,1,0:T(8,128)(2,1)S(1)} %all_to_all.10.mine_ref, bf16[8,592,128]{2,1,0:T(8,128)(2,1)S(1)} %collective-permute-done.1.theirs_ref), custom_call_target="tpu_custom_call" | custom-call | flops 24159191040 | bytes 2424832 | tf_op jit(solution)/shard_map/pallas_call | solution.py:356
  73.7 2.4 %collective-permute-done.4.refs_3_ = bf16[512,512]{1,0:T(8,128)(2,1)} collective-permute-done((bf16[512,512]{1,0:T(8,128)(2,1)S(1)}, bf16[512,512]{1,0:T(8,128)(2,1)}, u32[]{:S(2)}, u32[]{:S(2)}) %collective-permute-start.4) | collective-permute-done | bytes 524320 | tf_op jit(solution)/shard_map/ppermute | solution.py:689
  76.1 3.7 %all-to-all-start.1 = ((bf16[8,192,128]{2,1,0:T(8,128)(2,1)}), bf16[8,192,128]{2,1,0:T(8,128)(2,1)S(1)}, u32[]{:S(2)}, u32[]{:S(2)}) async-start(bf16[8,192,128]{2,1,0:T(8,128)(2,1)} %copy-done.6), calls=%async_computation.1 | async-start | bytes 786432 | tf_op jit(solution)/shard_map/all_to_all | solution.py:739
  80.3 2.0 %collective-permute-start.10 = (bf16[512,512]{1,0:T(8,128)(2,1)}, bf16[512,512]{1,0:T(8,128)(2,1)}, u32[]{:S(2)}, u32[]{:S(2)}) collective-permute-start(bf16[512,512]{1,0:T(8,128)(2,1)} %copy-done.14), channel_id=1, source_target_pairs={{0,4},{4,0},{8,12},{12,8},{16,20},{20,16},{24,28},{28,24},{1,5},{5... | collective-permute-start | bytes 1572872 | tf_op jit(solution)/shard_map/ppermute | solution.py:689
  82.3 1.5 collective-permute-start.9
  83.7 7.8 %all-to-all-done.1.own_ref = bf16[8,192,128]{2,1,0:T(8,128)(2,1)S(1)} async-done(((bf16[8,192,128]{2,1,0:T(8,128)(2,1)}), bf16[8,192,128]{2,1,0:T(8,128)(2,1)S(1)}, u32[]{:S(2)}, u32[]{:S(2)}) %all-to-all-start.1) | async-done | bytes 393248 | tf_op jit(solution)/shard_map/all_to_all | solution.py:739
  92.1 2.8 %collective-permute-done.11.weight_ref = bf16[256,1024]{1,0:T(8,128)(2,1)S(1)} collective-permute-done((bf16[256,1024]{1,0:T(8,128)(2,1)}, bf16[256,1024]{1,0:T(8,128)(2,1)S(1)}, u32[]{:S(2)}, u32[]{:S(2)}) %collective-permute-start.11) | collective-permute-done | bytes 524320 | tf_op jit(solution)/shard_map/ppermute | solution.py:685
  94.8 2.0 %collective-permute-done.10.refs_0_ = bf16[512,512]{1,0:T(8,128)(2,1)} collective-permute-done((bf16[512,512]{1,0:T(8,128)(2,1)}, bf16[512,512]{1,0:T(8,128)(2,1)}, u32[]{:S(2)}, u32[]{:S(2)}) %collective-permute-start.10) | collective-permute-done | bytes 524320 | tf_op jit(solution)/shard_map/ppermute | solution.py:689
  96.8 2.7 %collective-permute-done.9.refs_2_ = bf16[512,512]{1,0:T(8,128)(2,1)} collective-permute-done((bf16[512,512]{1,0:T(8,128)(2,1)}, bf16[512,512]{1,0:T(8,128)(2,1)}, u32[]{:S(2)}, u32[]{:S(2)}) %collective-permute-start.9) | collective-permute-done | bytes 524320 | tf_op jit(solution)/shard_map/ppermute | solution.py:689
  99.5 1.8 %collective-permute-done.8.own_ref = bf16[8,192,128]{2,1,0:T(8,128)(2,1)} collective-permute-done((bf16[8,192,128]{2,1,0:T(8,128)(2,1)S(1)}, bf16[8,192,128]{2,1,0:T(8,128)(2,1)}, u32[]{:S(2)}, u32[]{:S(2)}) %collective-permute-start.8) | collective-permute-done | bytes 393248 | tf_op jit(solution)/shard_map/ppermute | solution.py:685
  104.4 3.5 %shard_map.102 = (f32[384,1024]{1,0:T(8,128)S(1)}, bf16[384,768]{1,0:T(8,128)(2,1)S(1)}, f32[8,128]{1,0:T(8,128)}) custom-call(s32[1]{0:T(128)} %bitcast.core_ref, f32[8,128]{1,0:T(8,128)S(1)} %get-tuple-element.43.rank_ref, bf16[768,1024]{1,0:T(8,128)(2,1)S(1)} %copy-done.3, bf16[8,192,128]{2,1,0:T(8,128)(2,1)S(1)} %all-to-all-done.1.own_ref, ...), custom_call_target="tpu_custom_call" | custom-call | flops 4026531840 | bytes 8388608 | tf_op jit(solution)/shard_map/pallas_call | solution.py:516
  108.0 4.2 %shard_map.103 = (f32[192,1024]{1,0:T(8,128)S(1)}, bf16[384,256]{1,0:T(8,128)(2,1)S(1)}, bf16[384,256]{1,0:T(8,128)(2,1)S(1)}) custom-call(s32[1]{0:T(128)} %bitcast.core_ref, s32[1]{0:T(128)} %bitcast.1.chip_ref, f32[384,1024]{1,0:T(8,128)S(1)} %get-tuple-element.48.base_ref, bf16[384,768]{1,0:T(8,128)(2,1)S(1)} %get-tuple-element.49.order_ref, ...), custom_call_target="tpu_custom_call" | custom-call | flops 4026531840 | bytes 8388608 | tf_op jit(solution)/shard_map/pallas_call | solution.py:547
  112.3 5.4 %shard_map.104 = (f32[384,256]{1,0:T(8,128)S(1)}, f32[384,256]{1,0:T(8,128)S(1)}, f32[384,256]{1,0:T(8,128)S(1)}) custom-call(bf16[384,256]{1,0:T(8,128)(2,1)S(1)} %get-tuple-element.55.query_ref, bf16[512,512]{1,0:T(8,128)(2,1)S(1)} %copy-done.5, bf16[512,512]{1,0:T(8,128)(2,1)S(1)} %copy-done.13, bf16[512,512]{1,0:T(8,128)(2,1)S(1)} %copy-done.15, ...), custom_call_target="tpu_custom_call" | custom-call | flops 6442450944 | bytes 2490368 | tf_op jit(solution)/shard_map/pallas_call | solution.py:646
  117.8 5.6 %shard_map.105 = (f32[384,256]{1,0:T(8,128)S(1)}, f32[384,256]{1,0:T(8,128)S(1)}, f32[384,256]{1,0:T(8,128)S(1)}) custom-call(bf16[384,256]{1,0:T(8,128)(2,1)S(1)} %collective-permute-done.15.query_ref, bf16[512,512]{1,0:T(8,128)(2,1)S(1)} %copy-done.5, bf16[512,512]{1,0:T(8,128)(2,1)S(1)} %copy-done.13, bf16[512,512]{1,0:T(8,128)(2,1)S(1)} %copy-done.15, ...), custom_call_target="tpu_custom_call" | custom-call | flops 6442450944 | bytes 2490368 | tf_op jit(solution)/shard_map/pallas_call | solution.py:646
  123.4 3.7 %collective-permute-done.17.refs_3_ = bf16[512,512]{1,0:T(8,128)(2,1)S(1)} collective-permute-done((bf16[512,512]{1,0:T(8,128)(2,1)}, bf16[512,512]{1,0:T(8,128)(2,1)S(1)}, u32[]{:S(2)}, u32[]{:S(2)}) %collective-permute-start.17) | collective-permute-done | bytes 524320 | tf_op jit(solution)/shard_map/ppermute | solution.py:689
  127.1 6.8 %shard_map.107 = bf16[384,256]{1,0:T(8,128)(2,1)S(1)} custom-call(bf16[384,256]{1,0:T(8,128)(2,1)S(1)} %collective-permute-done.15.query_ref, bf16[512,512]{1,0:T(8,128)(2,1)} %collective-permute-done.10.refs_0_, bf16[512,512]{1,0:T(8,128)(2,1)S(1)} %collective-permute-done.16.refs_1_, bf16[512,512]{1,0:T(8,128)(2,1)} %collective-permute-done.9.refs_2_, ...), custom_call_target="tpu_custom_call" | custom-call | flops 6442450944 | bytes 2490368 | tf_op jit(solution)/shard_map/pallas_call | solution.py:646
  140.2 6.6 %shard_map.106 = bf16[384,256]{1,0:T(8,128)(2,1)S(1)} custom-call(bf16[384,256]{1,0:T(8,128)(2,1)S(1)} %get-tuple-element.55.query_ref, bf16[512,512]{1,0:T(8,128)(2,1)} %collective-permute-done.10.refs_0_, bf16[512,512]{1,0:T(8,128)(2,1)S(1)} %copy-done.19, bf16[512,512]{1,0:T(8,128)(2,1)} %collective-permute-done.9.refs_2_, ...), custom_call_target="tpu_custom_call" | custom-call | flops 6442450944 | bytes 2490368 | tf_op jit(solution)/shard_map/pallas_call | solution.py:646
  146.9 1.6 %collective-permute-start.22 = (bf16[192,256]{1,0:T(8,128)(2,1)S(1)}, bf16[192,256]{1,0:T(8,128)(2,1)S(1)}, u32[]{:S(2)}, u32[]{:S(2)}) collective-permute-start(bf16[192,256]{1,0:T(8,128)(2,1)S(1)} %dynamic-slice_bitcast_fusion), channel_id=1, source_target_pairs={{0,2},{2,0},{1,3},{3,1},{4,6},{6,4},{5,7},{7,5},{8,10},{10,8},{9,1... | collective-permute-start | bytes 294920 | tf_op jit(solution)/shard_map/ppermute | solution.py:685
  (94 shorter events, 21.7 us)
Async XLA Ops:
  0.0 3.8 %collective-permute-start = (bf16[3,1024,256]{2,1,0:T(8,128)(2,1)}, bf16[3,1024,256]{2,1,0:T(8,128)(2,1)}, u32[]{:S(2)}, u32[]{:S(2)}) collective-permute-start(bf16[3,1024,256]{2,1,0:T(8,128)(2,1)} %own_ref.1), channel_id=1, source_target_pairs={{0,1},{1,0},{2,3},{3,2},{4,5},{5,4},{6,7},{7,6},{8,9},{9,8},{10,11... | collective-permute-start | bytes 4718600 | tf_op jit(solution)/shard_map/ppermute | solution.py:685
  47.2 4.7 %collective-permute-start.1 = (bf16[8,592,128]{2,1,0:T(8,128)(2,1)S(1)}, bf16[8,592,128]{2,1,0:T(8,128)(2,1)S(1)}, u32[]{:S(2)}, u32[]{:S(2)}) collective-permute-start(bf16[8,592,128]{2,1,0:T(8,128)(2,1)S(1)} %all_to_all.10.mine_ref), channel_id=1, source_target_pairs={{0,1},{1,0},{2,3},{3,2},{4,5},{5,4},{6,7},{7,6},{8,9},{9,8},{10,11... | collective-permute-start | bytes 3637256 | tf_op jit(solution)/shard_map/ppermute | solution.py:685
  47.3 24.1 %collective-permute-start.2 = (bf16[512,512]{1,0:T(8,128)(2,1)S(1)}, bf16[512,512]{1,0:T(8,128)(2,1)S(1)}, u32[]{:S(2)}, u32[]{:S(2)}) collective-permute-start(bf16[512,512]{1,0:T(8,128)(2,1)S(1)} %pad_maximum_fusion.refs_0_), channel_id=1, source_target_pairs={{0,4},{4,0},{8,12},{12,8},{16,20},{20,16},{24,28},{28,24},{1,5},{5... | collective-permute-start | bytes 1572872 | tf_op jit(solution)/shard_map/ppermute | solution.py:689
  48.5 23.6 %collective-permute-start.3 = (bf16[512,512]{1,0:T(8,128)(2,1)S(1)}, bf16[512,512]{1,0:T(8,128)(2,1)S(1)}, u32[]{:S(2)}, u32[]{:S(2)}) collective-permute-start(bf16[512,512]{1,0:T(8,128)(2,1)S(1)} %pad_maximum_fusion.refs_0_), channel_id=1, source_target_pairs={{0,8},{4,12},{8,0},{12,4},{16,24},{20,28},{24,16},{28,20},{1,9},{5... | collective-permute-start | bytes 1572872 | tf_op jit(solution)/shard_map/ppermute | solution.py:689
  48.6 23.5 %collective-permute-start.5 = (bf16[256,1024]{1,0:T(8,128)(2,1)S(1)}, bf16[256,1024]{1,0:T(8,128)(2,1)S(1)}, u32[]{:S(2)}, u32[]{:S(2)}) collective-permute-start(bf16[256,1024]{1,0:T(8,128)(2,1)S(1)} %copy-done.9), channel_id=1, source_target_pairs={{0,2},{2,0},{1,3},{3,1},{4,6},{6,4},{5,7},{7,5},{8,10},{10,8},{9,1... | collective-permute-start | bytes 1572872 | tf_op jit(solution)/shard_map/ppermute | solution.py:685
  50.1 25.9 %collective-permute-start.4 = (bf16[512,512]{1,0:T(8,128)(2,1)S(1)}, bf16[512,512]{1,0:T(8,128)(2,1)}, u32[]{:S(2)}, u32[]{:S(2)}) collective-permute-start(bf16[512,512]{1,0:T(8,128)(2,1)S(1)} %pad_maximum_fusion.refs_0_), channel_id=1, source_target_pairs={{0,16},{4,20},{8,24},{12,28},{16,0},{20,4},{24,8},{28,12},{1,17},{... | collective-permute-start | bytes 1572872 | tf_op jit(solution)/shard_map/ppermute | solution.py:689
  76.1 15.5 %all-to-all-start.1 = ((bf16[8,192,128]{2,1,0:T(8,128)(2,1)}), bf16[8,192,128]{2,1,0:T(8,128)(2,1)S(1)}, u32[]{:S(2)}, u32[]{:S(2)}) async-start(bf16[8,192,128]{2,1,0:T(8,128)(2,1)} %copy-done.6), calls=%async_computation.1 | async-start | bytes 786432 | tf_op jit(solution)/shard_map/all_to_all | solution.py:739
  79.7 15.1 %collective-permute-start.11 = (bf16[256,1024]{1,0:T(8,128)(2,1)}, bf16[256,1024]{1,0:T(8,128)(2,1)S(1)}, u32[]{:S(2)}, u32[]{:S(2)}) collective-permute-start(bf16[256,1024]{1,0:T(8,128)(2,1)} %param.19), channel_id=1, source_target_pairs={{0,2},{2,0},{1,3},{3,1},{4,6},{6,4},{5,7},{7,5},{8,10},{10,8},{9,1... | collective-permute-start | bytes 1572872 | tf_op jit(solution)/shard_map/ppermute | solution.py:685
  80.3 16.5 %collective-permute-start.10 = (bf16[512,512]{1,0:T(8,128)(2,1)}, bf16[512,512]{1,0:T(8,128)(2,1)}, u32[]{:S(2)}, u32[]{:S(2)}) collective-permute-start(bf16[512,512]{1,0:T(8,128)(2,1)} %copy-done.14), channel_id=1, source_target_pairs={{0,4},{4,0},{8,12},{12,8},{16,20},{20,16},{24,28},{28,24},{1,5},{5... | collective-permute-start | bytes 1572872 | tf_op jit(solution)/shard_map/ppermute | solution.py:689
  82.3 17.3 %collective-permute-start.9 = (bf16[512,512]{1,0:T(8,128)(2,1)}, bf16[512,512]{1,0:T(8,128)(2,1)}, u32[]{:S(2)}, u32[]{:S(2)}) collective-permute-start(bf16[512,512]{1,0:T(8,128)(2,1)} %collective-permute-done.4.refs_3_), channel_id=1, source_target_pairs={{0,8},{4,12},{8,0},{12,4},{16,24},{20,28},{24,16},{28,20},{1,9},{5... | collective-permute-start | bytes 1572872 | tf_op jit(solution)/shard_map/ppermute | solution.py:689
  83.7 17.6 %collective-permute-start.7 = (bf16[256,1024]{1,0:T(8,128)(2,1)}, bf16[256,1024]{1,0:T(8,128)(2,1)}, u32[]{:S(2)}, u32[]{:S(2)}) collective-permute-start(bf16[256,1024]{1,0:T(8,128)(2,1)} %weight_ref.1), channel_id=1, source_target_pairs={{0,1},{1,0},{2,3},{3,2},{4,5},{5,4},{6,7},{7,6},{8,9},{9,8},{10,11... | collective-permute-start | bytes 1572872 | tf_op jit(solution)/shard_map/ppermute | solution.py:685
  91.6 9.8 %collective-permute-start.8 = (bf16[8,192,128]{2,1,0:T(8,128)(2,1)S(1)}, bf16[8,192,128]{2,1,0:T(8,128)(2,1)}, u32[]{:S(2)}, u32[]{:S(2)}) collective-permute-start(bf16[8,192,128]{2,1,0:T(8,128)(2,1)S(1)} %all-to-all-done.1.own_ref), channel_id=1, source_target_pairs={{0,2},{2,0},{1,3},{3,1},{4,6},{6,4},{5,7},{7,5},{8,10},{10,8},{9,1... | collective-permute-start | bytes 1179656 | tf_op jit(solution)/shard_map/ppermute | solution.py:685
  94.8 7.9 %collective-permute-start.6 = (bf16[8,192,128]{2,1,0:T(8,128)(2,1)S(1)}, bf16[8,192,128]{2,1,0:T(8,128)(2,1)}, u32[]{:S(2)}, u32[]{:S(2)}) collective-permute-start(bf16[8,192,128]{2,1,0:T(8,128)(2,1)S(1)} %all-to-all-done.1.own_ref), channel_id=1, source_target_pairs={{0,1},{1,0},{2,3},{3,2},{4,5},{5,4},{6,7},{7,6},{8,9},{9,8},{10,11... | collective-permute-start | bytes 1179656 | tf_op jit(solution)/shard_map/ppermute | solution.py:685
  96.8 11.1 %collective-permute-start.14 = (bf16[1024,256]{1,0:T(8,128)(2,1)}, bf16[1024,256]{1,0:T(8,128)(2,1)}, u32[]{:S(2)}, u32[]{:S(2)}) collective-permute-start(bf16[1024,256]{1,0:T(8,128)(2,1)} %query_weight_ref.1), channel_id=1, source_target_pairs={{0,1},{1,0},{2,3},{3,2},{4,5},{5,4},{6,7},{7,6},{8,9},{9,8},{10,11... | collective-permute-start | bytes 1572872 | tf_op jit(solution)/shard_map/ppermute | solution.py:685
  99.5 8.4 %collective-permute-start.13 = (bf16[256,1024]{1,0:T(8,128)(2,1)}, bf16[256,1024]{1,0:T(8,128)(2,1)}, u32[]{:S(2)}, u32[]{:S(2)}) collective-permute-start(bf16[256,1024]{1,0:T(8,128)(2,1)} %copy-done.16), channel_id=1, source_target_pairs={{0,1},{1,0},{2,3},{3,2},{4,5},{5,4},{6,7},{7,6},{8,9},{9,8},{10,11... | collective-permute-start | bytes 1572872 | tf_op jit(solution)/shard_map/ppermute | solution.py:685
  101.3 6.6 %collective-permute-start.12 = (bf16[8,192,128]{2,1,0:T(8,128)(2,1)}, bf16[8,192,128]{2,1,0:T(8,128)(2,1)}, u32[]{:S(2)}, u32[]{:S(2)}) collective-permute-start(bf16[8,192,128]{2,1,0:T(8,128)(2,1)} %collective-permute-done.8.own_ref), channel_id=1, source_target_pairs={{0,1},{1,0},{2,3},{3,2},{4,5},{5,4},{6,7},{7,6},{8,9},{9,8},{10,11... | collective-permute-start | bytes 1179656 | tf_op jit(solution)/shard_map/ppermute | solution.py:685
  101.3 16.4 %collective-permute-start.16 = (bf16[512,512]{1,0:T(8,128)(2,1)}, bf16[512,512]{1,0:T(8,128)(2,1)S(1)}, u32[]{:S(2)}, u32[]{:S(2)}) collective-permute-start(bf16[512,512]{1,0:T(8,128)(2,1)} %collective-permute-done.4.refs_3_), channel_id=1, source_target_pairs={{0,4},{4,0},{8,12},{12,8},{16,20},{20,16},{24,28},{28,24},{1,5},{5... | collective-permute-start | bytes 1572872 | tf_op jit(solution)/shard_map/ppermute | solution.py:689
  102.7 24.4 %collective-permute-start.17 = (bf16[512,512]{1,0:T(8,128)(2,1)}, bf16[512,512]{1,0:T(8,128)(2,1)S(1)}, u32[]{:S(2)}, u32[]{:S(2)}) collective-permute-start(bf16[512,512]{1,0:T(8,128)(2,1)} %collective-permute-done.9.refs_2_), channel_id=1, source_target_pairs={{0,4},{4,0},{8,12},{12,8},{16,20},{20,16},{24,28},{28,24},{1,5},{5... | collective-permute-start | bytes 1572872 | tf_op jit(solution)/shard_map/ppermute | solution.py:689
  112.2 5.5 %collective-permute-start.15 = (bf16[384,256]{1,0:T(8,128)(2,1)S(1)}, bf16[384,256]{1,0:T(8,128)(2,1)S(1)}, u32[]{:S(2)}, u32[]{:S(2)}) collective-permute-start(bf16[384,256]{1,0:T(8,128)(2,1)S(1)} %get-tuple-element.57), channel_id=1, source_target_pairs={{0,1},{1,0},{2,3},{3,2},{4,5},{5,4},{6,7},{7,6},{8,9},{9,8},{10,11... | collective-permute-start | bytes 589832 | tf_op jit(solution)/shard_map/ppermute | solution.py:685
  134.0 1.6 %collective-permute-start.18 = (bf16[384,256]{1,0:T(8,128)(2,1)S(1)}, bf16[384,256]{1,0:T(8,128)(2,1)}, u32[]{:S(2)}, u32[]{:S(2)}) collective-permute-start(bf16[384,256]{1,0:T(8,128)(2,1)S(1)} %shard_map.107), channel_id=1, source_target_pairs={{0,1},{1,0},{2,3},{3,2},{4,5},{5,4},{6,7},{7,6},{8,9},{9,8},{10,11... | collective-permute-start | bytes 589832 | tf_op jit(solution)/shard_map/ppermute | solution.py:685
  134.0 14.4 %collective-permute-start.20 = (bf16[256,1024]{1,0:T(8,128)(2,1)}, bf16[256,1024]{1,0:T(8,128)(2,1)}, u32[]{:S(2)}, u32[]{:S(2)}) collective-permute-start(bf16[256,1024]{1,0:T(8,128)(2,1)} %param.19), channel_id=1, source_target_pairs={{0,1},{1,0},{2,3},{3,2},{4,5},{5,4},{6,7},{7,6},{8,9},{9,8},{10,11... | collective-permute-start | bytes 1572872 | tf_op jit(solution)/shard_map/ppermute | solution.py:685
  134.5 15.2 %collective-permute-start.21 = (bf16[256,1024]{1,0:T(8,128)(2,1)S(1)}, bf16[256,1024]{1,0:T(8,128)(2,1)S(1)}, u32[]{:S(2)}, u32[]{:S(2)}) collective-permute-start(bf16[256,1024]{1,0:T(8,128)(2,1)S(1)} %collective-permute-done.11.weight_ref), channel_id=1, source_target_pairs={{0,1},{1,0},{2,3},{3,2},{4,5},{5,4},{6,7},{7,6},{8,9},{9,8},{10,11... | collective-permute-start | bytes 1572872 | tf_op jit(solution)/shard_map/ppermute | solution.py:685
  136.5 10.3 %collective-permute-start.19 = (bf16[192,256]{1,0:T(8,128)(2,1)S(1)}, bf16[192,256]{1,0:T(8,128)(2,1)S(1)}, u32[]{:S(2)}, u32[]{:S(2)}) collective-permute-start(bf16[192,256]{1,0:T(8,128)(2,1)S(1)} %get-tuple-element.80), channel_id=1, source_target_pairs={{0,2},{2,0},{1,3},{3,1},{4,6},{6,4},{5,7},{7,5},{8,10},{10,8},{9,1... | collective-permute-start | bytes 294920 | tf_op jit(solution)/shard_map/ppermute | solution.py:685
  146.9 4.7 %collective-permute-start.22 = (bf16[192,256]{1,0:T(8,128)(2,1)S(1)}, bf16[192,256]{1,0:T(8,128)(2,1)S(1)}, u32[]{:S(2)}, u32[]{:S(2)}) collective-permute-start(bf16[192,256]{1,0:T(8,128)(2,1)S(1)} %dynamic-slice_bitcast_fusion), channel_id=1, source_target_pairs={{0,2},{2,0},{1,3},{3,1},{4,6},{6,4},{5,7},{7,5},{8,10},{10,8},{9,1... | collective-permute-start | bytes 294920 | tf_op jit(solution)/shard_map/ppermute | solution.py:685
  (26 other events, 202.1 us)

commit v5 on v4

--- a/solution.py
+++ b/solution.py
@@ -16,6 +16,7 @@
 BATCH = 4
 CORE_SWAP = ((0, 1), (1, 0), (2, 3), (3, 2))
 CHIP_SWAP = ((0, 2), (2, 0), (1, 3), (3, 1))
+BOTH_SWAP = ((0, 3), (3, 0), (1, 2), (2, 1))
 SIDE_SWAP = tuple((i, i ^ 1) for i in range(8))
 NEXT_SWAP = tuple((i, i ^ 2) for i in range(8))
 SKIP_SWAP = tuple((i, i ^ 4) for i in range(8))
@@ -38,8 +39,10 @@
 
 
 def project_kernel(
-    core_ref, vox_ref, gain_ref, place_ref, own_ref, other_ref, out_ref, rank_ref, normed_ref, ids_ref
+    core_ref, seq_ref, vox_ref, gain_ref, place_ref, own_ref, other_ref, *refs
 ):
+    *out_refs, rank_ref, normed_ref, ids_ref, blob_ref, local_ref, copy_sem = refs
+    vox_copy = pltpu.make_async_copy(vox_ref, local_ref, copy_sem.at[0])
     step = pl.program_id(0)
     rows = normed_ref.shape[0]
     packed = rows // 2
@@ -47,6 +50,7 @@
 
     @pl.when(step == 0)
     def _():
+        vox_copy.start()
         places = place_ref[...].astype(jnp.float32)
         place_rows = [places[g : g + 1] for g in range(groups)]
         place_columns = [columns_of(row) for row in place_rows]
@@ -94,11 +98,12 @@
             jnp.float32
         )
         order = jnp.concatenate([one_hot(row == wanted) for row in rank_rows], axis=1)
-        values = jnp.dot(order, vox_ref[...], preferred_element_type=jnp.float32)
+        vox_copy.wait()
+        values = jnp.dot(order, local_ref[...], preferred_element_type=jnp.float32)
         spread = jnp.mean(values * values, axis=-1, keepdims=True)
         normed_ref[...] = (values * lax.rsqrt(spread + 1e-06) * gain_ref[...]).astype(jnp.bfloat16)
 
-    def emit(weight_ref):
+    def emit(weight_ref, holder):
         normed = normed_ref[...]
         low = low_lanes((rows, LANES))
         low_packed = low_lanes((packed, LANES))
@@ -121,77 +126,67 @@
                 ),
             )
             for side, (keyval, queries) in enumerate(pairs):
-                head = at // HD + side
-                out_ref[head, :rows] = keyval.astype(jnp.bfloat16)
-                out_ref[head, rows : rows + ID_ROWS] = ids_ref[...]
-                out_ref[head, rows + ID_ROWS :] = queries.astype(jnp.bfloat16)
+                head = holder * (weight_ref.shape[2] // HD) + at // HD + side
+                target = head ^ seq_ref[0]
+                blob_ref[target, :rows] = keyval.astype(jnp.bfloat16)
+                blob_ref[target, rows : rows + ID_ROWS] = ids_ref[...]
+                blob_ref[target, rows + ID_ROWS :] = queries.astype(jnp.bfloat16)
 
     @pl.when(step == 0)
     def _():
-        emit(own_ref)
+        emit(own_ref, core_ref[0])
 
     @pl.when(step == 1)
     def _():
-        emit(other_ref)
-
-
-def project(core, vox, gain, places, own_weight, other_weight):
+        emit(other_ref, 1 - core_ref[0])
+        for target, out_ref in enumerate(out_refs):
+            out_ref[...] = blob_ref[target]
+
+
+def project(core, seq, vox, gain, places, own_weight, other_weight):
     row_count, width = vox.shape
     rows = row_count // 2
     local_width = own_weight.shape[2]
     heads = 2 * local_width // HD
     blob = rows + ID_ROWS + rows // 2
 
-    def out_map(step, core_ref):
-        return (jnp.where(step == 0, core_ref[0], 1 - core_ref[0]), 0, 0)
-
-    def whole(step, core_ref):
-        return (0, 0)
-
+    def fixed(array):
+        return pl.BlockSpec(array.shape, lambda step, *refs: (0,) * array.ndim)
+
+    outs = [jax.ShapeDtypeStruct((blob, LANES), jnp.bfloat16)] * heads
+    outs.append(jax.ShapeDtypeStruct((8, LANES), jnp.float32))
+    operands = (vox, gain, places, own_weight, other_weight)
     return pl.pallas_call(
         project_kernel,
-        out_shape=(
-            jax.ShapeDtypeStruct((heads, blob, LANES), jnp.bfloat16),
-            jax.ShapeDtypeStruct((8, LANES), jnp.float32),
-        ),
+        out_shape=outs,
         grid_spec=pltpu.PrefetchScalarGridSpec(
-            num_scalar_prefetch=1,
+            num_scalar_prefetch=2,
             grid=(2,),
-            in_specs=[
-                pl.BlockSpec((row_count, width), whole),
-                pl.BlockSpec((1, width), whole),
-                pl.BlockSpec(places.shape, whole),
-                pl.BlockSpec(own_weight.shape, lambda step, core_ref: (0, 0, 0)),
-                pl.BlockSpec(own_weight.shape, lambda step, core_ref: (0, 0, 0)),
-            ],
-            out_specs=(pl.BlockSpec((heads // 2, blob, LANES), out_map), pl.BlockSpec((8, LANES), whole)),
+            in_specs=[pl.BlockSpec(memory_space=pl.ANY)]
+            + [fixed(operand) for operand in operands[1:]],
+            out_specs=[fixed(out) for out in outs],
             scratch_shapes=[
                 pltpu.VMEM((rows, width), jnp.bfloat16),
                 pltpu.VMEM((ID_ROWS, LANES), jnp.bfloat16),
+                pltpu.VMEM((heads, blob, LANES), jnp.bfloat16),
+                pltpu.VMEM((row_count, width), jnp.bfloat16),
+                pltpu.SemaphoreType.DMA((1,)),
             ],
         ),
         compiler_params=pltpu.CompilerParams(vmem_limit_bytes=28 * MEGA),
-    )(core, vox, gain, places, own_weight, other_weight)
+    )(core, seq, *operands)
 
 
 def window_kernel(
     core_ref,
-    mine_ref,
-    theirs_ref,
-    out_ref,
-    wire_ref,
-    key_ref,
-    window_ref,
-    query_ref,
-    column_ref,
-    sum_ref,
-    total_ref,
-    plan_ref,
-    plan_smem,
-    late_smem,
-    copy_sem,
+    seq_ref,
+    *refs,
 ):
-    sources, packed, _ = out_ref.shape
+    sources = (len(refs) - 10) // 2
+    mine_refs, theirs_refs, refs = refs[:sources], refs[sources : 2 * sources], refs[2 * sources :]
+    out_ref, key_ref, window_ref, query_ref, column_ref, *refs = refs
+    sum_ref, total_ref, plan_ref, plan_smem, late_smem, copy_sem = refs
+    packed = out_ref.shape[1]
     rows = 2 * packed
     blocks = rows // LANES
     last = 2 * rows // WBLK
@@ -200,29 +195,13 @@
 
     low = low_lanes((8, LANES))
     real = lax.broadcasted_iota(jnp.int32, (8, LANES), 0) < 2 * blocks
-    copies = [
-        pltpu.make_async_copy(source, target, copy_sem.at[index])
-        for index, (source, target) in enumerate(
-            (
-                (mine_ref.at[:, pl.ds(rows, ID_ROWS + packed)], wire_ref),
-                (
-                    mine_ref.at[:, pl.ds(0, rows)],
-                    key_ref.at[:, pl.ds(pl.multiple_of(core * rows, LANES), rows)],
-                ),
-                (
-                    theirs_ref.at[:, pl.ds(0, rows)],
-                    key_ref.at[:, pl.ds(pl.multiple_of((1 - core) * rows, LANES), rows)],
-                ),
-            )
-        )
-    ]
-    for copy in copies:
-        copy.start()
+    for index, (mine_ref, theirs_ref) in enumerate(zip(mine_refs, theirs_refs)):
+        for ref, side in ((mine_ref, core), (theirs_ref, 1 - core)):
+            key_ref[index, pl.ds(pl.multiple_of(side * rows, LANES), rows)] = ref[:rows]
     key_ref[:, 2 * rows :] = jnp.zeros((sources, 2 * LANES, LANES), jnp.bfloat16)
-    copies[0].wait()
     bounds = []
     for index in range(sources):
-        tile = wire_ref[index, :ID_ROWS].astype(jnp.float32)
+        tile = mine_refs[index][rows : rows + ID_ROWS].astype(jnp.float32)
         ids = tile[:8] * 256.0 + tile[8:]
         bounds.append(ids[2 * blocks : 2 * blocks + 1])
         even = jnp.where(real, ids, -1.0)
@@ -257,11 +236,9 @@
             )
     plan_ref[0] = first.astype(jnp.int32)
     plan_ref[1] = jnp.floor((beyond - first + 3.0) * 0.25).astype(jnp.int32)
-    plan_copy = pltpu.make_async_copy(plan_ref, plan_smem, copy_sem.at[3])
+    plan_copy = pltpu.make_async_copy(plan_ref, plan_smem, copy_sem.at[0])
     plan_copy.start()
     plan_copy.wait()
-    copies[1].wait()
-    copies[2].wait()
 
     def fold(pair, other, turn, query_part, query_ids, sums, total):
         start = jnp.minimum(plan_smem[0, other, pair] + 4 * turn, last)
@@ -283,17 +260,20 @@
             total + jnp.dot(rounded, keyval, preferred_element_type=jnp.float32),
         )
 
-    def sweep(source, carry):
-        wire = wire_ref[source, ID_ROWS:].astype(jnp.float32)
+    for source, ref in enumerate(mine_refs):
+        wire = ref[rows + ID_ROWS :].astype(jnp.float32)
         query = jnp.concatenate(
             [jnp.where(low_packed, wire, 0.0), jnp.where(low_packed, swap_halves(wire), 0.0)],
             axis=0,
         ).astype(jnp.bfloat16)
         for block in range(blocks):
+            query_ref[source * blocks + block] = query[block * LANES : (block + 1) * LANES]
+
+    def sweep(source, carry):
+        for block in range(blocks):
             at = source * blocks + block
-            query_part = query[block * LANES : (block + 1) * LANES]
+            query_part = query_ref[at]
             query_ids = columns_of(window_ref[source, 0, pl.ds(core * blocks + block, 1)])
-            query_ref[at] = query_part
             column_ref[at] = query_ids
             sums = jnp.zeros((LANES, LANES), jnp.float32)
             total = jnp.zeros((LANES, LANES), jnp.float32)
@@ -342,13 +322,13 @@
             ],
             axis=0,
         )
-        out_ref[source] = jnp.where(low_packed, swap_halves(mixed[:packed]), mixed[packed:]).astype(
+        out_ref[source ^ seq_ref[0]] = jnp.where(low_packed, swap_halves(mixed[:packed]), mixed[packed:]).astype(
             jnp.bfloat16
         )
 
 
-def window_mixing(core, mine, theirs, packed):
-    sources = mine.shape[0]
+def window_mixing(core, seq, mine, theirs, packed):
+    sources = len(mine)
     rows = 2 * packed
     blocks = rows // LANES
     vmem = pl.BlockSpec(memory_space=pltpu.VMEM)
@@ -356,10 +336,9 @@
     return pl.pallas_call(
         window_kernel,
         out_shape=jax.ShapeDtypeStruct((sources, packed, LANES), jnp.bfloat16),
-        in_specs=[smem] + [pl.BlockSpec(memory_space=pltpu.HBM)] * 2,
+        in_specs=[smem] * 2 + [vmem] * (2 * sources),
         out_specs=vmem,
         scratch_shapes=[
-            pltpu.VMEM((sources, ID_ROWS + packed, LANES), jnp.bfloat16),
             pltpu.VMEM((sources, 2 * rows + 2 * LANES, LANES), jnp.bfloat16),
             pltpu.VMEM((sources, 2, 8, LANES), jnp.float32),
             pltpu.VMEM((sources * blocks + 1, LANES, LANES), jnp.bfloat16),
@@ -369,15 +348,15 @@
             pltpu.VMEM((2, sources, LANES), jnp.int32),
             pltpu.SMEM((2, sources, LANES), jnp.int32),
             pltpu.SMEM((sources * sources * blocks + 2 * BATCH,), jnp.int32),
-            pltpu.SemaphoreType.DMA((4,)),
+            pltpu.SemaphoreType.DMA((1,)),
         ],
         compiler_params=pltpu.CompilerParams(vmem_limit_bytes=24 * MEGA),
         cost_estimate=pl.CostEstimate(
             flops=80 * LANES * (sources * packed) ** 2,
             transcendentals=2 * (sources * packed) ** 2,
-            bytes_accessed=2 * (mine.size + theirs.size),
+            bytes_accessed=4 * sources * mine[0].size,
         ),
-    )(core, mine, theirs)
+    )(core, seq, *mine, *theirs)
 
 
 def fetch(refs, local_ref, copy_sem):
@@ -399,7 +378,7 @@
         for pair in range(heads // 2):
             holder = core if pair < heads // 4 else 1 - core
             head = holder * (heads // 2) + (pair % (heads // 4)) * 2
-            first, second = ref[head].astype(jnp.float32), ref[head + 1].astype(jnp.float32)
+            first, second = (ref[at].astype(jnp.float32) for at in (head, head + 1))
             at = pair * LANES
             mix_ref[pl.ds(offset, share), at : at + LANES] = jnp.where(
                 low, first, swap_halves(second)
@@ -567,118 +546,86 @@
     )(core, chip, base, order, gain, *mixes, *weights, *query_weights)
 
 
-def cross_kernel(piece_count, merging, query_ref, *refs):
-    piece_refs, refs = refs[:piece_count], refs[piece_count:]
-    if merging:
-        *old_refs, out_ref, score_ref, local_ref, copy_sem = refs
-    else:
-        *out_refs, score_ref, local_ref, copy_sem = refs
-    rows, local_width = query_ref.shape
+def cross_kernel(chip_ref, *refs):
+    query_refs, piece_refs, out_refs, score_ref = refs[:2], refs[2:-5], refs[-5:-1], refs[-1]
+    rows, local_width = query_refs[0].shape
+    share = rows // 2
     low = low_lanes((rows, LANES))
     zero = jnp.zeros((), jnp.bfloat16)
     chunk = piece_refs[0].shape[0]
-    copies = [
-        pltpu.make_async_copy(ref, local_ref.at[index], copy_sem.at[index])
-        for index, ref in enumerate(piece_refs)
-    ]
-    for copy in copies:
-        copy.start()
+    chip = chip_ref[0]
 
     def lane_groups(values):
         return [values[:, g : g + LANES] for g in range(0, chunk, LANES)]
 
-    for pair in range(0, local_width, LANES):
-        if merging:
-            old_peak, old_sums, old_total = (ref[:, pair : pair + LANES] for ref in old_refs)
-        results = []
-        for head in range(2):
-            query = jnp.where(low == (head == 0), query_ref[:, pair : pair + LANES], zero)
-            peak = jnp.full((rows, LANES), -jnp.inf, jnp.float32)
-            for index in range(piece_count):
-                if pair + head == 0:
-                    copies[index].wait()
-                scores = lax.dot_general(
-                    query,
-                    local_ref[index, :, pair : pair + LANES],
-                    (((1,), (1,)), ((), ())),
-                    preferred_element_type=jnp.float32,
-                )
-                score_ref[head, :, index * chunk : (index + 1) * chunk] = scores
-                peak = functools.reduce(jnp.maximum, lane_groups(scores), peak)
-            row_max = jnp.max(peak, axis=-1, keepdims=True)
-            if merging:
-                row_max = jnp.maximum(row_max, old_peak[:, head * HD : head * HD + 1])
-            sums = jnp.zeros((rows, LANES), jnp.float32)
-            total = jnp.zeros((rows, LANES), jnp.float32)
-            for index in range(piece_count):
-                weights = jnp.exp(
-                    score_ref[head, :, index * chunk : (index + 1) * chunk] - row_max
-                )
-                sums = functools.reduce(jnp.add, lane_groups(weights), sums)
-                total = total + jnp.dot(
-                    weights.astype(jnp.bfloat16),
-                    local_ref[index, :, local_width + pair : local_width + pair + LANES],
-                    preferred_element_type=jnp.float32,
-                )
-            results.append((row_max, jnp.sum(sums, axis=-1, keepdims=True), total))
-        new_peak, new_sums, new_total = (
-            jnp.where(low, first, second) for first, second in zip(*results)
-        )
-        if merging:
-            scale = jnp.exp(old_peak - new_peak)
-            out_ref[:, pair : pair + LANES] = (
-                (new_total + old_total * scale) / (new_sums + old_sums * scale)
-            ).astype(jnp.bfloat16)
-        else:
-            for ref, values in zip(out_refs, (new_peak, new_sums, new_total)):
-                ref[:, pair : pair + LANES] = values
-
-
-def cross_mixing(queries, pieces, state=()):
-    rows, local_width = queries.shape
+    for turn, query_ref in enumerate(query_refs):
+        for pair in range(0, local_width, LANES):
+            mixes = []
+            for head in range(2):
+                query = jnp.where(low == (head == 0), query_ref[:, pair : pair + LANES], zero)
+                peak = jnp.full((rows, LANES), -jnp.inf, jnp.float32)
+                for index, ref in enumerate(piece_refs):
+                    scores = lax.dot_general(
+                        query,
+                        ref[:, pair : pair + LANES],
+                        (((1,), (1,)), ((), ())),
+                        preferred_element_type=jnp.float32,
+                    )
+                    score_ref[head, :, index * chunk : (index + 1) * chunk] = scores
+                    peak = functools.reduce(jnp.maximum, lane_groups(scores), peak)
+                row_max = jnp.max(peak, axis=-1, keepdims=True)
+                sums = jnp.zeros((rows, LANES), jnp.float32)
+                total = jnp.zeros((rows, LANES), jnp.float32)
+                for index, ref in enumerate(piece_refs):
+                    weights = jnp.exp(
+                        score_ref[head, :, index * chunk : (index + 1) * chunk] - row_max
+                    )
+                    sums = functools.reduce(jnp.add, lane_groups(weights), sums)
+                    total = total + jnp.dot(
+                        weights.astype(jnp.bfloat16),
+                        ref[:, local_width + pair : local_width + pair + LANES],
+                        preferred_element_type=jnp.float32,
+                    )
+                mixes.append(total / jnp.sum(sums, axis=-1, keepdims=True))
+            mixed = jnp.where(low, mixes[0], mixes[1])
+            halves = (mixed[:share], mixed[share:])
+            for side, out_ref in enumerate(out_refs[2 * turn : 2 * turn + 2]):
+                out_ref[:, pair : pair + LANES] = jnp.where(
+                    chip == side, halves[0], halves[1]
+                ).astype(jnp.bfloat16)
+
+
+def cross_mixing(chip, queries, pieces):
+    rows, local_width = queries[0].shape
     tokens = sum(piece.shape[0] for piece in pieces)
-    scored = rows * tokens * local_width // HD
     block = pl.BlockSpec(memory_space=pltpu.VMEM)
-    if state:
-        outs = jax.ShapeDtypeStruct((rows, local_width), jnp.bfloat16)
-    else:
-        outs = (jax.ShapeDtypeStruct((rows, local_width), jnp.float32),) * 3
     return pl.pallas_call(
-        functools.partial(cross_kernel, len(pieces), bool(state)),
-        out_shape=outs,
-        in_specs=[block]
-        + [pl.BlockSpec(memory_space=pltpu.HBM)] * len(pieces)
-        + [block] * len(state),
-        out_specs=block if state else (block,) * 3,
-        scratch_shapes=[
-            pltpu.VMEM((2, rows, tokens), jnp.float32),
-            pltpu.VMEM((len(pieces), *pieces[0].shape), jnp.bfloat16),
-            pltpu.SemaphoreType.DMA((len(pieces),)),
-        ],
-        compiler_params=pltpu.CompilerParams(vmem_limit_bytes=20 * MEGA),
-        cost_estimate=pl.CostEstimate(
-            flops=16 * LANES * scored,
-            transcendentals=scored,
-            bytes_accessed=4 * (tokens * local_width + queries.size),
-        ),
-    )(queries, *pieces, *state)
-
-
-def finish_kernel(base_ref, mix_ref, weight_ref, out_ref):
-    out_ref[...] = (
-        base_ref[...] + jnp.dot(mix_ref[...], weight_ref[...], preferred_element_type=jnp.float32)
-    ).astype(jnp.bfloat16)
-
-
-def finish(base, mix, weight):
+        cross_kernel,
+        out_shape=[jax.ShapeDtypeStruct((rows // 2, local_width), jnp.bfloat16)] * 4,
+        in_specs=[pl.BlockSpec(memory_space=pltpu.SMEM)] + [block] * (2 + len(pieces)),
+        out_specs=[block] * 4,
+        scratch_shapes=[pltpu.VMEM((2, rows, tokens), jnp.float32)],
+        compiler_params=pltpu.CompilerParams(vmem_limit_bytes=28 * MEGA),
+    )(chip, *queries, *pieces)
+
+
+def finish_kernel(base_ref, *refs):
+    mix_refs, weight_refs, out_ref = refs[:3], refs[3:6], refs[6]
+    total = base_ref[...]
+    for mix_ref, weight_ref in zip(mix_refs, weight_refs):
+        total = total + jnp.dot(mix_ref[...], weight_ref[...], preferred_element_type=jnp.float32)
+    out_ref[...] = total.astype(jnp.bfloat16)
+
+
+def finish(base, mixes, weights):
+    operands = (base, *mixes, *weights)
     return pl.pallas_call(
         finish_kernel,
         out_shape=jax.ShapeDtypeStruct(base.shape, jnp.bfloat16),
-        grid=(1,),
-        in_specs=[whole(base), whole(mix), whole(weight)],
-        out_specs=whole(base),
-        compiler_params=pltpu.CompilerParams(vmem_limit_bytes=8 * MEGA),
-    )(base, mix, weight)
+        in_specs=[pl.BlockSpec(memory_space=pltpu.VMEM)] * len(operands),
+        out_specs=pl.BlockSpec(memory_space=pltpu.VMEM),
+        compiler_params=pltpu.CompilerParams(vmem_limit_bytes=12 * MEGA),
+    )(*operands)
 
 
 def swap(array, pairs):
@@ -687,6 +634,13 @@
 
 def across(array, pairs):
     return lax.ppermute(array, "seq", pairs)
+
+
+def spread_out(blobs):
+    count = len(blobs)
+    return [blobs[0]] + [
+        across(blobs[step], [(i, i ^ step) for i in range(count)]) for step in range(1, count)
+    ]
 
 
 def by_head(
@@ -702,6 +656,7 @@
     cross_out_weight,
 ):
     model_index = lax.axis_index("mp").astype(jnp.int32)
+    seq = lax.axis_index("seq").astype(jnp.int32).reshape(1)
     core = (model_index % 2).reshape(1)
     chip = (model_index // 2).reshape(1)
     row_count, width = voxels.shape
@@ -715,8 +670,9 @@
     ]
     own_piece = jnp.concatenate(cond_pair, axis=1)
     voxels, own_piece = lax.optimization_barrier((voxels, own_piece))
-    sent, ranks = project(
+    *sent, ranks = project(
         core,
+        seq,
         voxels,
         norm_gain.reshape(1, width),
         destination.reshape(row_count // LANES, LANES),
@@ -724,25 +680,39 @@
         other_qkv,
     )
 
-    mine = lax.all_to_all(sent, "seq", split_axis=0, concat_axis=0, tiled=True)
-    theirs = swap(mine, CORE_SWAP)
-    side_piece = across(own_piece, SIDE_SWAP)
-    next_piece = across(own_piece, NEXT_SWAP)
-    chip_self = swap(self_out_weight, CHIP_SWAP)
-    late_piece, _ = lax.optimization_barrier((own_piece, mine))
+    mine = spread_out(sent)
+    theirs = [swap(blob, CORE_SWAP) for blob in mine]
+    late_piece, *mine = lax.optimization_barrier((own_piece, *mine))
+    side_piece = across(late_piece, SIDE_SWAP)
+    next_piece = across(late_piece, NEXT_SWAP)
     skip_piece = across(late_piece, SKIP_SWAP)
-    mixed = window_mixing(core, mine, theirs, share)
-    mixed, side_piece, next_piece, skip_piece, chip_self = lax.optimization_barrier(
-        (mixed, side_piece, next_piece, skip_piece, chip_self)
+    mixed = window_mixing(core, seq, mine, theirs, share)
+    mixed, side_piece, next_piece, skip_piece = lax.optimization_barrier(
+        (mixed, side_piece, next_piece, skip_piece)
     )
 
     near = lax.all_to_all(mixed, "seq", split_axis=0, concat_axis=0, tiled=True)
     last_piece = across(skip_piece, NEXT_SWAP)
-    next_side_piece = across(next_piece, SIDE_SWAP)
     skip_side_piece = across(skip_piece, SIDE_SWAP)
-    chip_cross = swap(cross_out_weight, CHIP_SWAP)
+    chip_self = swap(self_out_weight, CHIP_SWAP)
     far = swap(near, CHIP_SWAP)
     near_other = swap(near, CORE_SWAP)
+    far, last_piece, skip_side_piece, chip_self = lax.optimization_barrier(
+        (far, last_piece, skip_side_piece, chip_self)
+    )
+    last_side_piece = across(last_piece, SIDE_SWAP)
+    next_side_piece = across(side_piece, NEXT_SWAP)
+    far_other = swap(far, CORE_SWAP)
+    pieces = [
+        own_piece,
+        side_piece,
+        next_piece,
+        next_side_piece,
+        skip_piece,
+        skip_side_piece,
+        last_piece,
+        last_side_piece,
+    ]
     base, order, token = near_part(
         core,
         ranks,
@@ -750,11 +720,6 @@
         (near, near_other),
         (self_out_weight, swap(self_out_weight, CORE_SWAP)),
     )
-    far, last_piece, next_side_piece, chip_cross, _ = lax.optimization_barrier(
-        (far, last_piece, next_side_piece, chip_cross, token)
-    )
-    last_side_piece = across(last_piece, SIDE_SWAP)
-    far_other = swap(far, CORE_SWAP)
     own_hidden, own_query, other_query = far_part(
         core,
         chip,
@@ -767,38 +732,14 @@
     )
 
     asked = swap(other_query, CORE_SWAP)
-    early = (own_piece, side_piece, next_piece, skip_piece)
-    own_state = cross_mixing(own_query, early)
-    asked, skip_side_piece, *own_state = lax.optimization_barrier(
-        (asked, skip_side_piece, *own_state)
-    )
-    asked_state = cross_mixing(asked, early)
-    last_side_piece, *asked_state = lax.optimization_barrier((last_side_piece, *asked_state))
-    late = (next_side_piece, skip_side_piece, last_piece, last_side_piece)
-    answered = swap(cross_mixing(asked, late, tuple(asked_state)), CORE_SWAP)
-
-    def halved(mix):
-        halves = mix.reshape(2, share, mix.shape[1])
-        return (
-            lax.dynamic_index_in_dim(halves, at, 0, keepdims=False) for at in (chip[0], 1 - chip[0])
-        )
-
-    other_kept, other_leaving = halved(answered)
-    other_arrived = swap(other_leaving, CHIP_SWAP)
-    own_mix = cross_mixing(own_query, late, tuple(own_state))
-    own_mix, other_arrived, other_kept = lax.optimization_barrier(
-        (own_mix, other_arrived, other_kept)
-    )
-    own_kept, own_leaving = halved(own_mix)
-    own_arrived = swap(own_leaving, CHIP_SWAP)
-    crossed = own_hidden
-    for part, weight in (
-        (other_kept, swap(cross_out_weight, CORE_SWAP)),
-        (other_arrived, swap(chip_cross, CORE_SWAP)),
-        (own_kept, cross_out_weight),
-    ):
-        crossed = crossed + jnp.dot(part, weight, preferred_element_type=jnp.float32)
-    return finish(crossed, own_arrived, chip_cross)
+    late_weight, own_query = lax.optimization_barrier((cross_out_weight, own_query))
+    chip_cross = swap(late_weight, CHIP_SWAP)
+    kept, to_chip, to_core, to_both = cross_mixing(chip, (own_query, asked), pieces)
+    kept, chip_cross = lax.optimization_barrier((kept, chip_cross))
+    weights = (chip_cross, swap(chip_cross, CORE_SWAP), swap(cross_out_weight, CORE_SWAP))
+    mixes = (swap(to_chip, CHIP_SWAP), swap(to_both, BOTH_SWAP), swap(to_core, CORE_SWAP))
+    base = own_hidden + jnp.dot(kept, cross_out_weight, preferred_element_type=jnp.float32)
+    return finish(base, mixes, weights)
 
 
 def rms_norm(matrix, gain):

time: 153 us -> 143 us (0.935)
  blocking collectives: 36.7 us -> 0 us
  starting transfers between devices: 18.3 us -> 44.9 us
  waiting for transfers between devices: 24.8 us -> 39 us
  Pallas kernels: 56.6 us -> 50.6 us
  local copies, waits for them, and re-layouts: 10.8 us -> 5.19 us
  matrix products: 4.9 us -> 2.27 us
    all_to_all x1 -> x0, blocking collectives: 36.7 us -> none  [by_head(): mine = lax.all_to_all(sent, 'seq', split_axis=0, concat_axis=0, tiled=True)]
    ppermute x7 -> x14, starting transfers between devices: 8.66 us -> 27.7 us  [across(): return lax.ppermute(array, 'seq', pairs)]
    ppermute x7 -> x14, waiting for transfers between devices: 10.8 us -> 23.5 us  [across(): return lax.ppermute(array, 'seq', pairs)]
    pallas_call x5 -> x2, Pallas kernels: 29.3 us -> 23.6 us  [the longest x1 18.1 us: cross_mixing(): pl.pallas_call(cross_kernel, out_shape=[jax.ShapeDtypeStruct((rows // 2,...]
    unnamed x52 -> x32, local copies, waits for them, and re-layouts: 9.87 us -> 5.19 us
    ppermute x16 -> x23, starting transfers between devices: 5.95 us -> 10.2 us  [swap(): return lax.ppermute(array, 'mp', pairs)]
    all_to_all x1, starting transfers between devices: 3.65 us -> 7.04 us  [by_head(): near = lax.all_to_all(mixed, 'seq', split_axis=0, concat_axis=0, tiled=True)]
    dot_general x3 -> x1, matrix products: 2.89 us -> 0.27 us  [by_head(): jnp.dot(kept, cross_out_weight, preferred_element_type=jnp.float32)]
  transfers between devices with their start and end apart: 24 -> 38, of which waited for: 10 -> 13; matrix products, arithmetic and copies ran while one was open for 4% -> 2% of each run, Pallas kernels for 29% -> 31%
where the time goes in v5:
time: 143 us; the launch traced here: 142 us
  Pallas kernels  50.6 us (35%)
  starting transfers between devices  44.9 us (31%)
  waiting for transfers between devices  39 us (27%)
  local copies, waits for them, and re-layouts  5.19 us (4%)
  matrix products  2.27 us (2%)
    ppermute x14, starting transfers between devices, across(): return lax.ppermute(array, 'seq', pairs)  27.7 us
    ppermute x14, waiting for transfers between devices, across(): return lax.ppermute(array, 'seq', pairs)  23.5 us
    pallas_call x1, Pallas kernels, cross_mixing(): pl.pallas_call(cross_kernel, out_shape=[jax.ShapeDtypeStruct((rows // 2,...  18.1 us
    pallas_call x1, Pallas kernels, window_mixing(): pl.pallas_call(window_kernel, out_shape=jax.ShapeDtypeStruct((sources, pa...  17.9 us
    ppermute x23, starting transfers between devices, swap(): return lax.ppermute(array, 'mp', pairs)  10.2 us
    ppermute x23, waiting for transfers between devices, swap(): return lax.ppermute(array, 'mp', pairs)  8.78 us
    all_to_all x1, starting transfers between devices, by_head(): near = lax.all_to_all(mixed, 'seq', split_axis=0, concat_axis=0, tiled=True)  7.04 us
    all_to_all x1, waiting for transfers between devices, by_head(): near = lax.all_to_all(mixed, 'seq', split_axis=0, concat_axis=0, tiled=True)  6.82 us
  transfers between devices with their start and end apart: 38, of which 13 were waited for; matrix products, arithmetic and copies ran while one was open for 2% of the time, Pallas kernels for 31%

profile of v5, /device:TPU:0, one launch (start us, length us, event | category | flops | bytes accessed | tf_op | source)
XLA Modules:
  0.0 142.5 jit_solution(16872966813768318289)
XLA Ops:
  5.6 5.6 %shard_map.100 = (bf16[592,128]{1,0:T(8,128)(2,1)S(1)}, bf16[592,128]{1,0:T(8,128)(2,1)S(1)}, bf16[592,128]{1,0:T(8,128)(2,1)S(1)}, bf16[592,128]{1,0:T(8,128)(2...) custom-call(s32[1]{0:T(128)} %bitcast.core_ref, ...), custom_call_target="tpu_custom_call" | custom-call | tf_op jit(solution)/shard_map/pallas_call | solution.py:159
  11.2 3.0 %collective-permute-start.1 = (bf16[592,128]{1,0:T(8,128)(2,1)S(1)}, bf16[592,128]{1,0:T(8,128)(2,1)S(1)}, u32[]{:S(2)}, u32[]{:S(2)}) collective-permute-start(bf16[592,128]{1,0:T(8,128)(2,1)S(1)} %get-tuple-element.50), channel_id=1, source_target_pairs={{0,4},{4,0},{8,12},{12,8},{16,20},{20,16},{24,28},{28,24},{1,5},{5... | collective-permute-start | bytes 454664 | tf_op jit(solution)/shard_map/ppermute | solution.py:636
  14.2 1.6 %collective-permute-start.2 = (bf16[592,128]{1,0:T(8,128)(2,1)S(1)}, bf16[592,128]{1,0:T(8,128)(2,1)S(1)}, u32[]{:S(2)}, u32[]{:S(2)}) collective-permute-start(bf16[592,128]{1,0:T(8,128)(2,1)S(1)} %get-tuple-element.51), channel_id=1, source_target_pairs={{0,8},{4,12},{8,0},{12,4},{16,24},{20,28},{24,16},{28,20},{1,9},{5... | collective-permute-start | bytes 454664 | tf_op jit(solution)/shard_map/ppermute | solution.py:636
  15.8 3.0 %collective-permute-start.4 = (bf16[592,128]{1,0:T(8,128)(2,1)S(1)}, bf16[592,128]{1,0:T(8,128)(2,1)S(1)}, u32[]{:S(2)}, u32[]{:S(2)}) collective-permute-start(bf16[592,128]{1,0:T(8,128)(2,1)S(1)} %get-tuple-element.53), channel_id=1, source_target_pairs={{0,16},{4,20},{8,24},{12,28},{16,0},{20,4},{24,8},{28,12},{1,17},{... | collective-permute-start | bytes 454664 | tf_op jit(solution)/shard_map/ppermute | solution.py:636
  20.1 3.6 %collective-permute-start.6 = (bf16[592,128]{1,0:T(8,128)(2,1)S(1)}, bf16[592,128]{1,0:T(8,128)(2,1)S(1)}, u32[]{:S(2)}, u32[]{:S(2)}) collective-permute-start(bf16[592,128]{1,0:T(8,128)(2,1)S(1)} %get-tuple-element.55), channel_id=1, source_target_pairs={{0,24},{4,28},{8,16},{12,20},{16,8},{20,12},{24,0},{28,4},{1,25},{... | collective-permute-start | bytes 454664 | tf_op jit(solution)/shard_map/ppermute | solution.py:636
  23.7 2.8 %collective-permute-done.2.refs_2_ = bf16[592,128]{1,0:T(8,128)(2,1)S(1)} collective-permute-done((bf16[592,128]{1,0:T(8,128)(2,1)S(1)}, bf16[592,128]{1,0:T(8,128)(2,1)S(1)}, u32[]{:S(2)}, u32[]{:S(2)}) %collective-permute-start.2) | collective-permute-done | bytes 151584 | tf_op jit(solution)/shard_map/ppermute | solution.py:636
  28.1 12.7 %collective-permute-done.5.refs_5_ = bf16[592,128]{1,0:T(8,128)(2,1)S(1)} collective-permute-done((bf16[592,128]{1,0:T(8,128)(2,1)S(1)}, bf16[592,128]{1,0:T(8,128)(2,1)S(1)}, u32[]{:S(2)}, u32[]{:S(2)}) %collective-permute-start.5) | collective-permute-done | bytes 151584 | tf_op jit(solution)/shard_map/ppermute | solution.py:636
  43.2 4.9 %collective-permute-start.17 = (bf16[512,512]{1,0:T(8,128)(2,1)S(1)}, bf16[512,512]{1,0:T(8,128)(2,1)S(1)}, u32[]{:S(2)}, u32[]{:S(2)}) collective-permute-start(bf16[512,512]{1,0:T(8,128)(2,1)S(1)} %pad_maximum_fusion.refs_2_), channel_id=1, source_target_pairs={{0,8},{4,12},{8,0},{12,4},{16,24},{20,28},{24,16},{28,20},{1,9},{5... | collective-permute-start | bytes 1572872 | tf_op jit(solution)/shard_map/ppermute | solution.py:636
  48.0 2.0 %collective-permute-start.18 = (bf16[512,512]{1,0:T(8,128)(2,1)S(1)}, bf16[512,512]{1,0:T(8,128)(2,1)}, u32[]{:S(2)}, u32[]{:S(2)}) collective-permute-start(bf16[512,512]{1,0:T(8,128)(2,1)S(1)} %pad_maximum_fusion.refs_2_), channel_id=1, source_target_pairs={{0,16},{4,20},{8,24},{12,28},{16,0},{20,4},{24,8},{28,12},{1,17},{... | collective-permute-start | bytes 1572872 | tf_op jit(solution)/shard_map/ppermute | solution.py:636
  50.0 17.9 %shard_map.101 = bf16[8,192,128]{2,1,0:T(8,128)(2,1)S(1)} custom-call(s32[1]{0:T(128)} %bitcast.core_ref, s32[1]{0:T(128)} %bitcast.2.seq_ref, bf16[592,128]{1,0:T(8,128)(2,1)S(1)} %get-tuple-element.57.refs_0_, bf16[592,128]{1,0:T(8,128)(2,1)S(1)} %collective-permute-done.1.refs_1_, bf16[592,128]{1,0:T(8,128)(2,1)S(1)} %collective-permute-done.2.refs_2_, ...), custom_call_target="tpu_custom_call" | custom-call | flops 24159191040 | bytes 2424832 | tf_op jit(solution)/shard_map/pallas_call | solution.py:336
  68.7 2.7 %collective-permute-done.17.refs_4_ = bf16[512,512]{1,0:T(8,128)(2,1)S(1)} collective-permute-done((bf16[512,512]{1,0:T(8,128)(2,1)S(1)}, bf16[512,512]{1,0:T(8,128)(2,1)S(1)}, u32[]{:S(2)}, u32[]{:S(2)}) %collective-permute-start.17) | collective-permute-done | bytes 524320 | tf_op jit(solution)/shard_map/ppermute | solution.py:636
  72.2 7.0 %all-to-all-start = ((bf16[8,192,128]{2,1,0:T(8,128)(2,1)}), bf16[8,192,128]{2,1,0:T(8,128)(2,1)S(1)}, u32[]{:S(2)}, u32[]{:S(2)}) async-start(bf16[8,192,128]{2,1,0:T(8,128)(2,1)} %copy-done.8), calls=%async_computation | async-start | bytes 786432 | tf_op jit(solution)/shard_map/all_to_all | solution.py:694
  80.8 2.0 %collective-permute-start.22 = (bf16[512,512]{1,0:T(8,128)(2,1)}, bf16[512,512]{1,0:T(8,128)(2,1)}, u32[]{:S(2)}, u32[]{:S(2)}) collective-permute-start(bf16[512,512]{1,0:T(8,128)(2,1)} %collective-permute-done.18.refs_6_), channel_id=1, source_target_pairs={{0,8},{4,12},{8,0},{12,4},{16,24},{20,28},{24,16},{28,20},{1,9},{5... | collective-permute-start | bytes 1572872 | tf_op jit(solution)/shard_map/ppermute | solution.py:636
  84.2 6.8 %all-to-all-done.own_ref = bf16[8,192,128]{2,1,0:T(8,128)(2,1)S(1)} async-done(((bf16[8,192,128]{2,1,0:T(8,128)(2,1)}), bf16[8,192,128]{2,1,0:T(8,128)(2,1)S(1)}, u32[]{:S(2)}, u32[]{:S(2)}) %all-to-all-start) | async-done | bytes 393248 | tf_op jit(solution)/shard_map/all_to_all | solution.py:694
  92.6 1.8 %collective-permute-done.24.weight_ref = bf16[256,1024]{1,0:T(8,128)(2,1)} collective-permute-done((bf16[256,1024]{1,0:T(8,128)(2,1)}, bf16[256,1024]{1,0:T(8,128)(2,1)}, u32[]{:S(2)}, u32[]{:S(2)}) %collective-permute-start.24) | collective-permute-done | bytes 524320 | tf_op jit(solution)/shard_map/ppermute | solution.py:632
  94.4 3.9 %collective-permute-done.22.refs_8_ = bf16[512,512]{1,0:T(8,128)(2,1)} collective-permute-done((bf16[512,512]{1,0:T(8,128)(2,1)}, bf16[512,512]{1,0:T(8,128)(2,1)}, u32[]{:S(2)}, u32[]{:S(2)}) %collective-permute-start.22) | collective-permute-done | bytes 524320 | tf_op jit(solution)/shard_map/ppermute | solution.py:636
  98.3 1.9 %collective-permute-done.21.own_ref = bf16[8,192,128]{2,1,0:T(8,128)(2,1)} collective-permute-done((bf16[8,192,128]{2,1,0:T(8,128)(2,1)S(1)}, bf16[8,192,128]{2,1,0:T(8,128)(2,1)}, u32[]{:S(2)}, u32[]{:S(2)}) %collective-permute-start.21) | collective-permute-done | bytes 393248 | tf_op jit(solution)/shard_map/ppermute | solution.py:632
  100.7 1.7 %collective-permute-start.29 = (bf16[512,512]{1,0:T(8,128)(2,1)}, bf16[512,512]{1,0:T(8,128)(2,1)S(1)}, u32[]{:S(2)}, u32[]{:S(2)}) collective-permute-start(bf16[512,512]{1,0:T(8,128)(2,1)} %copy-done.4), channel_id=1, source_target_pairs={{0,8},{4,12},{8,0},{12,4},{16,24},{20,28},{24,16},{28,20},{1,9},{5... | collective-permute-start | bytes 1572872 | tf_op jit(solution)/shard_map/ppermute | solution.py:636
  104.9 3.4 %shard_map.102 = (f32[384,1024]{1,0:T(8,128)S(1)}, bf16[384,768]{1,0:T(8,128)(2,1)S(1)}, f32[8,128]{1,0:T(8,128)}) custom-call(s32[1]{0:T(128)} %bitcast.core_ref, f32[8,128]{1,0:T(8,128)S(1)} %get-tuple-element.47.rank_ref, bf16[768,1024]{1,0:T(8,128)(2,1)S(1)} %copy-done.3, bf16[8,192,128]{2,1,0:T(8,128)(2,1)S(1)} %all-to-all-done.own_ref, ...), custom_call_target="tpu_custom_call" | custom-call | flops 4026531840 | bytes 8388608 | tf_op jit(solution)/shard_map/pallas_call | solution.py:495
  108.4 4.4 %shard_map.103 = (f32[192,1024]{1,0:T(8,128)S(1)}, bf16[384,256]{1,0:T(8,128)(2,1)S(1)}, bf16[384,256]{1,0:T(8,128)(2,1)S(1)}) custom-call(s32[1]{0:T(128)} %bitcast.core_ref, s32[1]{0:T(128)} %bitcast.1.chip_ref, f32[384,1024]{1,0:T(8,128)S(1)} %get-tuple-element.67.base_ref, bf16[384,768]{1,0:T(8,128)(2,1)S(1)} %get-tuple-element.68.order_ref, ...), custom_call_target="tpu_custom_call" | custom-call | flops 4026531840 | bytes 8388608 | tf_op jit(solution)/shard_map/pallas_call | solution.py:526
  112.8 1.6 %collective-permute-start.31 = (bf16[256,1024]{1,0:T(8,128)(2,1)S(1)}, bf16[256,1024]{1,0:T(8,128)(2,1)S(1)}, u32[]{:S(2)}, u32[]{:S(2)}) collective-permute-start(bf16[256,1024]{1,0:T(8,128)(2,1)S(1)} %copy-done.14), channel_id=1, source_target_pairs={{0,2},{2,0},{1,3},{3,1},{4,6},{6,4},{5,7},{7,5},{8,10},{10,8},{9,1... | collective-permute-start | bytes 1572872 | tf_op jit(solution)/shard_map/ppermute | solution.py:632
  116.2 18.1 %shard_map.104 = (bf16[192,256]{1,0:T(8,128)(2,1)S(1)}, bf16[192,256]{1,0:T(8,128)(2,1)S(1)}, bf16[192,256]{1,0:T(8,128)(2,1)S(1)}, bf16[192,256]{1,0:T(8,128)(2,1)S(1)}) custom-call(s32[1]{0:T(128)} %bitcast.1.chip_ref, bf16[384,256]{1,0:T(8,128)(2,1)S(1)} %get-tuple-element.74.refs_0_, bf16[384,256]{1,0:T(8,128)(2,1)S(1)} %collective-permute-done.28.refs_1_, ...), custom_call_target="tpu_custom_call" | custom-call | tf_op jit(solution)/shard_map/pallas_call | solution.py:602
  134.3 1.6 %collective-permute-start.32 = (bf16[192,256]{1,0:T(8,128)(2,1)S(1)}, bf16[192,256]{1,0:T(8,128)(2,1)S(1)}, u32[]{:S(2)}, u32[]{:S(2)}) collective-permute-start(bf16[192,256]{1,0:T(8,128)(2,1)S(1)} %get-tuple-element.83), channel_id=1, source_target_pairs={{0,2},{2,0},{1,3},{3,1},{4,6},{6,4},{5,7},{7,5},{8,10},{10,8},{9,1... | collective-permute-start | bytes 294920 | tf_op jit(solution)/shard_map/ppermute | solution.py:632
  136.9 3.1 %collective-permute-done.32.refs_0_ = bf16[192,256]{1,0:T(8,128)(2,1)S(1)} collective-permute-done((bf16[192,256]{1,0:T(8,128)(2,1)S(1)}, bf16[192,256]{1,0:T(8,128)(2,1)S(1)}, u32[]{:S(2)}, u32[]{:S(2)}) %collective-permute-start.32) | collective-permute-done | bytes 98336 | tf_op jit(solution)/shard_map/ppermute | solution.py:632
  (95 shorter events, 25.2 us)
Async XLA Ops:
  11.2 8.9 %collective-permute-start.1 = (bf16[592,128]{1,0:T(8,128)(2,1)S(1)}, bf16[592,128]{1,0:T(8,128)(2,1)S(1)}, u32[]{:S(2)}, u32[]{:S(2)}) collective-permute-start(bf16[592,128]{1,0:T(8,128)(2,1)S(1)} %get-tuple-element.50), channel_id=1, source_target_pairs={{0,4},{4,0},{8,12},{12,8},{16,20},{20,16},{24,28},{28,24},{1,5},{5... | collective-permute-start | bytes 454664 | tf_op jit(solution)/shard_map/ppermute | solution.py:636
  14.2 12.3 %collective-permute-start.2 = (bf16[592,128]{1,0:T(8,128)(2,1)S(1)}, bf16[592,128]{1,0:T(8,128)(2,1)S(1)}, u32[]{:S(2)}, u32[]{:S(2)}) collective-permute-start(bf16[592,128]{1,0:T(8,128)(2,1)S(1)} %get-tuple-element.51), channel_id=1, source_target_pairs={{0,8},{4,12},{8,0},{12,4},{16,24},{20,28},{24,16},{28,20},{1,9},{5... | collective-permute-start | bytes 454664 | tf_op jit(solution)/shard_map/ppermute | solution.py:636
  15.8 11.8 %collective-permute-start.3 = (bf16[592,128]{1,0:T(8,128)(2,1)S(1)}, bf16[592,128]{1,0:T(8,128)(2,1)S(1)}, u32[]{:S(2)}, u32[]{:S(2)}) collective-permute-start(bf16[592,128]{1,0:T(8,128)(2,1)S(1)} %get-tuple-element.52), channel_id=1, source_target_pairs={{0,12},{4,8},{8,4},{12,0},{16,28},{20,24},{24,20},{28,16},{1,13},{... | collective-permute-start | bytes 454664 | tf_op jit(solution)/shard_map/ppermute | solution.py:636
  15.8 11.8 %collective-permute-start.4 = (bf16[592,128]{1,0:T(8,128)(2,1)S(1)}, bf16[592,128]{1,0:T(8,128)(2,1)S(1)}, u32[]{:S(2)}, u32[]{:S(2)}) collective-permute-start(bf16[592,128]{1,0:T(8,128)(2,1)S(1)} %get-tuple-element.53), channel_id=1, source_target_pairs={{0,16},{4,20},{8,24},{12,28},{16,0},{20,4},{24,8},{28,12},{1,17},{... | collective-permute-start | bytes 454664 | tf_op jit(solution)/shard_map/ppermute | solution.py:636
  18.8 22.0 %collective-permute-start.5 = (bf16[592,128]{1,0:T(8,128)(2,1)S(1)}, bf16[592,128]{1,0:T(8,128)(2,1)S(1)}, u32[]{:S(2)}, u32[]{:S(2)}) collective-permute-start(bf16[592,128]{1,0:T(8,128)(2,1)S(1)} %get-tuple-element.54), channel_id=1, source_target_pairs={{0,20},{4,16},{8,28},{12,24},{16,4},{20,0},{24,12},{28,8},{1,21},{... | collective-permute-start | bytes 454664 | tf_op jit(solution)/shard_map/ppermute | solution.py:636
  20.1 20.7 %collective-permute-start.6 = (bf16[592,128]{1,0:T(8,128)(2,1)S(1)}, bf16[592,128]{1,0:T(8,128)(2,1)S(1)}, u32[]{:S(2)}, u32[]{:S(2)}) collective-permute-start(bf16[592,128]{1,0:T(8,128)(2,1)S(1)} %get-tuple-element.55), channel_id=1, source_target_pairs={{0,24},{4,28},{8,16},{12,20},{16,8},{20,12},{24,0},{28,4},{1,25},{... | collective-permute-start | bytes 454664 | tf_op jit(solution)/shard_map/ppermute | solution.py:636
  26.5 14.8 %collective-permute-start.7 = (bf16[592,128]{1,0:T(8,128)(2,1)S(1)}, bf16[592,128]{1,0:T(8,128)(2,1)S(1)}, u32[]{:S(2)}, u32[]{:S(2)}) collective-permute-start(bf16[592,128]{1,0:T(8,128)(2,1)S(1)} %get-tuple-element.56), channel_id=1, source_target_pairs={{0,28},{4,24},{8,20},{12,16},{16,12},{20,8},{24,4},{28,0},{1,29},{... | collective-permute-start | bytes 454664 | tf_op jit(solution)/shard_map/ppermute | solution.py:636
  27.6 13.8 %collective-permute-start.8 = (bf16[592,128]{1,0:T(8,128)(2,1)S(1)}, bf16[592,128]{1,0:T(8,128)(2,1)S(1)}, u32[]{:S(2)}, u32[]{:S(2)}) collective-permute-start(bf16[592,128]{1,0:T(8,128)(2,1)S(1)} %get-tuple-element.57.refs_0_), channel_id=1, source_target_pairs={{0,1},{1,0},{2,3},{3,2},{4,5},{5,4},{6,7},{7,6},{8,9},{9,8},{10,11... | collective-permute-start | bytes 454664 | tf_op jit(solution)/shard_map/ppermute | solution.py:632
  27.6 14.2 %collective-permute-start.10 = (bf16[592,128]{1,0:T(8,128)(2,1)S(1)}, bf16[592,128]{1,0:T(8,128)(2,1)S(1)}, u32[]{:S(2)}, u32[]{:S(2)}) collective-permute-start(bf16[592,128]{1,0:T(8,128)(2,1)S(1)} %collective-permute-done.2.refs_2_), channel_id=1, source_target_pairs={{0,1},{1,0},{2,3},{3,2},{4,5},{5,4},{6,7},{7,6},{8,9},{9,8},{10,11... | collective-permute-start | bytes 454664 | tf_op jit(solution)/shard_map/ppermute | solution.py:632
  42.4 26.3 %collective-permute-start.16 = (bf16[512,512]{1,0:T(8,128)(2,1)S(1)}, bf16[512,512]{1,0:T(8,128)(2,1)S(1)}, u32[]{:S(2)}, u32[]{:S(2)}) collective-permute-start(bf16[512,512]{1,0:T(8,128)(2,1)S(1)} %pad_maximum_fusion.refs_2_), channel_id=1, source_target_pairs={{0,4},{4,0},{8,12},{12,8},{16,20},{20,16},{24,28},{28,24},{1,5},{5... | collective-permute-start | bytes 1572872 | tf_op jit(solution)/shard_map/ppermute | solution.py:636
  43.2 28.2 %collective-permute-start.17 = (bf16[512,512]{1,0:T(8,128)(2,1)S(1)}, bf16[512,512]{1,0:T(8,128)(2,1)S(1)}, u32[]{:S(2)}, u32[]{:S(2)}) collective-permute-start(bf16[512,512]{1,0:T(8,128)(2,1)S(1)} %pad_maximum_fusion.refs_2_), channel_id=1, source_target_pairs={{0,8},{4,12},{8,0},{12,4},{16,24},{20,28},{24,16},{28,20},{1,9},{5... | collective-permute-start | bytes 1572872 | tf_op jit(solution)/shard_map/ppermute | solution.py:636
  48.0 24.1 %collective-permute-start.18 = (bf16[512,512]{1,0:T(8,128)(2,1)S(1)}, bf16[512,512]{1,0:T(8,128)(2,1)}, u32[]{:S(2)}, u32[]{:S(2)}) collective-permute-start(bf16[512,512]{1,0:T(8,128)(2,1)S(1)} %pad_maximum_fusion.refs_2_), channel_id=1, source_target_pairs={{0,16},{4,20},{8,24},{12,28},{16,0},{20,4},{24,8},{28,12},{1,17},{... | collective-permute-start | bytes 1572872 | tf_op jit(solution)/shard_map/ppermute | solution.py:636
  72.2 18.9 %all-to-all-start = ((bf16[8,192,128]{2,1,0:T(8,128)(2,1)}), bf16[8,192,128]{2,1,0:T(8,128)(2,1)S(1)}, u32[]{:S(2)}, u32[]{:S(2)}) async-start(bf16[8,192,128]{2,1,0:T(8,128)(2,1)} %copy-done.8), calls=%async_computation | async-start | bytes 786432 | tf_op jit(solution)/shard_map/all_to_all | solution.py:694
  79.2 15.2 %collective-permute-start.24 = (bf16[256,1024]{1,0:T(8,128)(2,1)}, bf16[256,1024]{1,0:T(8,128)(2,1)}, u32[]{:S(2)}, u32[]{:S(2)}) collective-permute-start(bf16[256,1024]{1,0:T(8,128)(2,1)} %weight_ref.1), channel_id=1, source_target_pairs={{0,2},{2,0},{1,3},{3,1},{4,6},{6,4},{5,7},{7,5},{8,10},{10,8},{9,1... | collective-permute-start | bytes 1572872 | tf_op jit(solution)/shard_map/ppermute | solution.py:632
  80.8 17.5 %collective-permute-start.22 = (bf16[512,512]{1,0:T(8,128)(2,1)}, bf16[512,512]{1,0:T(8,128)(2,1)}, u32[]{:S(2)}, u32[]{:S(2)}) collective-permute-start(bf16[512,512]{1,0:T(8,128)(2,1)} %collective-permute-done.18.refs_6_), channel_id=1, source_target_pairs={{0,8},{4,12},{8,0},{12,4},{16,24},{20,28},{24,16},{28,20},{1,9},{5... | collective-permute-start | bytes 1572872 | tf_op jit(solution)/shard_map/ppermute | solution.py:636
  82.8 15.5 %collective-permute-start.23 = (bf16[512,512]{1,0:T(8,128)(2,1)}, bf16[512,512]{1,0:T(8,128)(2,1)}, u32[]{:S(2)}, u32[]{:S(2)}) collective-permute-start(bf16[512,512]{1,0:T(8,128)(2,1)} %collective-permute-done.18.refs_6_), channel_id=1, source_target_pairs={{0,4},{4,0},{8,12},{12,8},{16,20},{20,16},{24,28},{28,24},{1,5},{5... | collective-permute-start | bytes 1572872 | tf_op jit(solution)/shard_map/ppermute | solution.py:636
  91.1 9.1 %collective-permute-start.21 = (bf16[8,192,128]{2,1,0:T(8,128)(2,1)S(1)}, bf16[8,192,128]{2,1,0:T(8,128)(2,1)}, u32[]{:S(2)}, u32[]{:S(2)}) collective-permute-start(bf16[8,192,128]{2,1,0:T(8,128)(2,1)S(1)} %all-to-all-done.own_ref), channel_id=1, source_target_pairs={{0,2},{2,0},{1,3},{3,1},{4,6},{6,4},{5,7},{7,5},{8,10},{10,8},{9,1... | collective-permute-start | bytes 1179656 | tf_op jit(solution)/shard_map/ppermute | solution.py:632
  98.3 10.1 %collective-permute-start.27 = (bf16[1024,256]{1,0:T(8,128)(2,1)}, bf16[1024,256]{1,0:T(8,128)(2,1)}, u32[]{:S(2)}, u32[]{:S(2)}) collective-permute-start(bf16[1024,256]{1,0:T(8,128)(2,1)} %query_weight_ref.1), channel_id=1, source_target_pairs={{0,1},{1,0},{2,3},{3,2},{4,5},{5,4},{6,7},{7,6},{8,9},{9,8},{10,11... | collective-permute-start | bytes 1572872 | tf_op jit(solution)/shard_map/ppermute | solution.py:632
  100.2 8.2 %collective-permute-start.26 = (bf16[256,1024]{1,0:T(8,128)(2,1)}, bf16[256,1024]{1,0:T(8,128)(2,1)}, u32[]{:S(2)}, u32[]{:S(2)}) collective-permute-start(bf16[256,1024]{1,0:T(8,128)(2,1)} %collective-permute-done.24.weight_ref), channel_id=1, source_target_pairs={{0,1},{1,0},{2,3},{3,2},{4,5},{5,4},{6,7},{7,6},{8,9},{9,8},{10,11... | collective-permute-start | bytes 1572872 | tf_op jit(solution)/shard_map/ppermute | solution.py:632
  100.2 8.2 %collective-permute-start.25 = (bf16[8,192,128]{2,1,0:T(8,128)(2,1)}, bf16[8,192,128]{2,1,0:T(8,128)(2,1)}, u32[]{:S(2)}, u32[]{:S(2)}) collective-permute-start(bf16[8,192,128]{2,1,0:T(8,128)(2,1)} %collective-permute-done.21.own_ref), channel_id=1, source_target_pairs={{0,1},{1,0},{2,3},{3,2},{4,5},{5,4},{6,7},{7,6},{8,9},{9,8},{10,11... | collective-permute-start | bytes 1179656 | tf_op jit(solution)/shard_map/ppermute | solution.py:632
  100.7 14.3 %collective-permute-start.29 = (bf16[512,512]{1,0:T(8,128)(2,1)}, bf16[512,512]{1,0:T(8,128)(2,1)S(1)}, u32[]{:S(2)}, u32[]{:S(2)}) collective-permute-start(bf16[512,512]{1,0:T(8,128)(2,1)} %copy-done.4), channel_id=1, source_target_pairs={{0,8},{4,12},{8,0},{12,4},{16,24},{20,28},{24,16},{28,20},{1,9},{5... | collective-permute-start | bytes 1572872 | tf_op jit(solution)/shard_map/ppermute | solution.py:636
  102.4 13.8 %collective-permute-start.30 = (bf16[512,512]{1,0:T(8,128)(2,1)}, bf16[512,512]{1,0:T(8,128)(2,1)S(1)}, u32[]{:S(2)}, u32[]{:S(2)}) collective-permute-start(bf16[512,512]{1,0:T(8,128)(2,1)} %collective-permute-done.22.refs_8_), channel_id=1, source_target_pairs={{0,4},{4,0},{8,12},{12,8},{16,20},{20,16},{24,28},{28,24},{1,5},{5... | collective-permute-start | bytes 1572872 | tf_op jit(solution)/shard_map/ppermute | solution.py:636
  112.8 21.4 %collective-permute-start.31 = (bf16[256,1024]{1,0:T(8,128)(2,1)S(1)}, bf16[256,1024]{1,0:T(8,128)(2,1)S(1)}, u32[]{:S(2)}, u32[]{:S(2)}) collective-permute-start(bf16[256,1024]{1,0:T(8,128)(2,1)S(1)} %copy-done.14), channel_id=1, source_target_pairs={{0,2},{2,0},{1,3},{3,1},{4,6},{6,4},{5,7},{7,5},{8,10},{10,8},{9,1... | collective-permute-start | bytes 1572872 | tf_op jit(solution)/shard_map/ppermute | solution.py:632
  114.4 22.5 %collective-permute-start.36 = (bf16[256,1024]{1,0:T(8,128)(2,1)S(1)}, bf16[256,1024]{1,0:T(8,128)(2,1)S(1)}, u32[]{:S(2)}, u32[]{:S(2)}) collective-permute-start(bf16[256,1024]{1,0:T(8,128)(2,1)S(1)} %copy-done.14), channel_id=1, source_target_pairs={{0,1},{1,0},{2,3},{3,2},{4,5},{5,4},{6,7},{7,6},{8,9},{9,8},{10,11... | collective-permute-start | bytes 1572872 | tf_op jit(solution)/shard_map/ppermute | solution.py:632
  (30 other events, 188.8 us)

commit v6 on v5

--- a/solution.py
+++ b/solution.py
@@ -13,7 +13,7 @@
 LANES = 128
 ID_ROWS = 16
 MEGA = 1024 * 1024
-BATCH = 4
+BATCH = 8
 CORE_SWAP = ((0, 1), (1, 0), (2, 3), (3, 2))
 CHIP_SWAP = ((0, 2), (2, 0), (1, 3), (3, 1))
 BOTH_SWAP = ((0, 3), (3, 0), (1, 2), (2, 1))
@@ -162,7 +162,7 @@
         grid_spec=pltpu.PrefetchScalarGridSpec(
             num_scalar_prefetch=2,
             grid=(2,),
-            in_specs=[pl.BlockSpec(memory_space=pl.ANY)]
+            in_specs=[pl.BlockSpec(memory_space=pltpu.HBM)]
             + [fixed(operand) for operand in operands[1:]],
             out_specs=[fixed(out) for out in outs],
             scratch_shapes=[
@@ -283,7 +283,7 @@
             total_ref[at] = total
         return carry
 
-    lax.fori_loop(0, sources, sweep, 0)
+    lax.fori_loop(0, sources, sweep, 0, unroll=4)
     spare = sources * blocks
     query_ref[spare] = jnp.zeros((LANES, LANES), jnp.bfloat16)
     column_ref[spare] = jnp.zeros((LANES, LANES), jnp.float32)
@@ -304,10 +304,14 @@
         turns = functools.reduce(jnp.maximum, [plan_smem[1, other, at] for other, at in pairs])
 
         def more(turn, carry):
-            for other, at in pairs:
-                sum_ref[at], total_ref[at] = fold(
-                    at, other, turn, query_ref[at], column_ref[at], sum_ref[at], total_ref[at]
-                )
+            nothing = jnp.zeros((LANES, LANES), jnp.float32)
+            parts = [
+                fold(at, other, turn, query_ref[at], column_ref[at], nothing, nothing)
+                for other, at in pairs
+            ]
+            for (other, at), (sums, total) in zip(pairs, parts):
+                sum_ref[at] = sum_ref[at] + sums
+                total_ref[at] = total_ref[at] + total
             return carry
 
         return lax.fori_loop(1, turns, more, carry)
@@ -669,7 +673,7 @@
         for part in range(2)
     ]
     own_piece = jnp.concatenate(cond_pair, axis=1)
-    voxels, own_piece = lax.optimization_barrier((voxels, own_piece))
+    destination, own_piece = lax.optimization_barrier((destination, own_piece))
     *sent, ranks = project(
         core,
         seq,

time: 143 us -> 143 us (level)
  transfers between devices with their start and end apart: 38 -> 38, of which waited for: 13 -> 13; matrix products, arithmetic and copies ran while one was open for 2% -> 2% of each run, Pallas kernels for 31% -> 30%
where the time goes in v6:
time: 143 us; the launch traced here: 142 us
  Pallas kernels  50.1 us (35%)
  starting transfers between devices  44.9 us (31%)
  waiting for transfers between devices  39.5 us (28%)
  local copies, waits for them, and re-layouts  5.19 us (4%)
  matrix products  2.27 us (2%)
    ppermute x14, starting transfers between devices, across(): return lax.ppermute(array, 'seq', pairs)  27.7 us
    ppermute x14, waiting for transfers between devices, across(): return lax.ppermute(array, 'seq', pairs)  23.9 us
    pallas_call x1, Pallas kernels, cross_mixing(): pl.pallas_call(cross_kernel, out_shape=[jax.ShapeDtypeStruct((rows // 2,...  18.1 us
    pallas_call x1, Pallas kernels, window_mixing(): pl.pallas_call(window_kernel, out_shape=jax.ShapeDtypeStruct((sources, pa...  17.4 us
    ppermute x23, starting transfers between devices, swap(): return lax.ppermute(array, 'mp', pairs)  10.2 us
    ppermute x23, waiting for transfers between devices, swap(): return lax.ppermute(array, 'mp', pairs)  8.78 us
    all_to_all x1, starting transfers between devices, by_head(): near = lax.all_to_all(mixed, 'seq', split_axis=0, concat_axis=0, tiled=True)  7.04 us
    all_to_all x1, waiting for transfers between devices, by_head(): near = lax.all_to_all(mixed, 'seq', split_axis=0, concat_axis=0, tiled=True)  6.82 us
  transfers between devices with their start and end apart: 38, of which 13 were waited for; matrix products, arithmetic and copies ran while one was open for 2% of the time, Pallas kernels for 30%

profile of v6, /device:TPU:0, one launch (start us, length us, event | category | flops | bytes accessed | tf_op | source)
XLA Modules:
  0.0 142.5 jit_solution(15126171128637676519)
XLA Ops:
  5.6 5.6 %shard_map.100 = (bf16[592,128]{1,0:T(8,128)(2,1)S(1)}, bf16[592,128]{1,0:T(8,128)(2,1)S(1)}, bf16[592,128]{1,0:T(8,128)(2,1)S(1)}, bf16[592,128]{1,0:T(8,128)(2...) custom-call(s32[1]{0:T(128)} %bitcast.core_ref, ...), custom_call_target="tpu_custom_call" | custom-call | tf_op jit(solution)/shard_map/pallas_call | solution.py:159
  11.2 3.0 %collective-permute-start.1 = (bf16[592,128]{1,0:T(8,128)(2,1)S(1)}, bf16[592,128]{1,0:T(8,128)(2,1)S(1)}, u32[]{:S(2)}, u32[]{:S(2)}) collective-permute-start(bf16[592,128]{1,0:T(8,128)(2,1)S(1)} %get-tuple-element.50), channel_id=1, source_target_pairs={{0,4},{4,0},{8,12},{12,8},{16,20},{20,16},{24,28},{28,24},{1,5},{5... | collective-permute-start | bytes 454664 | tf_op jit(solution)/shard_map/ppermute | solution.py:640
  14.2 1.6 %collective-permute-start.2 = (bf16[592,128]{1,0:T(8,128)(2,1)S(1)}, bf16[592,128]{1,0:T(8,128)(2,1)S(1)}, u32[]{:S(2)}, u32[]{:S(2)}) collective-permute-start(bf16[592,128]{1,0:T(8,128)(2,1)S(1)} %get-tuple-element.51), channel_id=1, source_target_pairs={{0,8},{4,12},{8,0},{12,4},{16,24},{20,28},{24,16},{28,20},{1,9},{5... | collective-permute-start | bytes 454664 | tf_op jit(solution)/shard_map/ppermute | solution.py:640
  15.8 3.0 %collective-permute-start.4 = (bf16[592,128]{1,0:T(8,128)(2,1)S(1)}, bf16[592,128]{1,0:T(8,128)(2,1)S(1)}, u32[]{:S(2)}, u32[]{:S(2)}) collective-permute-start(bf16[592,128]{1,0:T(8,128)(2,1)S(1)} %get-tuple-element.53), channel_id=1, source_target_pairs={{0,16},{4,20},{8,24},{12,28},{16,0},{20,4},{24,8},{28,12},{1,17},{... | collective-permute-start | bytes 454664 | tf_op jit(solution)/shard_map/ppermute | solution.py:640
  20.1 3.6 %collective-permute-start.6 = (bf16[592,128]{1,0:T(8,128)(2,1)S(1)}, bf16[592,128]{1,0:T(8,128)(2,1)S(1)}, u32[]{:S(2)}, u32[]{:S(2)}) collective-permute-start(bf16[592,128]{1,0:T(8,128)(2,1)S(1)} %get-tuple-element.55), channel_id=1, source_target_pairs={{0,24},{4,28},{8,16},{12,20},{16,8},{20,12},{24,0},{28,4},{1,25},{... | collective-permute-start | bytes 454664 | tf_op jit(solution)/shard_map/ppermute | solution.py:640
  23.7 2.8 %collective-permute-done.2.refs_2_ = bf16[592,128]{1,0:T(8,128)(2,1)S(1)} collective-permute-done((bf16[592,128]{1,0:T(8,128)(2,1)S(1)}, bf16[592,128]{1,0:T(8,128)(2,1)S(1)}, u32[]{:S(2)}, u32[]{:S(2)}) %collective-permute-start.2) | collective-permute-done | bytes 151584 | tf_op jit(solution)/shard_map/ppermute | solution.py:640
  28.1 12.7 %collective-permute-done.5.refs_5_ = bf16[592,128]{1,0:T(8,128)(2,1)S(1)} collective-permute-done((bf16[592,128]{1,0:T(8,128)(2,1)S(1)}, bf16[592,128]{1,0:T(8,128)(2,1)S(1)}, u32[]{:S(2)}, u32[]{:S(2)}) %collective-permute-start.5) | collective-permute-done | bytes 151584 | tf_op jit(solution)/shard_map/ppermute | solution.py:640
  43.2 4.9 %collective-permute-start.17 = (bf16[512,512]{1,0:T(8,128)(2,1)S(1)}, bf16[512,512]{1,0:T(8,128)(2,1)S(1)}, u32[]{:S(2)}, u32[]{:S(2)}) collective-permute-start(bf16[512,512]{1,0:T(8,128)(2,1)S(1)} %pad_maximum_fusion.refs_2_), channel_id=1, source_target_pairs={{0,8},{4,12},{8,0},{12,4},{16,24},{20,28},{24,16},{28,20},{1,9},{5... | collective-permute-start | bytes 1572872 | tf_op jit(solution)/shard_map/ppermute | solution.py:640
  48.0 2.0 %collective-permute-start.18 = (bf16[512,512]{1,0:T(8,128)(2,1)S(1)}, bf16[512,512]{1,0:T(8,128)(2,1)}, u32[]{:S(2)}, u32[]{:S(2)}) collective-permute-start(bf16[512,512]{1,0:T(8,128)(2,1)S(1)} %pad_maximum_fusion.refs_2_), channel_id=1, source_target_pairs={{0,16},{4,20},{8,24},{12,28},{16,0},{20,4},{24,8},{28,12},{1,17},{... | collective-permute-start | bytes 1572872 | tf_op jit(solution)/shard_map/ppermute | solution.py:640
  50.0 17.4 %shard_map.101 = bf16[8,192,128]{2,1,0:T(8,128)(2,1)S(1)} custom-call(s32[1]{0:T(128)} %bitcast.core_ref, s32[1]{0:T(128)} %bitcast.2.seq_ref, bf16[592,128]{1,0:T(8,128)(2,1)S(1)} %get-tuple-element.57.refs_0_, bf16[592,128]{1,0:T(8,128)(2,1)S(1)} %collective-permute-done.1.refs_1_, bf16[592,128]{1,0:T(8,128)(2,1)S(1)} %collective-permute-done.2.refs_2_, ...), custom_call_target="tpu_custom_call" | custom-call | flops 24159191040 | bytes 2424832 | tf_op jit(solution)/shard_map/pallas_call | solution.py:340
  68.2 3.2 %collective-permute-done.17.refs_4_ = bf16[512,512]{1,0:T(8,128)(2,1)S(1)} collective-permute-done((bf16[512,512]{1,0:T(8,128)(2,1)S(1)}, bf16[512,512]{1,0:T(8,128)(2,1)S(1)}, u32[]{:S(2)}, u32[]{:S(2)}) %collective-permute-start.17) | collective-permute-done | bytes 524320 | tf_op jit(solution)/shard_map/ppermute | solution.py:640
  72.2 7.0 %all-to-all-start = ((bf16[8,192,128]{2,1,0:T(8,128)(2,1)}), bf16[8,192,128]{2,1,0:T(8,128)(2,1)S(1)}, u32[]{:S(2)}, u32[]{:S(2)}) async-start(bf16[8,192,128]{2,1,0:T(8,128)(2,1)} %copy-done.8), calls=%async_computation | async-start | bytes 786432 | tf_op jit(solution)/shard_map/all_to_all | solution.py:698
  80.8 2.0 %collective-permute-start.22 = (bf16[512,512]{1,0:T(8,128)(2,1)}, bf16[512,512]{1,0:T(8,128)(2,1)}, u32[]{:S(2)}, u32[]{:S(2)}) collective-permute-start(bf16[512,512]{1,0:T(8,128)(2,1)} %collective-permute-done.18.refs_6_), channel_id=1, source_target_pairs={{0,8},{4,12},{8,0},{12,4},{16,24},{20,28},{24,16},{28,20},{1,9},{5... | collective-permute-start | bytes 1572872 | tf_op jit(solution)/shard_map/ppermute | solution.py:640
  84.2 6.8 %all-to-all-done.own_ref = bf16[8,192,128]{2,1,0:T(8,128)(2,1)S(1)} async-done(((bf16[8,192,128]{2,1,0:T(8,128)(2,1)}), bf16[8,192,128]{2,1,0:T(8,128)(2,1)S(1)}, u32[]{:S(2)}, u32[]{:S(2)}) %all-to-all-start) | async-done | bytes 393248 | tf_op jit(solution)/shard_map/all_to_all | solution.py:698
  92.6 1.8 %collective-permute-done.24.weight_ref = bf16[256,1024]{1,0:T(8,128)(2,1)} collective-permute-done((bf16[256,1024]{1,0:T(8,128)(2,1)}, bf16[256,1024]{1,0:T(8,128)(2,1)}, u32[]{:S(2)}, u32[]{:S(2)}) %collective-permute-start.24) | collective-permute-done | bytes 524320 | tf_op jit(solution)/shard_map/ppermute | solution.py:636
  94.4 3.9 %collective-permute-done.22.refs_8_ = bf16[512,512]{1,0:T(8,128)(2,1)} collective-permute-done((bf16[512,512]{1,0:T(8,128)(2,1)}, bf16[512,512]{1,0:T(8,128)(2,1)}, u32[]{:S(2)}, u32[]{:S(2)}) %collective-permute-start.22) | collective-permute-done | bytes 524320 | tf_op jit(solution)/shard_map/ppermute | solution.py:640
  98.3 1.9 %collective-permute-done.21.own_ref = bf16[8,192,128]{2,1,0:T(8,128)(2,1)} collective-permute-done((bf16[8,192,128]{2,1,0:T(8,128)(2,1)S(1)}, bf16[8,192,128]{2,1,0:T(8,128)(2,1)}, u32[]{:S(2)}, u32[]{:S(2)}) %collective-permute-start.21) | collective-permute-done | bytes 393248 | tf_op jit(solution)/shard_map/ppermute | solution.py:636
  100.7 1.7 %collective-permute-start.29 = (bf16[512,512]{1,0:T(8,128)(2,1)}, bf16[512,512]{1,0:T(8,128)(2,1)S(1)}, u32[]{:S(2)}, u32[]{:S(2)}) collective-permute-start(bf16[512,512]{1,0:T(8,128)(2,1)} %copy-done.4), channel_id=1, source_target_pairs={{0,8},{4,12},{8,0},{12,4},{16,24},{20,28},{24,16},{28,20},{1,9},{5... | collective-permute-start | bytes 1572872 | tf_op jit(solution)/shard_map/ppermute | solution.py:640
  104.9 3.4 %shard_map.102 = (f32[384,1024]{1,0:T(8,128)S(1)}, bf16[384,768]{1,0:T(8,128)(2,1)S(1)}, f32[8,128]{1,0:T(8,128)}) custom-call(s32[1]{0:T(128)} %bitcast.core_ref, f32[8,128]{1,0:T(8,128)S(1)} %get-tuple-element.47.rank_ref, bf16[768,1024]{1,0:T(8,128)(2,1)S(1)} %copy-done.3, bf16[8,192,128]{2,1,0:T(8,128)(2,1)S(1)} %all-to-all-done.own_ref, ...), custom_call_target="tpu_custom_call" | custom-call | flops 4026531840 | bytes 8388608 | tf_op jit(solution)/shard_map/pallas_call | solution.py:499
  108.4 4.4 %shard_map.103 = (f32[192,1024]{1,0:T(8,128)S(1)}, bf16[384,256]{1,0:T(8,128)(2,1)S(1)}, bf16[384,256]{1,0:T(8,128)(2,1)S(1)}) custom-call(s32[1]{0:T(128)} %bitcast.core_ref, s32[1]{0:T(128)} %bitcast.1.chip_ref, f32[384,1024]{1,0:T(8,128)S(1)} %get-tuple-element.67.base_ref, bf16[384,768]{1,0:T(8,128)(2,1)S(1)} %get-tuple-element.68.order_ref, ...), custom_call_target="tpu_custom_call" | custom-call | flops 4026531840 | bytes 8388608 | tf_op jit(solution)/shard_map/pallas_call | solution.py:530
  112.8 1.6 %collective-permute-start.31 = (bf16[256,1024]{1,0:T(8,128)(2,1)S(1)}, bf16[256,1024]{1,0:T(8,128)(2,1)S(1)}, u32[]{:S(2)}, u32[]{:S(2)}) collective-permute-start(bf16[256,1024]{1,0:T(8,128)(2,1)S(1)} %copy-done.14), channel_id=1, source_target_pairs={{0,2},{2,0},{1,3},{3,1},{4,6},{6,4},{5,7},{7,5},{8,10},{10,8},{9,1... | collective-permute-start | bytes 1572872 | tf_op jit(solution)/shard_map/ppermute | solution.py:636
  116.2 18.1 %shard_map.104 = (bf16[192,256]{1,0:T(8,128)(2,1)S(1)}, bf16[192,256]{1,0:T(8,128)(2,1)S(1)}, bf16[192,256]{1,0:T(8,128)(2,1)S(1)}, bf16[192,256]{1,0:T(8,128)(2,1)S(1)}) custom-call(s32[1]{0:T(128)} %bitcast.1.chip_ref, bf16[384,256]{1,0:T(8,128)(2,1)S(1)} %get-tuple-element.74.refs_0_, bf16[384,256]{1,0:T(8,128)(2,1)S(1)} %collective-permute-done.28.refs_1_, ...), custom_call_target="tpu_custom_call" | custom-call | tf_op jit(solution)/shard_map/pallas_call | solution.py:606
  134.3 1.6 %collective-permute-start.32 = (bf16[192,256]{1,0:T(8,128)(2,1)S(1)}, bf16[192,256]{1,0:T(8,128)(2,1)S(1)}, u32[]{:S(2)}, u32[]{:S(2)}) collective-permute-start(bf16[192,256]{1,0:T(8,128)(2,1)S(1)} %get-tuple-element.83), channel_id=1, source_target_pairs={{0,2},{2,0},{1,3},{3,1},{4,6},{6,4},{5,7},{7,5},{8,10},{10,8},{9,1... | collective-permute-start | bytes 294920 | tf_op jit(solution)/shard_map/ppermute | solution.py:636
  136.9 3.1 %collective-permute-done.32.refs_0_ = bf16[192,256]{1,0:T(8,128)(2,1)S(1)} collective-permute-done((bf16[192,256]{1,0:T(8,128)(2,1)S(1)}, bf16[192,256]{1,0:T(8,128)(2,1)S(1)}, u32[]{:S(2)}, u32[]{:S(2)}) %collective-permute-start.32) | collective-permute-done | bytes 98336 | tf_op jit(solution)/shard_map/ppermute | solution.py:636
  (95 shorter events, 25.3 us)
Async XLA Ops:
  11.2 8.9 %collective-permute-start.1 = (bf16[592,128]{1,0:T(8,128)(2,1)S(1)}, bf16[592,128]{1,0:T(8,128)(2,1)S(1)}, u32[]{:S(2)}, u32[]{:S(2)}) collective-permute-start(bf16[592,128]{1,0:T(8,128)(2,1)S(1)} %get-tuple-element.50), channel_id=1, source_target_pairs={{0,4},{4,0},{8,12},{12,8},{16,20},{20,16},{24,28},{28,24},{1,5},{5... | collective-permute-start | bytes 454664 | tf_op jit(solution)/shard_map/ppermute | solution.py:640
  14.2 12.3 %collective-permute-start.2 = (bf16[592,128]{1,0:T(8,128)(2,1)S(1)}, bf16[592,128]{1,0:T(8,128)(2,1)S(1)}, u32[]{:S(2)}, u32[]{:S(2)}) collective-permute-start(bf16[592,128]{1,0:T(8,128)(2,1)S(1)} %get-tuple-element.51), channel_id=1, source_target_pairs={{0,8},{4,12},{8,0},{12,4},{16,24},{20,28},{24,16},{28,20},{1,9},{5... | collective-permute-start | bytes 454664 | tf_op jit(solution)/shard_map/ppermute | solution.py:640
  15.8 11.8 %collective-permute-start.3 = (bf16[592,128]{1,0:T(8,128)(2,1)S(1)}, bf16[592,128]{1,0:T(8,128)(2,1)S(1)}, u32[]{:S(2)}, u32[]{:S(2)}) collective-permute-start(bf16[592,128]{1,0:T(8,128)(2,1)S(1)} %get-tuple-element.52), channel_id=1, source_target_pairs={{0,12},{4,8},{8,4},{12,0},{16,28},{20,24},{24,20},{28,16},{1,13},{... | collective-permute-start | bytes 454664 | tf_op jit(solution)/shard_map/ppermute | solution.py:640
  15.8 11.8 %collective-permute-start.4 = (bf16[592,128]{1,0:T(8,128)(2,1)S(1)}, bf16[592,128]{1,0:T(8,128)(2,1)S(1)}, u32[]{:S(2)}, u32[]{:S(2)}) collective-permute-start(bf16[592,128]{1,0:T(8,128)(2,1)S(1)} %get-tuple-element.53), channel_id=1, source_target_pairs={{0,16},{4,20},{8,24},{12,28},{16,0},{20,4},{24,8},{28,12},{1,17},{... | collective-permute-start | bytes 454664 | tf_op jit(solution)/shard_map/ppermute | solution.py:640
  18.8 22.0 %collective-permute-start.5 = (bf16[592,128]{1,0:T(8,128)(2,1)S(1)}, bf16[592,128]{1,0:T(8,128)(2,1)S(1)}, u32[]{:S(2)}, u32[]{:S(2)}) collective-permute-start(bf16[592,128]{1,0:T(8,128)(2,1)S(1)} %get-tuple-element.54), channel_id=1, source_target_pairs={{0,20},{4,16},{8,28},{12,24},{16,4},{20,0},{24,12},{28,8},{1,21},{... | collective-permute-start | bytes 454664 | tf_op jit(solution)/shard_map/ppermute | solution.py:640
  20.1 20.7 %collective-permute-start.6 = (bf16[592,128]{1,0:T(8,128)(2,1)S(1)}, bf16[592,128]{1,0:T(8,128)(2,1)S(1)}, u32[]{:S(2)}, u32[]{:S(2)}) collective-permute-start(bf16[592,128]{1,0:T(8,128)(2,1)S(1)} %get-tuple-element.55), channel_id=1, source_target_pairs={{0,24},{4,28},{8,16},{12,20},{16,8},{20,12},{24,0},{28,4},{1,25},{... | collective-permute-start | bytes 454664 | tf_op jit(solution)/shard_map/ppermute | solution.py:640
  26.5 14.8 %collective-permute-start.7 = (bf16[592,128]{1,0:T(8,128)(2,1)S(1)}, bf16[592,128]{1,0:T(8,128)(2,1)S(1)}, u32[]{:S(2)}, u32[]{:S(2)}) collective-permute-start(bf16[592,128]{1,0:T(8,128)(2,1)S(1)} %get-tuple-element.56), channel_id=1, source_target_pairs={{0,28},{4,24},{8,20},{12,16},{16,12},{20,8},{24,4},{28,0},{1,29},{... | collective-permute-start | bytes 454664 | tf_op jit(solution)/shard_map/ppermute | solution.py:640
  27.6 13.8 %collective-permute-start.8 = (bf16[592,128]{1,0:T(8,128)(2,1)S(1)}, bf16[592,128]{1,0:T(8,128)(2,1)S(1)}, u32[]{:S(2)}, u32[]{:S(2)}) collective-permute-start(bf16[592,128]{1,0:T(8,128)(2,1)S(1)} %get-tuple-element.57.refs_0_), channel_id=1, source_target_pairs={{0,1},{1,0},{2,3},{3,2},{4,5},{5,4},{6,7},{7,6},{8,9},{9,8},{10,11... | collective-permute-start | bytes 454664 | tf_op jit(solution)/shard_map/ppermute | solution.py:636
  27.6 14.2 %collective-permute-start.10 = (bf16[592,128]{1,0:T(8,128)(2,1)S(1)}, bf16[592,128]{1,0:T(8,128)(2,1)S(1)}, u32[]{:S(2)}, u32[]{:S(2)}) collective-permute-start(bf16[592,128]{1,0:T(8,128)(2,1)S(1)} %collective-permute-done.2.refs_2_), channel_id=1, source_target_pairs={{0,1},{1,0},{2,3},{3,2},{4,5},{5,4},{6,7},{7,6},{8,9},{9,8},{10,11... | collective-permute-start | bytes 454664 | tf_op jit(solution)/shard_map/ppermute | solution.py:636
  42.4 25.8 %collective-permute-start.16 = (bf16[512,512]{1,0:T(8,128)(2,1)S(1)}, bf16[512,512]{1,0:T(8,128)(2,1)S(1)}, u32[]{:S(2)}, u32[]{:S(2)}) collective-permute-start(bf16[512,512]{1,0:T(8,128)(2,1)S(1)} %pad_maximum_fusion.refs_2_), channel_id=1, source_target_pairs={{0,4},{4,0},{8,12},{12,8},{16,20},{20,16},{24,28},{28,24},{1,5},{5... | collective-permute-start | bytes 1572872 | tf_op jit(solution)/shard_map/ppermute | solution.py:640
  43.2 28.2 %collective-permute-start.17 = (bf16[512,512]{1,0:T(8,128)(2,1)S(1)}, bf16[512,512]{1,0:T(8,128)(2,1)S(1)}, u32[]{:S(2)}, u32[]{:S(2)}) collective-permute-start(bf16[512,512]{1,0:T(8,128)(2,1)S(1)} %pad_maximum_fusion.refs_2_), channel_id=1, source_target_pairs={{0,8},{4,12},{8,0},{12,4},{16,24},{20,28},{24,16},{28,20},{1,9},{5... | collective-permute-start | bytes 1572872 | tf_op jit(solution)/shard_map/ppermute | solution.py:640
  48.0 24.1 %collective-permute-start.18 = (bf16[512,512]{1,0:T(8,128)(2,1)S(1)}, bf16[512,512]{1,0:T(8,128)(2,1)}, u32[]{:S(2)}, u32[]{:S(2)}) collective-permute-start(bf16[512,512]{1,0:T(8,128)(2,1)S(1)} %pad_maximum_fusion.refs_2_), channel_id=1, source_target_pairs={{0,16},{4,20},{8,24},{12,28},{16,0},{20,4},{24,8},{28,12},{1,17},{... | collective-permute-start | bytes 1572872 | tf_op jit(solution)/shard_map/ppermute | solution.py:640
  72.2 18.9 %all-to-all-start = ((bf16[8,192,128]{2,1,0:T(8,128)(2,1)}), bf16[8,192,128]{2,1,0:T(8,128)(2,1)S(1)}, u32[]{:S(2)}, u32[]{:S(2)}) async-start(bf16[8,192,128]{2,1,0:T(8,128)(2,1)} %copy-done.8), calls=%async_computation | async-start | bytes 786432 | tf_op jit(solution)/shard_map/all_to_all | solution.py:698
  79.2 15.2 %collective-permute-start.24 = (bf16[256,1024]{1,0:T(8,128)(2,1)}, bf16[256,1024]{1,0:T(8,128)(2,1)}, u32[]{:S(2)}, u32[]{:S(2)}) collective-permute-start(bf16[256,1024]{1,0:T(8,128)(2,1)} %weight_ref.1), channel_id=1, source_target_pairs={{0,2},{2,0},{1,3},{3,1},{4,6},{6,4},{5,7},{7,5},{8,10},{10,8},{9,1... | collective-permute-start | bytes 1572872 | tf_op jit(solution)/shard_map/ppermute | solution.py:636
  80.8 17.5 %collective-permute-start.22 = (bf16[512,512]{1,0:T(8,128)(2,1)}, bf16[512,512]{1,0:T(8,128)(2,1)}, u32[]{:S(2)}, u32[]{:S(2)}) collective-permute-start(bf16[512,512]{1,0:T(8,128)(2,1)} %collective-permute-done.18.refs_6_), channel_id=1, source_target_pairs={{0,8},{4,12},{8,0},{12,4},{16,24},{20,28},{24,16},{28,20},{1,9},{5... | collective-permute-start | bytes 1572872 | tf_op jit(solution)/shard_map/ppermute | solution.py:640
  82.8 15.5 %collective-permute-start.23 = (bf16[512,512]{1,0:T(8,128)(2,1)}, bf16[512,512]{1,0:T(8,128)(2,1)}, u32[]{:S(2)}, u32[]{:S(2)}) collective-permute-start(bf16[512,512]{1,0:T(8,128)(2,1)} %collective-permute-done.18.refs_6_), channel_id=1, source_target_pairs={{0,4},{4,0},{8,12},{12,8},{16,20},{20,16},{24,28},{28,24},{1,5},{5... | collective-permute-start | bytes 1572872 | tf_op jit(solution)/shard_map/ppermute | solution.py:640
  91.1 9.1 %collective-permute-start.21 = (bf16[8,192,128]{2,1,0:T(8,128)(2,1)S(1)}, bf16[8,192,128]{2,1,0:T(8,128)(2,1)}, u32[]{:S(2)}, u32[]{:S(2)}) collective-permute-start(bf16[8,192,128]{2,1,0:T(8,128)(2,1)S(1)} %all-to-all-done.own_ref), channel_id=1, source_target_pairs={{0,2},{2,0},{1,3},{3,1},{4,6},{6,4},{5,7},{7,5},{8,10},{10,8},{9,1... | collective-permute-start | bytes 1179656 | tf_op jit(solution)/shard_map/ppermute | solution.py:636
  98.3 10.1 %collective-permute-start.27 = (bf16[1024,256]{1,0:T(8,128)(2,1)}, bf16[1024,256]{1,0:T(8,128)(2,1)}, u32[]{:S(2)}, u32[]{:S(2)}) collective-permute-start(bf16[1024,256]{1,0:T(8,128)(2,1)} %query_weight_ref.1), channel_id=1, source_target_pairs={{0,1},{1,0},{2,3},{3,2},{4,5},{5,4},{6,7},{7,6},{8,9},{9,8},{10,11... | collective-permute-start | bytes 1572872 | tf_op jit(solution)/shard_map/ppermute | solution.py:636
  100.2 8.2 %collective-permute-start.26 = (bf16[256,1024]{1,0:T(8,128)(2,1)}, bf16[256,1024]{1,0:T(8,128)(2,1)}, u32[]{:S(2)}, u32[]{:S(2)}) collective-permute-start(bf16[256,1024]{1,0:T(8,128)(2,1)} %collective-permute-done.24.weight_ref), channel_id=1, source_target_pairs={{0,1},{1,0},{2,3},{3,2},{4,5},{5,4},{6,7},{7,6},{8,9},{9,8},{10,11... | collective-permute-start | bytes 1572872 | tf_op jit(solution)/shard_map/ppermute | solution.py:636
  100.2 8.2 %collective-permute-start.25 = (bf16[8,192,128]{2,1,0:T(8,128)(2,1)}, bf16[8,192,128]{2,1,0:T(8,128)(2,1)}, u32[]{:S(2)}, u32[]{:S(2)}) collective-permute-start(bf16[8,192,128]{2,1,0:T(8,128)(2,1)} %collective-permute-done.21.own_ref), channel_id=1, source_target_pairs={{0,1},{1,0},{2,3},{3,2},{4,5},{5,4},{6,7},{7,6},{8,9},{9,8},{10,11... | collective-permute-start | bytes 1179656 | tf_op jit(solution)/shard_map/ppermute | solution.py:636
  100.7 14.3 %collective-permute-start.29 = (bf16[512,512]{1,0:T(8,128)(2,1)}, bf16[512,512]{1,0:T(8,128)(2,1)S(1)}, u32[]{:S(2)}, u32[]{:S(2)}) collective-permute-start(bf16[512,512]{1,0:T(8,128)(2,1)} %copy-done.4), channel_id=1, source_target_pairs={{0,8},{4,12},{8,0},{12,4},{16,24},{20,28},{24,16},{28,20},{1,9},{5... | collective-permute-start | bytes 1572872 | tf_op jit(solution)/shard_map/ppermute | solution.py:640
  102.4 13.8 %collective-permute-start.30 = (bf16[512,512]{1,0:T(8,128)(2,1)}, bf16[512,512]{1,0:T(8,128)(2,1)S(1)}, u32[]{:S(2)}, u32[]{:S(2)}) collective-permute-start(bf16[512,512]{1,0:T(8,128)(2,1)} %collective-permute-done.22.refs_8_), channel_id=1, source_target_pairs={{0,4},{4,0},{8,12},{12,8},{16,20},{20,16},{24,28},{28,24},{1,5},{5... | collective-permute-start | bytes 1572872 | tf_op jit(solution)/shard_map/ppermute | solution.py:640
  112.8 21.4 %collective-permute-start.31 = (bf16[256,1024]{1,0:T(8,128)(2,1)S(1)}, bf16[256,1024]{1,0:T(8,128)(2,1)S(1)}, u32[]{:S(2)}, u32[]{:S(2)}) collective-permute-start(bf16[256,1024]{1,0:T(8,128)(2,1)S(1)} %copy-done.14), channel_id=1, source_target_pairs={{0,2},{2,0},{1,3},{3,1},{4,6},{6,4},{5,7},{7,5},{8,10},{10,8},{9,1... | collective-permute-start | bytes 1572872 | tf_op jit(solution)/shard_map/ppermute | solution.py:636
  114.4 22.5 %collective-permute-start.36 = (bf16[256,1024]{1,0:T(8,128)(2,1)S(1)}, bf16[256,1024]{1,0:T(8,128)(2,1)S(1)}, u32[]{:S(2)}, u32[]{:S(2)}) collective-permute-start(bf16[256,1024]{1,0:T(8,128)(2,1)S(1)} %copy-done.14), channel_id=1, source_target_pairs={{0,1},{1,0},{2,3},{3,2},{4,5},{5,4},{6,7},{7,6},{8,9},{9,8},{10,11... | collective-permute-start | bytes 1572872 | tf_op jit(solution)/shard_map/ppermute | solution.py:636
  (30 other events, 189.2 us)
